TPU v7x, 128 devices: a whole 4x4x4 slice. The times are simulated.
128 devices in a mesh: gz: 8 (over z_hi, y), row: 16 (over z_lo, x, core).
Axes of the slice: x: 4, y: 4, z: 4 (z_hi: 2, z_lo: 2; z = z_hi * 2 + z_lo), core: 2. Of those that a mesh axis runs over, the one named last changes fastest.
Arguments:
- swirl: float32 [1536, 16384], P('gz', 'row'), may hold values from -6 to 6
- vorticity: float32 [1536, 16384], P('gz', 'row'), may hold values from -5 to 5
- base_swirl: float32 [1536, 16384], P('gz', 'row'), may hold values from -6 to 6
- vel_r: float32 [1536, 16384], P('gz', 'row'), may hold values from -6 to 6
- vel_z: float32 [1536, 16384], P('gz', 'row'), may hold values from -6 to 6
- swirl_coef: float32 [1536, 16384], P('gz', 'row'), may hold values from 0.5 to 2
- vort_coef: float32 [1536, 16384], P('gz', 'row'), may hold values from 0.5 to 2
Outputs:
- swirl_rate: float32 [1536, 16384], P('gz', 'row')
- vort_rate: float32 [1536, 16384], P('gz', 'row')
- potential: float32 [1536, 16384], P('gz', 'row')
All inputs are finite; a program needn't handle non-finite values.
Results may differ from a plain program's by a relative error of at most 0.0001.
Values sent between devices are 32-bit elements; how exact they have to be, the bound alone decides.
No kernel may reach another device: no remote copies, remote signals or barrier semaphores. Data moves between devices by JAX's collectives and lax.ppermute only.
A program may use at most 64 MiB of HBM per device.

v0:
```python
import jax
import jax.numpy as jnp
from jax import lax
from jax.sharding import PartitionSpec as P

LEVELS = 3
COARSE_ITERS = 10


def with_halo(value, sides, width):
    for axis, dim in sides:
        devices, length = (lax.axis_size(axis), value.shape[dim])
        up = [(i, (i + 1) % devices) for i in range(devices - 1)]
        down = [(j, i) for i, j in up]
        last = lax.slice_in_dim(value, length - width, length, axis=dim)
        leading = lax.slice_in_dim(value, 0, width, axis=dim)
        before = lax.ppermute(last, axis, up)
        after = lax.ppermute(leading, axis, down)
        value = jnp.concatenate([before, value, after], axis=dim)
    return value


def radial_coefs(col_start, col_count, level_no):
    spacing = float(2**level_no)
    columns = (jnp.arange(col_count) + col_start).astype(jnp.float32)
    radius = spacing * (columns + 0.5) + 16.0
    radial_term = 1.5 * spacing / radius
    return (1.0 + radial_term, 1.0 - radial_term)


def neighbours(padded, east_coef, west_coef):
    beside = padded[:-2, 1:-1] + padded[2:, 1:-1]
    beside = beside + east_coef * padded[1:-1, 2:]
    beside = beside + west_coef * padded[1:-1, :-2]
    return beside


def checker(row_count, col_count):
    total = jnp.arange(row_count)[:, None] + jnp.arange(col_count)[None, :]
    return total % 2 == 0


def relax_half(field, padded, source, cells, east_coef, west_coef, factor):
    updated = (factor * source + neighbours(padded, east_coef, west_coef)) * 0.25
    return jnp.where(cells, updated, field)


def apply_operator(field, padded, east_coef, west_coef, factor):
    return (4.0 * field - neighbours(padded, east_coef, west_coef)) / factor


def residual_of(field, padded, source, east_coef, west_coef, factor):
    return source - apply_operator(field, padded, east_coef, west_coef, factor)


def restrict_avg(resid):
    return (resid[0::2, 0::2] + resid[1::2, 0::2] + resid[0::2, 1::2] + resid[1::2, 1::2]) * 0.25


def prolongate(correction):
    return jnp.repeat(jnp.repeat(correction, 2, axis=0), 2, axis=1)


def rim(field):
    return with_halo(field, (("gz", 0), ("row", 1)), 1)


def coarse_solve(source):
    row_count, col_count = source.shape
    east_coef, west_coef = radial_coefs(0, col_count, LEVELS)
    factor = float(4**LEVELS)
    count = float(row_count * col_count)

    def one_turn(turn_no, carry):
        field, resid = carry
        image = apply_operator(resid, jnp.pad(resid, 1), east_coef, west_coef, factor)
        upper = jnp.sum(resid * image) / count
        lower = jnp.sum(image * image) / count
        alpha = upper / (lower + 1e-12)
        return (field + alpha * resid, resid - alpha * image)

    field, resid = lax.fori_loop(0, COARSE_ITERS, one_turn, (jnp.zeros_like(source), source))
    return field


def agglomerate(coarse):
    column_strip = lax.all_gather(coarse, "gz", axis=0, tiled=True)
    whole_grid = lax.all_gather(column_strip, "row", axis=1, tiled=True)
    solved = coarse_solve(whole_grid)
    row_count, col_count = coarse.shape
    corner = (lax.axis_index("gz") * row_count, lax.axis_index("row") * col_count)
    return lax.dynamic_slice(solved, corner, (row_count, col_count))


def v_cycle(source, level_no):
    row_count, col_count = source.shape
    col_start = lax.axis_index("row") * col_count
    east_coef, west_coef = radial_coefs(col_start, col_count, level_no)
    red_cells = checker(row_count, col_count)
    black_cells = jnp.logical_not(red_cells)
    factor = float(4**level_no)
    field = jnp.where(red_cells, factor * source * 0.25, 0.0)
    field = relax_half(field, rim(field), source, black_cells, east_coef, west_coef, factor)
    resid = residual_of(field, rim(field), source, east_coef, west_coef, factor)
    coarse = restrict_avg(resid)
    if level_no + 1 == LEVELS:
        correction = agglomerate(coarse)
    else:
        correction = v_cycle(coarse, level_no + 1)
    field = field + prolongate(correction)
    field = relax_half(field, rim(field), source, red_cells, east_coef, west_coef, factor)
    field = relax_half(field, rim(field), source, black_cells, east_coef, west_coef, factor)
    return field


def per_device(swirl, vorticity, base_swirl, vel_r, vel_z, swirl_coef, vort_coef):
    stacked = jnp.stack([swirl, vorticity, 2.0 * base_swirl * swirl])
    padded = with_halo(stacked, (("gz", 1), ("row", 2)), 1)
    along_z = (padded[:, 2:, 1:-1] - padded[:, :-2, 1:-1]) * 0.5
    along_r = (padded[:, 1:-1, 2:] - padded[:, 1:-1, :-2]) * 0.5
    swirl_rate = swirl_coef * swirl - vel_r * along_r[0] - vel_z * along_z[0]
    vort_rate = vort_coef * vorticity - vel_r * along_r[1] - vel_z * along_z[1] + along_z[2]
    potential = v_cycle(vorticity, 0)
    return (swirl_rate, vort_rate, potential)


def solution(mesh):
    in_specs = (
        P("gz", "row"),
        P("gz", "row"),
        P("gz", "row"),
        P("gz", "row"),
        P("gz", "row"),
        P("gz", "row"),
        P("gz", "row"),
    )
    out_specs = (P("gz", "row"), P("gz", "row"), P("gz", "row"))
    return jax.shard_map(
        per_device, mesh=mesh, in_specs=in_specs, out_specs=out_specs, check_vma=False
    )
```

profile of v0, /device:TPU:56, one launch (start us, length us, event | category | flops | bytes accessed | tf_op | source)
XLA Modules:
  0.0 585.5 jit_solution(13370380163215897712)
XLA Ops:
  16.5 9.5 %collective-permute-done.4 = f32[1,1024]{0,1:T(8,128)S(1)} collective-permute-done((f32[1,1024]{0,1:T(8,128)}, f32[1,1024]{0,1:T(8,128)S(1)}, u32[]{:S(2)}, u32[]{:S(2)}) %collective-permute-start.4) | collective-permute-done | bytes 4128 | tf_op jit(solution)/shard_map/ppermute | solution.py:17
  26.0 7.6 %collective-permute-done.5 = f32[1,1024]{0,1:T(8,128)S(1)} collective-permute-done((f32[1,1024]{0,1:T(8,128)}, f32[1,1024]{0,1:T(8,128)S(1)}, u32[]{:S(2)}, u32[]{:S(2)}) %collective-permute-start.5) | collective-permute-done | bytes 4128 | tf_op jit(solution)/shard_map/ppermute | solution.py:18
  52.5 5.9 %collective-permute-done.8 = f32[1,1024]{0,1:T(8,128)S(1)} collective-permute-done((f32[1,1024]{0,1:T(8,128)S(1)}, f32[1,1024]{0,1:T(8,128)S(1)}, u32[]{:S(2)}, u32[]{:S(2)}) %collective-permute-start.8) | collective-permute-done | bytes 4128 | tf_op jit(solution)/shard_map/ppermute | solution.py:17
  78.1 9.2 %slice.468 = f32[96,512]{0,1:T(8,128)S(1)} slice(f32[192,1024]{0,1:T(8,128)S(1)} %fusion.37), slice={[0:192:2], [0:1024:2]} | slice | bytes 393216 | tf_op jit(solution)/shard_map/slice | solution.py:57
  87.3 9.2 %slice.469 = f32[96,512]{0,1:T(8,128)S(1)} slice(f32[192,1024]{0,1:T(8,128)S(1)} %fusion.37), slice={[1:192:2], [0:1024:2]} | slice | bytes 393216 | tf_op jit(solution)/shard_map/slice | solution.py:57
  96.5 9.2 %slice.470 = f32[96,512]{0,1:T(8,128)S(1)} slice(f32[192,1024]{0,1:T(8,128)S(1)} %fusion.37), slice={[0:192:2], [1:1024:2]} | slice | bytes 393216 | tf_op jit(solution)/shard_map/slice | solution.py:57
  105.7 9.2 %slice.471 = f32[96,512]{0,1:T(8,128)S(1)} slice(f32[192,1024]{0,1:T(8,128)S(1)} %fusion.37), slice={[1:192:2], [1:1024:2]} | slice | bytes 393216 | tf_op jit(solution)/shard_map/slice | solution.py:57
  217.1 36.2 %all_gather.6 = f32[192,128]{1,0:T(8,128)} all-gather(f32[24,128]{1,0:T(8,128)S(1)} %copy.97), channel_id=1, replica_groups=mesh['gz'=8,'row'=16] {'gz'}, dimensions={0}, use_global_device_ids=true | all-gather | bytes 110592 | tf_op jit(solution)/shard_map/all_gather | solution.py:87
  253.3 32.2 %all-gather.2.cloned.1.call-done = f32[192,2048]{1,0:T(8,128)} async-done(((f32[192,128]{1,0:T(8,128)}), f32[192,2048]{1,0:T(8,128)}) %all-gather.2.cloned.1.call-update) | async-done | bytes 1572880 | tf_op jit(solution)/shard_map/all_gather | solution.py:88
  285.6 114.1 %while.15 = (s32[]{:T(128)}, f32[192,2048]{1,0:T(8,128)}, f32[192,2048]{1,0:T(8,128)}, s32[]{:T(128)}, f32[]{:T(128)}, /*index=5*/f32[]{:T(128)}, f32[]{:T(128)}, s32[]{:T(128)}) while((s32[]{:T(128)}, f32[192,2048]{1,0:T(8,128)}, f32[192,2048]{1,0:T(8,128)}, s32[]{:T(128)}, f32[]{:T(128)}, /*index=5*/f32[]{:T(128)}, f32[]{:T(128)}, ...), condition=%wide.region_3.4_spmd.clone, body=%wide.region_0.3_spmd.clone.sunk | while | flops 6699014 | bytes 23625956 | solution.py:82
  285.6 5.6 multiply_reduce_fusion.3
  295.7 5.6 multiply_reduce_fusion.3
  307.3 5.6 multiply_reduce_fusion.3
  318.8 5.6 multiply_reduce_fusion.3
  330.4 5.6 multiply_reduce_fusion.3
  341.9 5.6 multiply_reduce_fusion.3
  353.5 5.6 multiply_reduce_fusion.3
  365.0 5.6 multiply_reduce_fusion.3
  376.6 5.6 multiply_reduce_fusion.3
  388.1 5.6 multiply_reduce_fusion.3
  408.2 7.7 %collective-permute-done.29 = f32[1,256]{0,1:T(8,128)S(1)} collective-permute-done((f32[1,256]{0,1:T(8,128)S(1)}, f32[1,256]{0,1:T(8,128)S(1)}, u32[]{:S(2)}, u32[]{:S(2)}) %collective-permute-start.29) | collective-permute-done | bytes 1056 | tf_op jit(solution)/shard_map/ppermute | solution.py:18
  434.4 5.7 collective-permute-done.33
  458.4 5.8 collective-permute-done.37
  526.3 7.7 %collective-permute-done.45 = f32[1,1024]{0,1:T(8,128)S(1)} collective-permute-done((f32[1,1024]{0,1:T(8,128)S(1)}, f32[1,1024]{0,1:T(8,128)S(1)}, u32[]{:S(2)}, u32[]{:S(2)}) %collective-permute-start.45) | collective-permute-done | bytes 4128 | tf_op jit(solution)/shard_map/ppermute | solution.py:18
  (276 shorter events, 346.4 us)
Async XLA Ops:
  7.2 278.4 %all-gather.2.cloned.1.call-start = ((), (), s32[]{:S(2)}) async-start(), calls=%async_computation | async-start | bytes 1671168 | tf_op jit(solution)/shard_map/all_gather | solution.py:88
  10.0 16.0 %collective-permute-start.4 = (f32[1,1024]{0,1:T(8,128)}, f32[1,1024]{0,1:T(8,128)S(1)}, u32[]{:S(2)}, u32[]{:S(2)}) collective-permute-start(f32[1,1024]{0,1:T(8,128)} %get-tuple-element.140), channel_id=1, source_target_pairs={{0,16},{16,32},{32,48},{48,64},{64,80},{80,96},{96,112},{1,17},{17... | collective-permute-start | bytes 12296 | tf_op jit(solution)/shard_map/ppermute | solution.py:17
  14.6 19.1 %collective-permute-start.5 = (f32[1,1024]{0,1:T(8,128)}, f32[1,1024]{0,1:T(8,128)S(1)}, u32[]{:S(2)}, u32[]{:S(2)}) collective-permute-start(f32[1,1024]{0,1:T(8,128)} %get-tuple-element.141), channel_id=1, source_target_pairs={{16,0},{32,16},{48,32},{64,48},{80,64},{96,80},{112,96},{17,1},{33... | collective-permute-start | bytes 12296 | tf_op jit(solution)/shard_map/ppermute | solution.py:18
  46.6 11.8 %collective-permute-start.8 = (f32[1,1024]{0,1:T(8,128)S(1)}, f32[1,1024]{0,1:T(8,128)S(1)}, u32[]{:S(2)}, u32[]{:S(2)}) collective-permute-start(f32[1,1024]{0,1:T(8,128)S(1)} %get-tuple-element.138), channel_id=1, source_target_pairs={{0,16},{16,32},{32,48},{48,64},{64,80},{80,96},{96,112},{1,17},{17... | collective-permute-start | bytes 12296 | tf_op jit(solution)/shard_map/ppermute | solution.py:17
  48.5 15.4 %collective-permute-start.9 = (f32[1,1024]{0,1:T(8,128)S(1)}, f32[1,1024]{0,1:T(8,128)S(1)}, u32[]{:S(2)}, u32[]{:S(2)}) collective-permute-start(f32[1,1024]{0,1:T(8,128)S(1)} %get-tuple-element.139), channel_id=1, source_target_pairs={{16,0},{32,16},{48,32},{64,48},{80,64},{96,80},{112,96},{17,1},{33... | collective-permute-start | bytes 12296 | tf_op jit(solution)/shard_map/ppermute | solution.py:18
  117.1 11.9 %collective-permute-start.13 = (f32[1,512]{0,1:T(8,128)S(1)}, f32[1,512]{0,1:T(8,128)S(1)}, u32[]{:S(2)}, u32[]{:S(2)}) collective-permute-start(f32[1,512]{0,1:T(8,128)S(1)} %get-tuple-element.165), channel_id=1, source_target_pairs={{16,0},{32,16},{48,32},{64,48},{80,64},{96,80},{112,96},{17,1},{33... | collective-permute-start | bytes 6152 | tf_op jit(solution)/shard_map/ppermute | solution.py:18
  142.1 11.9 %collective-permute-start.17 = (f32[1,512]{0,1:T(8,128)S(1)}, f32[1,512]{0,1:T(8,128)S(1)}, u32[]{:S(2)}, u32[]{:S(2)}) collective-permute-start(f32[1,512]{0,1:T(8,128)S(1)} %get-tuple-element.163), channel_id=1, source_target_pairs={{16,0},{32,16},{48,32},{64,48},{80,64},{96,80},{112,96},{17,1},{33... | collective-permute-start | bytes 6152 | tf_op jit(solution)/shard_map/ppermute | solution.py:18
  173.4 10.5 %collective-permute-start.21 = (f32[1,256]{0,1:T(8,128)S(1)}, f32[1,256]{0,1:T(8,128)S(1)}, u32[]{:S(2)}, u32[]{:S(2)}) collective-permute-start(f32[1,256]{0,1:T(8,128)S(1)} %get-tuple-element.173), channel_id=1, source_target_pairs={{16,0},{32,16},{48,32},{64,48},{80,64},{96,80},{112,96},{17,1},{33... | collective-permute-start | bytes 3080 | tf_op jit(solution)/shard_map/ppermute | solution.py:18
  195.3 10.5 %collective-permute-start.25 = (f32[1,256]{0,1:T(8,128)S(1)}, f32[1,256]{0,1:T(8,128)S(1)}, u32[]{:S(2)}, u32[]{:S(2)}) collective-permute-start(f32[1,256]{0,1:T(8,128)S(1)} %get-tuple-element.171), channel_id=1, source_target_pairs={{16,0},{32,16},{48,32},{64,48},{80,64},{96,80},{112,96},{17,1},{33... | collective-permute-start | bytes 3080 | tf_op jit(solution)/shard_map/ppermute | solution.py:18
  405.0 10.9 %collective-permute-start.29 = (f32[1,256]{0,1:T(8,128)S(1)}, f32[1,256]{0,1:T(8,128)S(1)}, u32[]{:S(2)}, u32[]{:S(2)}) collective-permute-start(f32[1,256]{0,1:T(8,128)S(1)} %get-tuple-element.169), channel_id=1, source_target_pairs={{16,0},{32,16},{48,32},{64,48},{80,64},{96,80},{112,96},{17,1},{33... | collective-permute-start | bytes 3080 | tf_op jit(solution)/shard_map/ppermute | solution.py:18
  429.5 10.6 %collective-permute-start.33 = (f32[1,256]{0,1:T(8,128)S(1)}, f32[1,256]{0,1:T(8,128)S(1)}, u32[]{:S(2)}, u32[]{:S(2)}) collective-permute-start(f32[1,256]{0,1:T(8,128)S(1)} %get-tuple-element.167), channel_id=1, source_target_pairs={{16,0},{32,16},{48,32},{64,48},{80,64},{96,80},{112,96},{17,1},{33... | collective-permute-start | bytes 3080 | tf_op jit(solution)/shard_map/ppermute | solution.py:18
  450.0 8.4 %collective-permute-start.36 = (f32[1,512]{0,1:T(8,128)S(1)}, f32[1,512]{0,1:T(8,128)S(1)}, u32[]{:S(2)}, u32[]{:S(2)}) collective-permute-start(f32[1,512]{0,1:T(8,128)S(1)} %get-tuple-element.160), channel_id=1, source_target_pairs={{0,16},{16,32},{32,48},{48,64},{64,80},{80,96},{96,112},{1,17},{17... | collective-permute-start | bytes 6152 | tf_op jit(solution)/shard_map/ppermute | solution.py:17
  452.3 11.9 %collective-permute-start.37 = (f32[1,512]{0,1:T(8,128)S(1)}, f32[1,512]{0,1:T(8,128)S(1)}, u32[]{:S(2)}, u32[]{:S(2)}) collective-permute-start(f32[1,512]{0,1:T(8,128)S(1)} %get-tuple-element.161), channel_id=1, source_target_pairs={{16,0},{32,16},{48,32},{64,48},{80,64},{96,80},{112,96},{17,1},{33... | collective-permute-start | bytes 6152 | tf_op jit(solution)/shard_map/ppermute | solution.py:18
  474.4 8.4 %collective-permute-start.40 = (f32[1,512]{0,1:T(8,128)S(1)}, f32[1,512]{0,1:T(8,128)S(1)}, u32[]{:S(2)}, u32[]{:S(2)}) collective-permute-start(f32[1,512]{0,1:T(8,128)S(1)} %get-tuple-element.158), channel_id=1, source_target_pairs={{0,16},{16,32},{32,48},{48,64},{64,80},{80,96},{96,112},{1,17},{17... | collective-permute-start | bytes 6152 | tf_op jit(solution)/shard_map/ppermute | solution.py:17
  476.5 11.9 %collective-permute-start.41 = (f32[1,512]{0,1:T(8,128)S(1)}, f32[1,512]{0,1:T(8,128)S(1)}, u32[]{:S(2)}, u32[]{:S(2)}) collective-permute-start(f32[1,512]{0,1:T(8,128)S(1)} %get-tuple-element.159), channel_id=1, source_target_pairs={{16,0},{32,16},{48,32},{64,48},{80,64},{96,80},{112,96},{17,1},{33... | collective-permute-start | bytes 6152 | tf_op jit(solution)/shard_map/ppermute | solution.py:18
  488.5 10.2 %collective-permute-start.42 = (f32[98,1]{0,1:T(1,128)S(1)}, f32[98,1]{0,1:T(1,128)S(1)}, u32[]{:S(2)}, u32[]{:S(2)}) collective-permute-start(f32[98,1]{0,1:T(1,128)S(1)} %get-tuple-element.142), channel_id=1, source_target_pairs={{1,0},{2,1},{3,2},{4,3},{5,4},{6,5},{7,6},{8,7},{9,8},{10,9},{11,1... | collective-permute-start | bytes 1184 | tf_op jit(solution)/shard_map/ppermute | solution.py:18
  492.8 24.3 %collective-permute-start = (f32[3,1,1024]{2,1,0:T(1,128)S(1)}, f32[3,1,1024]{2,1,0:T(1,128)S(1)}, u32[]{:S(2)}, u32[]{:S(2)}) collective-permute-start(f32[3,1,1024]{2,1,0:T(1,128)S(1)} %get-tuple-element.125), channel_id=1, source_target_pairs={{0,16},{16,32},{32,48},{48,64},{64,80},{80,96},{96,112},{1,17},{17... | collective-permute-start | bytes 36872 | tf_op jit(solution)/shard_map/ppermute | solution.py:17
  494.7 22.4 %collective-permute-start.1 = (f32[3,1,1024]{2,1,0:T(1,128)S(1)}, f32[3,1,1024]{2,1,0:T(1,128)S(1)}, u32[]{:S(2)}, u32[]{:S(2)}) collective-permute-start(f32[3,1,1024]{2,1,0:T(1,128)S(1)} %get-tuple-element.124), channel_id=1, source_target_pairs={{16,0},{32,16},{48,32},{64,48},{80,64},{96,80},{112,96},{17,1},{33... | collective-permute-start | bytes 36872 | tf_op jit(solution)/shard_map/ppermute | solution.py:18
  509.7 16.6 %collective-permute-start.44 = (f32[1,1024]{0,1:T(8,128)S(1)}, f32[1,1024]{0,1:T(8,128)S(1)}, u32[]{:S(2)}, u32[]{:S(2)}) collective-permute-start(f32[1,1024]{0,1:T(8,128)S(1)} %get-tuple-element.136), channel_id=1, source_target_pairs={{0,16},{16,32},{32,48},{48,64},{64,80},{80,96},{96,112},{1,17},{17... | collective-permute-start | bytes 12296 | tf_op jit(solution)/shard_map/ppermute | solution.py:17
  515.2 18.8 %collective-permute-start.45 = (f32[1,1024]{0,1:T(8,128)S(1)}, f32[1,1024]{0,1:T(8,128)S(1)}, u32[]{:S(2)}, u32[]{:S(2)}) collective-permute-start(f32[1,1024]{0,1:T(8,128)S(1)} %get-tuple-element.137), channel_id=1, source_target_pairs={{16,0},{32,16},{48,32},{64,48},{80,64},{96,80},{112,96},{17,1},{33... | collective-permute-start | bytes 12296 | tf_op jit(solution)/shard_map/ppermute | solution.py:18
  517.3 35.1 %collective-permute-start.2 = (f32[3,194,1]{2,1,0:T(8,128)S(1)}, f32[3,194,1]{2,1,0:T(8,128)S(1)}, u32[]{:S(2)}, u32[]{:S(2)}) collective-permute-start(f32[3,194,1]{2,1,0:T(8,128)S(1)} %get-tuple-element.122), channel_id=1, source_target_pairs={{1,0},{2,1},{3,2},{4,3},{5,4},{6,5},{7,6},{8,7},{9,8},{10,9},{11,1... | collective-permute-start | bytes 6992 | tf_op jit(solution)/shard_map/ppermute | solution.py:18
  522.1 30.3 %collective-permute-start.3 = (f32[3,194,1]{2,1,0:T(8,128)S(1)}, f32[3,194,1]{2,1,0:T(8,128)S(1)}, u32[]{:S(2)}, u32[]{:S(2)}) collective-permute-start(f32[3,194,1]{2,1,0:T(8,128)S(1)} %get-tuple-element.123), channel_id=1, source_target_pairs={{0,1},{1,2},{2,3},{3,4},{4,5},{5,6},{6,7},{7,8},{8,9},{9,10},{10,1... | collective-permute-start | bytes 6992 | tf_op jit(solution)/shard_map/ppermute | solution.py:17
  546.5 11.8 %collective-permute-start.48 = (f32[1,1024]{0,1:T(8,128)S(1)}, f32[1,1024]{0,1:T(8,128)S(1)}, u32[]{:S(2)}, u32[]{:S(2)}) collective-permute-start(f32[1,1024]{0,1:T(8,128)S(1)} %get-tuple-element.134), channel_id=1, source_target_pairs={{0,16},{16,32},{32,48},{48,64},{64,80},{80,96},{96,112},{1,17},{17... | collective-permute-start | bytes 12296 | tf_op jit(solution)/shard_map/ppermute | solution.py:17
  548.5 15.4 %collective-permute-start.49 = (f32[1,1024]{0,1:T(8,128)S(1)}, f32[1,1024]{0,1:T(8,128)S(1)}, u32[]{:S(2)}, u32[]{:S(2)}) collective-permute-start(f32[1,1024]{0,1:T(8,128)S(1)} %get-tuple-element.135), channel_id=1, source_target_pairs={{16,0},{32,16},{48,32},{64,48},{80,64},{96,80},{112,96},{17,1},{33... | collective-permute-start | bytes 12296 | tf_op jit(solution)/shard_map/ppermute | solution.py:18
  (68 other events, 1069.8 us)
Sparse Core Ops, SparseCore 0:
  253.4 32.0 all-gather.1
where the time goes:
time: 590 us; the launch traced here: 585 us
  waiting for transfers between devices  189 us (32%)
  starting transfers between devices  145 us (25%)
  other arithmetic  114 us (19%)
  local copies, waits for them, and re-layouts  73 us (12%)
  blocking collectives  36.2 us (6%)
  between operations  15.4 us (3%)
  loops' own time  12.3 us (2%)
    ppermute x26, starting transfers between devices, with_halo(): after = lax.ppermute(leading, axis, down)  83.5 us
    ppermute x26, waiting for transfers between devices, with_halo(): before = lax.ppermute(last, axis, up)  83.5 us
    ppermute x26, waiting for transfers between devices, with_halo(): after = lax.ppermute(leading, axis, down)  73.3 us
    ppermute x26, starting transfers between devices, with_halo(): before = lax.ppermute(last, axis, up)  61.8 us
    reduce_sum x10, other arithmetic, one_turn(): lower = jnp.sum(image * image) / count  56.2 us
    all_gather x1, blocking collectives, agglomerate(): column_strip = lax.all_gather(coarse, 'gz', axis=0, tiled=True)  36.2 us
    sub x10, other arithmetic, one_turn(): return (field + alpha * resid, resid - alpha * image)  33.9 us
    all_gather x1, waiting for transfers between devices, agglomerate(): whole_grid = lax.all_gather(column_strip, 'row', axis=1, tiled=True)  32.2 us
  transfers between devices with their start and end apart: 53, of which 36 were waited for; matrix products, arithmetic and copies ran while one was open for 3% of the time, Pallas kernels for 0%

commit v1 on v0

v1 whole, which is shorter than its diff:
```python
import functools

import jax
import jax.numpy as jnp
from jax import lax
from jax.experimental import pallas as pl
from jax.experimental.pallas import tpu as pltpu
from jax.sharding import PartitionSpec as P

LEVELS = 3
ITERS = 10
BASIS = ITERS + 1
PAIRS = [(i, j) for i in range(BASIS) for j in range(i, BASIS)]
SLOTS = 72
AXES = ("gz", "row")

ROWS, COLS = 192, 1024
MARGIN = 32
EXT = ROWS + 2 * MARGIN
WIDE = COLS + 128
PAD = 8
TILES = WIDE // 128
F32 = jnp.float32


def iota(shape, dim):
    return lax.broadcasted_iota(jnp.int32, shape, dim)


def local_cols():
    lane = iota((8, WIDE), 1)
    return jnp.where(lane < COLS + 64, lane, lane - WIDE)


def place():
    return lax.axis_index("gz"), lax.axis_index("row"), lax.axis_size("gz"), lax.axis_size("row")


def lanes_inside(cols, width, row, row_count):
    low = jnp.where(row == 0, 0, -width)
    high = jnp.where(row == row_count - 1, width, 2 * width)
    return (cols >= low) & (cols < high)


def fill_coefs(coef):
    _, row, _, _ = place()
    cols = local_cols() + row * COLS
    for level in range(LEVELS):
        spacing = float(2**level)
        radius = spacing * (lax.shift_right_arithmetic(cols, level).astype(F32) + 0.5) + 16.0
        term = (1.5 * spacing) / radius
        coef[pl.ds(16 * level, 8), :] = 1.0 + term
        coef[pl.ds(16 * level + 8, 8), :] = 1.0 - term


def shift(x, by):
    return pltpu.roll(x, by % x.shape[1], 1)


def beside_of(ref, start, coef, level):
    step = 2**level
    view = ref.at[pl.ds(pl.multiple_of(start - 8, 8), 24), :]
    here = view[8:16, :]
    total = view[7:15, :] + view[9:17, :]
    total = total + coef[pl.ds(16 * level, 8), :] * shift(here, -step)
    return total + coef[pl.ds(16 * level + 8, 8), :] * shift(here, step), here


def masks(level):
    _, row, _, row_count = place()
    cols = local_cols()
    inside = lanes_inside(cols, COLS, row, row_count)
    odd = ((lax.shift_right_arithmetic(cols, level) + iota((8, WIDE), 0)) & 1) == 1
    return odd & inside, jnp.logical_not(odd) & inside, inside


def row_factor(first, count, margin, amount):
    gz, _, gz_count, _ = place()
    low = jnp.where(gz == 0, margin, 0)
    high = jnp.where(gz == gz_count - 1, count - margin, count)
    at = iota((8, 1), 0) + first
    return jnp.where((at >= low) & (at < high), amount, 0.0).astype(F32)


def down_level(level, source, black, pairs, coarse, coef):
    count = EXT >> level
    margin = MARGIN >> level
    scale = float(4**level)
    step = 2**level

    black_cells, _, _ = masks(level)

    @pl.loop(0, count // 8)
    def _(k):
        start = pl.multiple_of(PAD + 8 * k, 8)
        beside, here = beside_of(source, start, coef, level)
        value = here + 0.25 * beside
        factor = row_factor(8 * k, count, margin, 0.25 * scale)
        black[pl.ds(start, 8), :] = jnp.where(black_cells, value * factor, 0.0)

    @pl.loop(0, count // 8)
    def _(k):
        start = pl.multiple_of(PAD + 8 * k, 8)
        beside, _ = beside_of(black, start, coef, level)
        both = beside + shift(beside, -step)
        for tile in range(TILES):
            pairs[pl.ds(pl.multiple_of(EXT * tile + 8 * k, 8), 8), :] = both[:, 128 * tile : 128 * tile + 128]

    _, _, inside = masks(level)
    offset = PAD if level < LEVELS - 1 else 0

    @pl.loop(0, count // 16)
    def _(k):
        factor = row_factor(8 * k, count // 2, margin // 2, 0.25 / scale)
        for tile in range(TILES):
            lanes = slice(128 * tile, 128 * tile + 128)
            view = pairs.at[pl.ds(pl.multiple_of(EXT * tile + 16 * k, 16), 16), :]
            top = view[pl.ds(0, 8, stride=2), :]
            low = view[pl.ds(1, 8, stride=2), :]
            value = jnp.where(inside[:, lanes], (top + low) * factor, 0.0)
            coarse[pl.ds(pl.multiple_of(offset + 8 * k, 8), 8), lanes] = value


def zero_pads(refs, counts):
    for ref, count in zip(refs, counts):
        ref[pl.ds(0, PAD), :] = jnp.zeros((PAD, WIDE), F32)
        ref[pl.ds(PAD + count, PAD), :] = jnp.zeros((PAD, WIDE), F32)


def two_sum(a, b):
    total = a + b
    part = total - a
    return total, (a - (total - part)) + (b - part)


def halves(a):
    wide = a * 4097.0
    high = wide - (wide - a)
    return high, a - high


def two_prod(a, b):
    total = a * b
    ah, al = halves(a)
    bh, bl = halves(b)
    return total, ((ah * bh - total) + ah * bl + al * bh) + al * bl


def dd_add(a, b):
    total, rest = two_sum(a[0], b[0])
    rest = rest + (a[1] + b[1])
    high = total + rest
    return high, rest - (high - total)


def dd_mul(a, b):
    total, rest = two_prod(a[0], b[0])
    rest = rest + (a[0] * b[1] + a[1] * b[0])
    high = total + rest
    return high, rest - (high - total)


def first_kernel(vort, swirl, part, to_east, to_west, s0, s1, s2, b0, b1, b2, pairs, c3, coef):
    fill_coefs(coef)
    zero_pads((s0, s1, s2, b0, b1, b2), (EXT, EXT // 2, EXT // 4) * 2)
    s0[pl.ds(PAD, MARGIN), :] = jnp.zeros((MARGIN, WIDE), F32)
    s0[pl.ds(PAD + MARGIN + ROWS, MARGIN), :] = jnp.zeros((MARGIN, WIDE), F32)
    s0[pl.ds(PAD + MARGIN, ROWS), :COLS] = vort[...]
    s0[pl.ds(PAD + MARGIN, ROWS), COLS:] = jnp.zeros((ROWS, 128), F32)
    down_level(0, s0, b0, pairs, s1, coef)
    down_level(1, s1, b1, pairs, s2, coef)
    down_level(2, s2, b2, pairs, c3, coef)

    lane = iota((32, 128), 1)
    pick = (lane & 15) * 8
    main = jnp.zeros((32, 128), F32)
    for tile in range(TILES - 1):
        got = jnp.take_along_axis(c3[:, 128 * tile : 128 * tile + 128], pick, axis=1)
        main = jnp.where(lax.shift_right_logical(lane, 4) == tile, got, main)
    got = jnp.take_along_axis(c3[:, COLS:], pick, axis=1)
    side = jnp.where((lane < 8) | (lane >= 120), got, 0.0)
    part[:, :128] = main
    part[:, 128:] = side

    lane = iota((ROWS, 128), 1)
    last = vort[:, COLS - 128 :]
    to_east[:ROWS, :] = jnp.where(lane >= 96, last, pltpu.roll(swirl[:, COLS - 128 :], 64, 1))
    to_west[:ROWS, :] = jnp.where(lane < 32, vort[:, :128], pltpu.roll(swirl[:, :128], 64, 1))
    high = iota((32, 128), 1) >= 64
    to_east[ROWS:, :] = jnp.where(high, main, side)
    to_west[ROWS:, :] = jnp.where(high, side, main)


def level_scratch():
    shapes = [(EXT >> level) + 2 * PAD for level in range(LEVELS)]
    sources = [pltpu.VMEM((n, WIDE), F32) for n in shapes]
    blacks = [pltpu.VMEM((n, WIDE), F32) for n in shapes]
    return sources + blacks


def vmem():
    return pl.BlockSpec(memory_space=pltpu.VMEM)


def shaped(*dims):
    return jax.ShapeDtypeStruct(dims, F32)


PARAMS = dict(compiler_params=pltpu.CompilerParams(vmem_limit_bytes=40 * 2**20))


def run_first(vort, swirl):
    return pl.pallas_call(
        first_kernel,
        out_shape=(shaped(32, 256), shaped(ROWS + 32, 128), shaped(ROWS + 32, 128)),
        in_specs=[vmem()] * 2,
        out_specs=[vmem()] * 3,
        scratch_shapes=level_scratch()
        + [pltpu.VMEM((TILES * EXT, 128), F32), pltpu.VMEM((32, WIDE), F32), pltpu.VMEM((48, WIDE), F32)],
        name="down_own",
        **PARAMS,
    )(vort, swirl)


def second_kernel(part, from_west, from_east, vort, swirl, base, whole, to_next, to_prev):
    high = iota((32, 128), 1) >= 64
    west, east = from_west[ROWS:, :], from_east[ROWS:, :]
    main = part[:, :128] + jnp.where(high, east, west)
    side = part[:, 128:] + jnp.where(high, west, east)
    whole[:, :128] = main
    whole[:, 128:] = side
    lane = iota((32, 128), 1)
    for dest, first, edge, rows in ((to_next, ROWS - 32, ROWS - 1, slice(16, 32)), (to_prev, 0, 0, slice(0, 16))):
        for tile in range(TILES - 1):
            lanes = slice(128 * tile, 128 * tile + 128)
            dest[32 * tile : 32 * tile + 32, :] = vort[first : first + 32, lanes]
            row = swirl[edge : edge + 1, lanes]
            dest[320 + tile : 321 + tile, :] = row
            dest[328 + tile : 329 + tile, :] = 2.0 * base[edge : edge + 1, lanes] * row
        beyond = jnp.where(lane < 32, from_east[first : first + 32, :], 0.0)
        dest[256:288, :] = jnp.where(lane >= 96, from_west[first : first + 32, :], beyond)
        dest[288:304, :] = main[rows]
        dest[304:320, :] = side[rows]


def run_second(part, from_west, from_east, vort, swirl, base):
    return pl.pallas_call(
        second_kernel,
        out_shape=(shaped(32, 256), shaped(336, 128), shaped(336, 128)),
        in_specs=[vmem()] * 6,
        out_specs=[vmem()] * 3,
        name="pack_gz",
        **PARAMS,
    )(part, from_west, from_east, vort, swirl, base)


def third_kernel(whole, from_prev, from_next, basis, message, grid, gram_high, gram_low):
    gz, row, gz_count, row_count = place()
    grid[...] = jnp.zeros((48, 256), F32)
    grid[8:40, :] = whole[...]
    grid[0:16, :128] += from_prev[288:304, :]
    grid[0:16, 128:] += from_prev[304:320, :]
    grid[32:48, :128] += from_next[288:304, :]
    grid[32:48, 128:] += from_next[304:320, :]

    lane = iota((48, 256), 1)
    cols = jnp.where(lane < 192, lane, lane - 256)
    width = COLS >> LEVELS
    at = iota((48, 256), 0) - 12
    inside = lanes_inside(cols, width, row, row_count)
    low = jnp.where(gz == 0, 0, -64)
    high = jnp.where(gz == gz_count - 1, ROWS >> LEVELS, 128)
    inside = inside & (at >= low) & (at < high)
    spacing = float(2**LEVELS)
    radius = spacing * ((cols + row * width).astype(F32) + 0.5) + 16.0
    term = (1.5 * spacing) / radius
    east = jnp.where(inside, 0.25 + 0.25 * term, 0.0)
    west = jnp.where(inside, 0.25 - 0.25 * term, 0.0)
    quarter = jnp.where(inside, 0.25, 0.0)

    def average(x):
        total = quarter * (pltpu.roll(x, 1, 0) + pltpu.roll(x, 47, 0))
        total = total + east * pltpu.roll(x, 255, 1)
        return total + west * pltpu.roll(x, 1, 1)

    older = jnp.where(inside, grid[...], 0.0)
    newer = average(older)
    vectors = [older, newer]
    for _ in range(BASIS - 2):
        older, newer = newer, 2.0 * average(newer) - older
        vectors.append(newer)
    at = iota((32, 128), 0)
    own = (at >= 4) & (at < 28)
    parts = []
    for k in range(BASIS):
        if k < ITERS:
            basis[32 * k : 32 * k + 32, :] = vectors[k][8:40]
        masked = jnp.where(own, vectors[k][8:40, :128], 0.0)
        parts.append((masked,) + halves(masked))
    for slot, (i, j) in enumerate(PAIRS):
        a, ah, al = parts[i]
        b, bh, bl = parts[j]
        product = a * b
        error = ((ah * bh - product) + ah * bl + al * bh) + al * bl
        top, first = two_sum(product[0:8], product[8:16])
        bottom, second = two_sum(product[16:24], product[24:32])
        total, third = two_sum(top, bottom)
        rest = (error[0:8] + error[8:16]) + (error[16:24] + error[24:32])
        gram_high[8 * slot : 8 * slot + 8, :] = total
        gram_low[8 * slot : 8 * slot + 8, :] = rest + (first + second + third)
    gram_high[8 * len(PAIRS) :, :] = jnp.zeros((8 * (SLOTS - len(PAIRS)), 128), F32)
    gram_low[8 * len(PAIRS) :, :] = jnp.zeros((8 * (SLOTS - len(PAIRS)), 128), F32)
    total = None
    for s in range(8):
        term = (gram_high[pl.ds(s, SLOTS, stride=8), :], gram_low[pl.ds(s, SLOTS, stride=8), :])
        total = term if total is None else dd_add(total, term)
    for by in (64, 32, 16, 8, 4, 2, 1):
        total = dd_add(total, tuple(pltpu.roll(t, by, 1) for t in total))
    slot = iota((SLOTS, 128), 0)
    lane = iota((SLOTS, 128), 1)
    keep = lane < 0
    for number, (i, j) in enumerate(PAIRS):
        keep = keep | ((slot == number) & ((lane == BASIS * i + j) | (lane == BASIS * j + i)))
    rows = [jnp.sum(jnp.where(keep, t, 0.0), axis=0, keepdims=True) for t in total]
    odd = (iota(message.shape, 0) & 1) == 1
    message[...] = jnp.where(odd, rows[1], rows[0])


def run_third(whole, from_prev, from_next, devices):
    return pl.pallas_call(
        third_kernel,
        out_shape=(shaped(32 * ITERS, 256), shaped(2 * devices, 128)),
        in_specs=[vmem()] * 3,
        out_specs=[vmem()] * 2,
        scratch_shapes=[pltpu.VMEM((48, 256), F32), pltpu.VMEM((8 * SLOTS, 128), F32), pltpu.VMEM((8 * SLOTS, 128), F32)],
        name="basis_gram",
        **PARAMS,
    )(whole, from_prev, from_next)


def coarse_coefs(grams, cells):
    devices = grams.shape[0] // 2
    gram = (grams[pl.ds(0, devices, stride=2), :], grams[pl.ds(1, devices, stride=2), :])
    while gram[0].shape[0] > 8:
        half = gram[0].shape[0] // 2
        gram = dd_add(tuple(g[:half] for g in gram), tuple(g[half:] for g in gram))
    for by in (4, 2, 1):
        gram = dd_add(gram, tuple(pltpu.roll(g, by, 0) for g in gram))

    lane = iota((8, 128), 1)
    i = lane // BASIS
    j = lane - BASIS * i
    used = lane < BASIS * BASIS

    def weights(index):
        below = jnp.where(index == 0, 0.0, jnp.where(index == 1, 1.0, 0.5))
        above = jnp.where(index < BASIS - 1, 0.5, 0.0)
        return jnp.where(used, below, 0.0), jnp.where(used, above, 0.0)

    def image(a, weight, step):
        below, above = weight
        moved = dd_add(
            tuple(below * pltpu.roll(t, step, 1) for t in a), tuple(above * pltpu.roll(t, 128 - step, 1) for t in a)
        )
        return dd_add(a, tuple(-t for t in moved))

    weight_i, weight_j = weights(i), weights(j)
    none = jnp.zeros((8, 128), F32)
    a_i = (jnp.where(used & (i == 0), 1.0, 0.0), none)
    a_j = (jnp.where(used & (j == 0), 1.0, 0.0), none)
    first = iota((8, 128), 0) == 0
    solved = none
    tiny = float(4 ** (2 * LEVELS)) / 16.0 * cells * 1e-12
    for _ in range(ITERS):
        b_i = image(a_i, weight_i, BASIS)
        b_j = image(a_j, weight_j, 1)
        left = tuple(jnp.where(first, a, b) for a, b in zip(a_i, b_i))
        form = dd_mul(dd_mul(left, b_j), gram)
        for by in (64, 32, 16, 8, 4, 2, 1):
            form = dd_add(form, tuple(pltpu.roll(t, by, 1) for t in form))
        alpha = form[0][0:1] / (form[0][1:2] + tiny)
        alpha = jnp.broadcast_to(alpha, (8, 128))
        solved = solved + alpha * a_j[0]

        def less(a, b):
            high, rest = two_prod(alpha, b[0])
            return dd_add(a, (-high, -(rest + alpha * b[1])))

        a_i, a_j = less(a_i, b_i), less(a_j, b_j)
    return solved * (float(4**LEVELS) * 0.25)


def up_level(level, source, black, error, spread, work, coef, store):
    count = EXT >> level
    margin = MARGIN >> level
    scale = float(4**level)
    step = 2**level
    black_cells, red_cells, inside = masks(level)
    cols = local_cols()
    near = (lax.shift_right_arithmetic(cols, level) & 1) == 0

    @pl.loop(0, count // 16)
    def _(k):
        here = error[pl.ds(pl.multiple_of(8 * k, 8), 8), :]
        both = jnp.where(near, here, shift(here, step))
        for tile in range(TILES):
            value = both[:, 128 * tile : 128 * tile + 128]
            view = spread.at[pl.ds(pl.multiple_of(EXT * tile + 16 * k, 16), 16), :]
            view[pl.ds(0, 8, stride=2), :] = value
            view[pl.ds(1, 8, stride=2), :] = value

    @pl.loop(0, count // 8)
    def _(k):
        start = pl.multiple_of(PAD + 8 * k, 8)
        for tile in range(TILES):
            lanes = slice(128 * tile, 128 * tile + 128)
            add = spread[pl.ds(pl.multiple_of(EXT * tile + 8 * k, 8), 8), :]
            black[pl.ds(start, 8), lanes] += jnp.where(black_cells[:, lanes], add, 0.0)

    @pl.loop(0, count // 8)
    def _(k):
        start = pl.multiple_of(PAD + 8 * k, 8)
        beside, _ = beside_of(black, start, coef, level)
        value = scale * source[pl.ds(start, 8), :] + beside
        work[pl.ds(start, 8), :] = jnp.where(red_cells, value * row_factor(8 * k, count, margin, 0.25), 0.0)

    skip = margin // 8 if level == 0 else 0

    @pl.loop(skip, count // 8 - skip)
    def _(k):
        start = pl.multiple_of(PAD + 8 * k, 8)
        beside, here = beside_of(work, start, coef, level)
        value = scale * source[pl.ds(start, 8), :] + beside
        value = value * row_factor(8 * k, count, margin, 0.25)
        store(k - skip, jnp.where(black_cells, value, here))


def fourth_kernel(
    grams, basis, vort, from_west, from_east, from_prev, from_next, out,
    s0, s1, s2, b0, b1, b2, pairs, c3, coef, work, cells,
):
    fill_coefs(coef)
    zero_pads((s0, s1, s2, b0, b1, b2), (EXT, EXT // 2, EXT // 4) * 2)
    lane = iota((ROWS, 128), 1)
    s0[pl.ds(PAD + MARGIN, ROWS), :COLS] = vort[...]
    beyond = jnp.where(lane < 32, from_east[:ROWS, :], 0.0)
    s0[pl.ds(PAD + MARGIN, ROWS), COLS:] = jnp.where(lane >= 96, from_west[:ROWS, :], beyond)
    for tile in range(TILES):
        lanes = slice(128 * tile, 128 * tile + 128)
        s0[pl.ds(PAD, MARGIN), lanes] = from_prev[32 * tile : 32 * tile + 32, :]
        s0[pl.ds(PAD + MARGIN + ROWS, MARGIN), lanes] = from_next[32 * tile : 32 * tile + 32, :]
    down_level(0, s0, b0, pairs, s1, coef)
    down_level(1, s1, b1, pairs, s2, coef)
    down_level(2, s2, b2, pairs, c3, coef)

    solved = coarse_coefs(grams, cells)
    value = jnp.zeros((32, 256), F32)
    for k in range(ITERS):
        value = value + solved[0:1, k : k + 1] * basis[32 * k : 32 * k + 32, :]
    lane = iota((32, 128), 1)
    for tile in range(TILES):
        pick = lax.shift_right_logical(lane, 3) + 16 * tile
        half = value[:, :128]
        if tile == TILES - 1:
            pick = jnp.where(lane < 64, lax.shift_right_logical(lane, 3), lax.shift_right_logical(lane, 3) + 112)
            half = value[:, 128:]
        c3[:, 128 * tile : 128 * tile + 128] = jnp.take_along_axis(half, pick, axis=1)

    def keep(ref):
        def store(k, v):
            ref[pl.ds(pl.multiple_of(8 * k, 8), 8), :] = v

        return store

    def give(k, v):
        out[pl.ds(pl.multiple_of(8 * k, 8), 8), :] = v[:, :COLS]

    zero_pads((work,), (EXT // 4,))
    up_level(2, s2, b2, c3, pairs, work, coef, keep(s2))
    zero_pads((work,), (EXT // 2,))
    up_level(1, s1, b1, s2, pairs, work, coef, keep(s1))
    zero_pads((work,), (EXT,))
    up_level(0, s0, b0, s1, pairs, work, coef, give)


def run_fourth(grams, basis, vort, from_west, from_east, from_prev, from_next):
    cells = float((ROWS >> LEVELS) * (COLS >> LEVELS) * lax.axis_size("gz") * lax.axis_size("row"))
    return pl.pallas_call(
        functools.partial(fourth_kernel, cells=cells),
        out_shape=shaped(ROWS, COLS),
        in_specs=[vmem()] * 7,
        out_specs=vmem(),
        scratch_shapes=level_scratch()
        + [pltpu.VMEM((TILES * EXT, 128), F32), pltpu.VMEM((32, WIDE), F32), pltpu.VMEM((48, WIDE), F32)]
        + [pltpu.VMEM((EXT + 2 * PAD, WIDE), F32)],
        name="v_cycle",
        **PARAMS,
    )(grams, basis, vort, from_west, from_east, from_prev, from_next)


def rates_kernel(
    swirl, vort, base, from_west, from_east, from_prev, from_next, vel_r, vel_z, swirl_coef, vort_coef, swirl_out, vort_out
):
    tile = pl.program_id(0)
    lane = iota((ROWS, 128), 1)
    at = iota((ROWS, 128), 0)
    start = pl.multiple_of(128 * tile, 128)
    lanes = pl.ds(start, 128)
    before = pl.ds(pl.multiple_of(jnp.maximum(start - 128, 0), 128), 128)
    after = pl.ds(pl.multiple_of(jnp.minimum(start + 128, COLS - 128), 128), 128)

    def slope_r(ref, west, east):
        here = ref[:, lanes]
        left = jnp.where(tile == 0, west, pltpu.roll(ref[:, before], 1, 1))
        right = jnp.where(tile == COLS // 128 - 1, east, pltpu.roll(ref[:, after], 127, 1))
        ahead = jnp.where(lane == 127, right, pltpu.roll(here, 127, 1))
        behind = jnp.where(lane == 0, left, pltpu.roll(here, 1, 1))
        return (ahead - behind) * 0.5

    def slope_z(here, top, bottom):
        ahead = jnp.where(at == ROWS - 1, bottom, pltpu.roll(here, ROWS - 1, 0))
        behind = jnp.where(at == 0, top, pltpu.roll(here, 1, 0))
        return (ahead - behind) * 0.5

    west, east = from_west[:ROWS, :], from_east[:ROWS, :]
    u_r = slope_r(swirl, pltpu.roll(west, 65, 1), pltpu.roll(east, 63, 1))
    w_r = slope_r(vort, pltpu.roll(west, 1, 1), pltpu.roll(east, 127, 1))
    u, w = swirl[:, lanes], vort[:, lanes]
    product = 2.0 * base[:, lanes] * u
    u_z = slope_z(u, from_prev[pl.ds(320 + tile, 1), :], from_next[pl.ds(320 + tile, 1), :])
    p_z = slope_z(product, from_prev[pl.ds(328 + tile, 1), :], from_next[pl.ds(328 + tile, 1), :])
    w_z = slope_z(w, from_prev[pl.ds(32 * tile + 31, 1), :], from_next[pl.ds(32 * tile, 1), :])
    swirl_out[...] = swirl_coef[...] * u - vel_r[...] * u_r - vel_z[...] * u_z
    vort_out[...] = vort_coef[...] * w - vel_r[...] * w_r - vel_z[...] * w_z + p_z


def run_rates(swirl, vort, base, from_west, from_east, from_prev, from_next, vel_r, vel_z, swirl_coef, vort_coef):
    block = pl.BlockSpec((ROWS, 128), lambda t: (0, t))

    def whole(shape):
        return pl.BlockSpec(shape, lambda t: (0, 0))

    big = whole((ROWS, COLS))
    return pl.pallas_call(
        rates_kernel,
        grid=(COLS // 128,),
        out_shape=(shaped(ROWS, COLS), shaped(ROWS, COLS)),
        in_specs=[big] * 3 + [whole((ROWS + 32, 128))] * 2 + [whole((336, 128))] * 2 + [block] * 4,
        out_specs=[block] * 2,
        name="rates",
        cost_estimate=pl.CostEstimate(flops=30 * ROWS * COLS, bytes_accessed=36 * ROWS * COLS, transcendentals=0),
        **PARAMS,
    )(swirl, vort, base, from_west, from_east, from_prev, from_next, vel_r, vel_z, swirl_coef, vort_coef)


def both_ways(axis, up, down):
    count = lax.axis_size(axis)
    ahead = [(i, i + 1) for i in range(count - 1)]
    back = [(i + 1, i) for i in range(count - 1)]
    return lax.ppermute(up, axis, ahead), lax.ppermute(down, axis, back)


def per_device(swirl, vorticity, base_swirl, vel_r, vel_z, swirl_coef, vort_coef):
    devices = lax.axis_size("gz") * lax.axis_size("row")
    part, to_east, to_west = run_first(vorticity, swirl)
    from_west, from_east = both_ways("row", to_east, to_west)
    whole, to_next, to_prev = run_second(part, from_west, from_east, vorticity, swirl, base_swirl)
    from_prev, from_next = both_ways("gz", to_next, to_prev)
    basis, message = run_third(whole, from_prev, from_next, devices)
    grams = lax.all_to_all(message, AXES, 0, 0, tiled=True)
    potential = run_fourth(grams, basis, vorticity, from_west, from_east, from_prev, from_next)
    swirl_rate, vort_rate = run_rates(
        swirl, vorticity, base_swirl, from_west, from_east, from_prev, from_next, vel_r, vel_z, swirl_coef, vort_coef
    )
    return swirl_rate, vort_rate, potential


def solution(mesh):
    spec = P("gz", "row")
    return jax.shard_map(per_device, mesh=mesh, in_specs=(spec,) * 7, out_specs=(spec,) * 3, check_vma=False)
```

time: 590 us -> 104 us (0.18)
  the two profiles are of different devices: /device:TPU:56 before, /device:TPU:1 now
where the time goes in v1:
time: 104 us; the launch traced here: 103 us
  Pallas kernels  60.7 us (58%)
  starting transfers between devices  25.3 us (24%)
  waiting for transfers between devices  9.69 us (9%)
  local copies, waits for them, and re-layouts  6.8 us (7%)
    pallas_call x1, Pallas kernels, run_fourth(): pl.pallas_call(functools.partial(fourth_kernel, cells=cells), out_shape=s...  37.1 us
    pallas_call x1, Pallas kernels, run_first(): pl.pallas_call(first_kernel, out_shape=(shaped(32, 256), shaped(ROWS + 32...  16.1 us
    all_to_all x1, starting transfers between devices, per_device(): grams = lax.all_to_all(message, AXES, 0, 0, tiled=True)  14.3 us
    ppermute x4, starting transfers between devices, both_ways(): return (lax.ppermute(up, axis, ahead), lax.ppermute(down, axis, back))  11.1 us
    ppermute x4, waiting for transfers between devices, both_ways(): return (lax.ppermute(up, axis, ahead), lax.ppermute(down, axis, back))  9.03 us
    unnamed x18, local copies, waits for them, and re-layouts  6.8 us
    pallas_call x1, Pallas kernels, run_rates(): pl.pallas_call(rates_kernel, grid=(COLS // 128,), out_shape=(shaped(ROWS,...  5.02 us
    pallas_call x1, Pallas kernels, run_third(): pl.pallas_call(third_kernel, out_shape=(shaped(32 * ITERS, 256), shaped(2...  2.4 us
  transfers between devices with their start and end apart: 5, of which 4 were waited for; matrix products, arithmetic and copies ran while one was open for 0% of the time, Pallas kernels for 5%

profile of v1, /device:TPU:1, one launch (start us, length us, event | category | flops | bytes accessed | tf_op | source)
XLA Modules:
  0.0 103.2 jit_solution(11507895927010484850)
XLA Ops:
  0.6 0.0 copy-start
  0.6 1.1 %copy-done = f32[192,1024]{1,0:T(8,128)S(1)} copy-done((f32[192,1024]{1,0:T(8,128)S(1)}, f32[192,1024]{1,0:T(8,128)}, u32[]{:S(2)}) %copy-start) | copy-done | bytes 786456
  1.8 1.1 %copy-done.2 = f32[192,1024]{1,0:T(8,128)S(1)} copy-done((f32[192,1024]{1,0:T(8,128)S(1)}, f32[192,1024]{1,0:T(8,128)}, u32[]{:S(2)}) %copy-start.2) | copy-done | bytes 786456
  2.9 16.1 %down_own.1 = (f32[32,256]{1,0:T(8,128)S(1)}, f32[224,128]{1,0:T(8,128)S(1)}, f32[224,128]{1,0:T(8,128)S(1)}) custom-call(f32[192,1024]{1,0:T(8,128)S(1)} %copy-done, f32[192,1024]{1,0:T(8,128)S(1)} %copy-done.2), custom_call_target="tpu_custom_call" | custom-call | tf_op jit(solution)/shard_map/down_own/pallas_call | solution.py:213
  19.0 4.5 %collective-permute-start = (f32[224,128]{1,0:T(8,128)S(1)}, f32[224,128]{1,0:T(8,128)S(1)}, u32[]{:S(2)}, u32[]{:S(2)}) collective-permute-start(f32[224,128]{1,0:T(8,128)S(1)} %get-tuple-element.13), channel_id=1, source_target_pairs={{0,1},{1,2},{2,3},{3,4},{4,5},{5,6},{6,7},{7,8},{8,9},{9,10},{10,1... | collective-permute-start | bytes 344072 | tf_op jit(solution)/shard_map/ppermute | solution.py:560
  23.5 1.9 %collective-permute-start.1 = (f32[224,128]{1,0:T(8,128)S(1)}, f32[224,128]{1,0:T(8,128)S(1)}, u32[]{:S(2)}, u32[]{:S(2)}) collective-permute-start(f32[224,128]{1,0:T(8,128)S(1)} %get-tuple-element.14), channel_id=1, source_target_pairs={{1,0},{2,1},{3,2},{4,3},{5,4},{6,5},{7,6},{8,7},{9,8},{10,9},{11,1... | collective-permute-start | bytes 344072 | tf_op jit(solution)/shard_map/ppermute | solution.py:560
  25.5 0.0 collective-permute-done.from_west
  25.5 4.2 %collective-permute-done.1.from_east = f32[224,128]{1,0:T(8,128)S(1)} collective-permute-done((f32[224,128]{1,0:T(8,128)S(1)}, f32[224,128]{1,0:T(8,128)S(1)}, u32[]{:S(2)}, u32[]{:S(2)}) %collective-permute-start.1) | collective-permute-done | bytes 114720 | tf_op jit(solution)/shard_map/ppermute | solution.py:560
  29.7 3.3 %collective-permute-start.2 = (f32[336,128]{1,0:T(8,128)S(1)}, f32[336,128]{1,0:T(8,128)S(1)}, u32[]{:S(2)}, u32[]{:S(2)}) collective-permute-start(f32[336,128]{1,0:T(8,128)S(1)} %get-tuple-element.16), channel_id=1, source_target_pairs={{0,16},{16,32},{32,48},{48,64},{64,80},{80,96},{96,112},{1,17},{17... | collective-permute-start | bytes 516104 | tf_op jit(solution)/shard_map/ppermute | solution.py:560
  33.0 1.3 %collective-permute-start.3 = (f32[336,128]{1,0:T(8,128)S(1)}, f32[336,128]{1,0:T(8,128)S(1)}, u32[]{:S(2)}, u32[]{:S(2)}) collective-permute-start(f32[336,128]{1,0:T(8,128)S(1)} %get-tuple-element.17), channel_id=1, source_target_pairs={{16,0},{32,16},{48,32},{64,48},{80,64},{96,80},{112,96},{17,1},{33... | collective-permute-start | bytes 516104 | tf_op jit(solution)/shard_map/ppermute | solution.py:560
  34.3 1.0 collective-permute-done.2.from_prev
  35.4 3.8 %collective-permute-done.3.from_next = f32[336,128]{1,0:T(8,128)S(1)} collective-permute-done((f32[336,128]{1,0:T(8,128)S(1)}, f32[336,128]{1,0:T(8,128)S(1)}, u32[]{:S(2)}, u32[]{:S(2)}) %collective-permute-start.3) | collective-permute-done | bytes 172064 | tf_op jit(solution)/shard_map/ppermute | solution.py:560
  39.2 2.4 %basis_gram.1 = (f32[320,256]{1,0:T(8,128)S(1)}, f32[256,128]{1,0:T(8,128)}) custom-call(f32[32,256]{1,0:T(8,128)S(1)} %get-tuple-element.20.whole, f32[336,128]{1,0:T(8,128)S(1)} %collective-permute-done.2.from_prev, f32[336,128]{1,0:T(8,128)S(1)} %collective-permute-done.3.from_next), custom_call_target="tpu_custom_call" | custom-call | tf_op jit(solution)/shard_map/basis_gram/pallas_call | solution.py:330
  41.6 14.3 %all-to-all-start = ((f32[128,2,128]{2,1,0:T(2,128)}), f32[128,2,128]{2,1,0:T(2,128)S(1)}, u32[]{:S(2)}, u32[]{:S(2)}) async-start(f32[128,2,128]{2,1,0:T(2,128)} %bitcast), calls=%async_computation | async-start | bytes 262144 | tf_op jit(solution)/shard_map/all_to_all | solution.py:570
  55.9 0.0 copy-done.1
  55.9 0.0 copy-done.3
  55.9 0.0 copy-start.5
  55.9 1.1 %copy-done.5 = f32[192,1024]{1,0:T(8,128)S(1)} copy-done((f32[192,1024]{1,0:T(8,128)S(1)}, f32[192,1024]{1,0:T(8,128)}, u32[]{:S(2)}) %copy-start.5) | copy-done | bytes 786456
  57.0 1.1 %copy-done.6 = f32[192,1024]{1,0:T(8,128)S(1)} copy-done((f32[192,1024]{1,0:T(8,128)S(1)}, f32[192,1024]{1,0:T(8,128)}, u32[]{:S(2)}) %copy-start.6) | copy-done | bytes 786456
  58.2 1.1 %copy-done.7 = f32[192,1024]{1,0:T(8,128)S(1)} copy-done((f32[192,1024]{1,0:T(8,128)S(1)}, f32[192,1024]{1,0:T(8,128)}, u32[]{:S(2)}) %copy-start.7) | copy-done | bytes 786456
  59.3 1.1 %copy-done.8 = f32[192,1024]{1,0:T(8,128)S(1)} copy-done((f32[192,1024]{1,0:T(8,128)S(1)}, f32[192,1024]{1,0:T(8,128)}, u32[]{:S(2)}) %copy-start.8) | copy-done | bytes 786456
  60.4 5.0 %rates.1 = (f32[192,1024]{1,0:T(8,128)}, f32[192,1024]{1,0:T(8,128)}) custom-call(f32[192,1024]{1,0:T(8,128)S(1)} %copy-done.3, f32[192,1024]{1,0:T(8,128)S(1)} %copy-done.1, f32[192,1024]{1,0:T(8,128)S(1)} %copy-done.4, f32[224,128]{1,0:T(8,128)S(1)} %collective-permute-done.from_west, f32[224,128]{1,0:T(8,128)S(1)} %collective-permute-done.1.from_east, ...), custom_call_target="tpu_custom_call" | custom-call | flops 5898240 | bytes 7077888 | tf_op jit(solution)/shard_map/rates/pallas_call | solution.py:544
  65.4 0.7 all-to-all-done
  66.1 37.1 %v_cycle.1 = f32[192,1024]{1,0:T(8,128)} custom-call(f32[256,128]{1,0:T(8,128)S(1)} %bitcast.2, f32[320,256]{1,0:T(8,128)S(1)} %get-tuple-element.22.basis, f32[192,1024]{1,0:T(8,128)S(1)} %copy-done.1, f32[224,128]{1,0:T(8,128)S(1)} %collective-permute-done.from_west, f32[224,128]{1,0:T(8,128)S(1)} %collective-permute-done.1.from_east, ...), custom_call_target="tpu_custom_call" | custom-call | tf_op jit(solution)/shard_map/v_cycle/pallas_call | solution.py:488
  (9 shorter events, 0.0 us)
Async XLA Ops:
  0.6 1.1 %copy-start = (f32[192,1024]{1,0:T(8,128)S(1)}, f32[192,1024]{1,0:T(8,128)}, u32[]{:S(2)}) copy-start(f32[192,1024]{1,0:T(8,128)} %vort.7) | copy-start | bytes 2359300
  1.8 1.1 %copy-start.2 = (f32[192,1024]{1,0:T(8,128)S(1)}, f32[192,1024]{1,0:T(8,128)}, u32[]{:S(2)}) copy-start(f32[192,1024]{1,0:T(8,128)} %swirl.5) | copy-start | bytes 2359300
  2.9 26.7 %copy-start.4 = (f32[192,1024]{1,0:T(8,128)S(1)}, f32[192,1024]{1,0:T(8,128)}, u32[]{:S(2)}) copy-start(f32[192,1024]{1,0:T(8,128)} %base.3) | copy-start | bytes 2359300
  19.0 6.4 %collective-permute-start = (f32[224,128]{1,0:T(8,128)S(1)}, f32[224,128]{1,0:T(8,128)S(1)}, u32[]{:S(2)}, u32[]{:S(2)}) collective-permute-start(f32[224,128]{1,0:T(8,128)S(1)} %get-tuple-element.13), channel_id=1, source_target_pairs={{0,1},{1,2},{2,3},{3,4},{4,5},{5,6},{6,7},{7,8},{8,9},{9,10},{10,1... | collective-permute-start | bytes 344072 | tf_op jit(solution)/shard_map/ppermute | solution.py:560
  23.5 6.1 %collective-permute-start.1 = (f32[224,128]{1,0:T(8,128)S(1)}, f32[224,128]{1,0:T(8,128)S(1)}, u32[]{:S(2)}, u32[]{:S(2)}) collective-permute-start(f32[224,128]{1,0:T(8,128)S(1)} %get-tuple-element.14), channel_id=1, source_target_pairs={{1,0},{2,1},{3,2},{4,3},{5,4},{6,5},{7,6},{8,7},{9,8},{10,9},{11,1... | collective-permute-start | bytes 344072 | tf_op jit(solution)/shard_map/ppermute | solution.py:560
  29.6 26.2 %copy-start.1 = (f32[192,1024]{1,0:T(8,128)S(1)}, f32[192,1024]{1,0:T(8,128)}, u32[]{:S(2)}) copy-start(f32[192,1024]{1,0:T(8,128)} %vort.7) | copy-start | bytes 2359300
  29.7 26.2 %copy-start.3 = (f32[192,1024]{1,0:T(8,128)S(1)}, f32[192,1024]{1,0:T(8,128)}, u32[]{:S(2)}) copy-start(f32[192,1024]{1,0:T(8,128)} %swirl.5) | copy-start | bytes 2359300
  29.7 5.7 %collective-permute-start.2 = (f32[336,128]{1,0:T(8,128)S(1)}, f32[336,128]{1,0:T(8,128)S(1)}, u32[]{:S(2)}, u32[]{:S(2)}) collective-permute-start(f32[336,128]{1,0:T(8,128)S(1)} %get-tuple-element.16), channel_id=1, source_target_pairs={{0,16},{16,32},{32,48},{48,64},{64,80},{80,96},{96,112},{1,17},{17... | collective-permute-start | bytes 516104 | tf_op jit(solution)/shard_map/ppermute | solution.py:560
  33.0 6.2 %collective-permute-start.3 = (f32[336,128]{1,0:T(8,128)S(1)}, f32[336,128]{1,0:T(8,128)S(1)}, u32[]{:S(2)}, u32[]{:S(2)}) collective-permute-start(f32[336,128]{1,0:T(8,128)S(1)} %get-tuple-element.17), channel_id=1, source_target_pairs={{16,0},{32,16},{48,32},{64,48},{80,64},{96,80},{112,96},{17,1},{33... | collective-permute-start | bytes 516104 | tf_op jit(solution)/shard_map/ppermute | solution.py:560
  41.6 24.5 %all-to-all-start = ((f32[128,2,128]{2,1,0:T(2,128)}), f32[128,2,128]{2,1,0:T(2,128)S(1)}, u32[]{:S(2)}, u32[]{:S(2)}) async-start(f32[128,2,128]{2,1,0:T(2,128)} %bitcast), calls=%async_computation | async-start | bytes 262144 | tf_op jit(solution)/shard_map/all_to_all | solution.py:570
  55.9 1.1 %copy-start.5 = (f32[192,1024]{1,0:T(8,128)S(1)}, f32[192,1024]{1,0:T(8,128)}, u32[]{:S(2)}) copy-start(f32[192,1024]{1,0:T(8,128)} %vel_r.1) | copy-start | bytes 2359300
  57.0 1.1 %copy-start.6 = (f32[192,1024]{1,0:T(8,128)S(1)}, f32[192,1024]{1,0:T(8,128)}, u32[]{:S(2)}) copy-start(f32[192,1024]{1,0:T(8,128)} %vel_z.1) | copy-start | bytes 2359300
  58.2 1.1 %copy-start.7 = (f32[192,1024]{1,0:T(8,128)S(1)}, f32[192,1024]{1,0:T(8,128)}, u32[]{:S(2)}) copy-start(f32[192,1024]{1,0:T(8,128)} %swirl_coef.1) | copy-start | bytes 2359300
  59.3 1.1 %copy-start.8 = (f32[192,1024]{1,0:T(8,128)S(1)}, f32[192,1024]{1,0:T(8,128)}, u32[]{:S(2)}) copy-start(f32[192,1024]{1,0:T(8,128)} %vort_coef.1) | copy-start | bytes 2359300

commit v2 on v1

v2 whole, which is shorter than its diff:
```python
import functools

import jax
import jax.numpy as jnp
from jax import lax
from jax.experimental import pallas as pl
from jax.experimental.pallas import tpu as pltpu
from jax.sharding import PartitionSpec as P

LEVELS = 3
ITERS = 10
BASIS = ITERS + 1
PAIRS = [(i, j) for i in range(BASIS) for j in range(i, BASIS)]
SLOTS = 72
AXES = ("gz", "row")

ROWS, COLS = 192, 1024
SPAN = 32
PAD = 8
TALL = SPAN + 2 * PAD
F32 = jnp.float32


def iota(shape, dim):
    return lax.broadcasted_iota(jnp.int32, shape, dim)


def place():
    return lax.axis_index("gz"), lax.axis_index("row"), lax.axis_size("gz"), lax.axis_size("row")


def lanes_inside(cols, width, row, row_count):
    low = jnp.where(row == 0, 0, -width)
    high = jnp.where(row == row_count - 1, width, 2 * width)
    return (cols >= low) & (cols < high)


def planes_of(level):
    return 8 >> level


def plane_rows(level):
    return planes_of(level) * (planes_of(level) + 1) * TALL


def base(level, b, p):
    return (b * (planes_of(level) + 1) + p) * TALL


COEF_AT = [0, 9, 14]
COEF_ROWS = 2 * 8 * 17


def side_place():
    lane = iota((8, 128), 1)
    h = lane & 15
    return lax.shift_right_logical(lane, 4), h, jnp.where(h < 8, h + 128, h - 16)


def fill_coefs(coef):
    _, row, _, _ = place()
    lane = iota((8, 128), 1)
    p_side, _, q_side = side_place()
    for level in range(LEVELS):
        count = planes_of(level)
        spacing = float(2**level)
        for p in range(count + 1):
            if p < count:
                cols = count * lane + p
            else:
                cols = count * q_side + lax.shift_right_logical(p_side, level)
            cols = cols + row * (COLS >> level)
            term = (1.5 * spacing) / (spacing * (cols.astype(F32) + 0.5) + 16.0)
            at = 16 * (COEF_AT[level] + p)
            coef[at : at + 8, :] = 1.0 + term
            coef[at + 8 : at + 16, :] = 1.0 - term


def coefs_of(coef, level, p):
    at = 16 * (COEF_AT[level] + p)
    return coef[at : at + 8, :], coef[at + 8 : at + 16, :]


def turn(x, by):
    return pltpu.roll(x, by % 128, 1)


def view_of(ref, level, b, p, k):
    return ref.at[pl.ds(pl.multiple_of(base(level, b, p) + 8 * k, 8), 24), :]


def here_of(ref, level, b, p, k):
    return view_of(ref, level, b, p, k)[8:16, :]


def put(ref, level, b, p, k, value):
    ref[pl.ds(pl.multiple_of(base(level, b, p) + PAD + 8 * k, 8), 8), :] = value


def vertical(ref, level, b, p, k):
    count = planes_of(level)
    above = view_of(ref, level, b - 1, p, k)[8:16, :] if b > 0 else view_of(ref, level, count - 1, p, k)[7:15, :]
    below = view_of(ref, level, b + 1, p, k)[8:16, :] if b < count - 1 else view_of(ref, level, 0, p, k)[9:17, :]
    return above + below


def beside_main(ref, coef, level, b, p, k):
    count = planes_of(level)
    step = 2**level
    lane = iota((8, 128), 1)
    east, west = coefs_of(coef, level, p)
    side = None
    if p == 0 or p == count - 1:
        side = here_of(ref, level, b, count, k)
    if p < count - 1:
        right = here_of(ref, level, b, p + 1, k)
    else:
        right = jnp.where(lane == 127, turn(side, -1), turn(here_of(ref, level, b, 0, k), -1))
    if p > 0:
        left = here_of(ref, level, b, p - 1, k)
    else:
        left = jnp.where(lane == 0, turn(side, 16 * step - 15), turn(here_of(ref, level, b, count - 1, k), 1))
    return (vertical(ref, level, b, p, k) + east * right) + west * left


def beside_side(ref, coef, level, b, k):
    count = planes_of(level)
    step = 2**level
    lane = iota((8, 128), 1)
    east, west = coefs_of(coef, level, count)
    side = here_of(ref, level, b, count, k)
    first, last = here_of(ref, level, b, 0, k), here_of(ref, level, b, count - 1, k)
    edge = 16 * (8 - step)
    right = jnp.where(lane >= edge, turn(side, -(16 * step + 1)), turn(side, -16 * step))
    right = jnp.where(lane == edge + 15, turn(first, edge + 15), right)
    left = jnp.where(lane < 16, turn(side, 16 * step + 1), turn(side, 16 * step))
    left = jnp.where(lane == 0, turn(last, 1), left)
    return (vertical(ref, level, b, count, k) + east * right) + west * left


def odd_side(level, b):
    p_side, _, _ = side_place()
    return ((lax.shift_right_logical(p_side, level) + b) & 1) == 1


def inside_factors(k):
    gz, row, gz_count, row_count = place()
    low = jnp.where(gz == 0, 4, 0)
    high = jnp.where(gz == gz_count - 1, SPAN - 4, SPAN)
    at = iota((8, 128), 0) + 8 * k
    main = jnp.where((at >= low) & (at < high), 1.0, 0.0).astype(F32)
    _, h, _ = side_place()
    first = jnp.where(row == row_count - 1, 8, 0)
    after = jnp.where(row == 0, 8, 16)
    return main, jnp.where((h >= first) & (h < after), main, 0.0)


def chunks(body):
    pl.loop(0, SPAN // 8)(body)


def down_level(level, source, black, coarse, coef):
    count = planes_of(level)

    @chunks
    def _(k):
        main, side = inside_factors(k)
        main, side = 0.25 * main, 0.25 * side
        for b in range(count):
            for p in range(1 - b % 2, count, 2):
                beside = beside_main(source, coef, level, b, p, k)
                put(black, level, b, p, k, (here_of(source, level, b, p, k) + 0.25 * beside) * main)
            beside = beside_side(source, coef, level, b, k)
            value = (here_of(source, level, b, count, k) + 0.25 * beside) * side
            put(black, level, b, count, k, jnp.where(odd_side(level, b), value, 0.0))

    step = 2**level
    p_side, _, _ = side_place()
    keep = (lax.shift_right_logical(p_side, level) & 1) == 0

    @chunks
    def _(k):
        main, side = inside_factors(k)
        for b in range(0, count, 2):
            for p in range(0, count, 2):
                value = beside_main(black, coef, level, b, p, k) + beside_main(black, coef, level, b + 1, p + 1, k)
                put(coarse, level + 1, b // 2, p // 2, k, value * main)
            even = beside_side(black, coef, level, b, k)
            odd = turn(beside_side(black, coef, level, b + 1, k), -16 * step)
            put(coarse, level + 1, b // 2, count // 2, k, jnp.where(keep, (even + odd) * side, 0.0))


def up_level(level, source, black, error, coef):
    count = planes_of(level)
    step = 2**level
    p_side, _, _ = side_place()
    moved = (lax.shift_right_logical(p_side, level) & 1) == 1

    @chunks
    def _(k):
        for b in range(count):
            for p in range(1 - b % 2, count, 2):
                value = here_of(error, level + 1, b // 2, p // 2, k)
                put(black, level, b, p, k, here_of(black, level, b, p, k) + value)
            value = here_of(error, level + 1, b // 2, count // 2, k)
            value = jnp.where(moved, turn(value, 16 * step), value)
            value = here_of(black, level, b, count, k) + value
            put(black, level, b, count, k, jnp.where(odd_side(level, b), value, 0.0))

    for colour in (0, 1):

        @chunks
        def _(k):
            main, side = inside_factors(k)
            main, side = 0.25 * main, 0.25 * side
            for b in range(count):
                for p in range((b + colour) % 2, count, 2):
                    beside = beside_main(black, coef, level, b, p, k)
                    put(black, level, b, p, k, (here_of(source, level, b, p, k) + beside) * main)
                beside = beside_side(black, coef, level, b, k)
                value = (here_of(source, level, b, count, k) + beside) * side
                mine = odd_side(level, b + 1 - colour)
                put(black, level, b, count, k, jnp.where(mine, value, here_of(black, level, b, count, k)))


def zero_pads(refs):
    for level, ref in refs:
        for b in range(planes_of(level)):
            for p in range(planes_of(level) + 1):
                at = base(level, b, p)
                ref[at : at + PAD, :] = jnp.zeros((PAD, 128), F32)
                ref[at + PAD + SPAN : at + TALL, :] = jnp.zeros((PAD, 128), F32)


def permuted(x):
    lane = iota(x.shape, 1)
    return jnp.take_along_axis(x, (lane & 15) * 8 + lax.shift_right_logical(lane, 4), axis=1)


def restored(x):
    lane = iota(x.shape, 1)
    return jnp.take_along_axis(x, (lane & 7) * 16 + lax.shift_right_logical(lane, 3), axis=1)


def exchanged(tiles):
    tiles = list(tiles)
    lane = iota(tiles[0].shape, 1)
    for bit in range(3):
        far = 2**bit
        low = (lax.shift_right_logical(lane, 4 + bit) & 1) == 0
        for k in range(8):
            if not k & far:
                a, c = tiles[k], tiles[k + far]
                tiles[k] = jnp.where(low, a, turn(c, 16 * far))
                tiles[k + far] = jnp.where(low, turn(a, -16 * far), c)
    return tiles


def two_sum(a, b):
    total = a + b
    part = total - a
    return total, (a - (total - part)) + (b - part)


def halves(a):
    wide = a * 4097.0
    high = wide - (wide - a)
    return high, a - high


def two_prod(a, b):
    total = a * b
    ah, al = halves(a)
    bh, bl = halves(b)
    return total, ((ah * bh - total) + ah * bl + al * bh) + al * bl


def dd_add(a, b):
    total, rest = two_sum(a[0], b[0])
    rest = rest + (a[1] + b[1])
    high = total + rest
    return high, rest - (high - total)


def dd_mul(a, b):
    total, rest = two_prod(a[0], b[0])
    rest = rest + (a[0] * b[1] + a[1] * b[0])
    high = total + rest
    return high, rest - (high - total)


def first_kernel(vort, swirl_first, swirl_last, part, to_east, to_west, planes, s0, s1, s2, s3, b0, b1, b2, coef):
    fill_coefs(coef)
    zero_pads(((0, s0), (1, s1), (2, s2), (0, b0), (1, b1), (2, b2)))
    low = (iota((8, 128), 1) & 15) < 8
    for b in range(8):
        for p in range(8):
            at = base(0, b, p) + PAD
            s0[at : at + 4, :] = jnp.zeros((4, 128), F32)
            s0[at + 28 : at + 32, :] = jnp.zeros((4, 128), F32)
        at = base(0, b, 8) + PAD
        s0[at : at + SPAN, :] = jnp.zeros((SPAN, 128), F32)
    for g in range(ROWS // 8):
        rows = slice(8 * g, 8 * g + 8)
        tiles = [permuted(vort[rows, 128 * k : 128 * k + 128]) for k in range(8)]
        to_east[rows, :] = jnp.where(low, turn(swirl_last[rows, :], 65), tiles[7])
        to_west[rows, :] = jnp.where(low, tiles[0], turn(swirl_first[rows, :], 8))
        for p, tile in enumerate(exchanged(tiles)):
            s0[pl.ds(base(0, 0, p) + PAD + 4 + g, 8, stride=9 * TALL), :] = tile
    for b in range(8):
        for p in range(8):
            at = base(0, b, p) + PAD + 4
            planes[24 * (8 * b + p) : 24 * (8 * b + p) + 24, :] = s0[at : at + 24, :]
    down_level(0, s0, b0, s1, coef)
    down_level(1, s1, b1, s2, coef)
    down_level(2, s2, b2, s3, coef)

    scale = 1.0 / float(4**LEVELS)
    main = s3[PAD : PAD + SPAN, :] * scale
    side = s3[TALL + PAD : TALL + PAD + SPAN, :] * scale
    lane = iota((SPAN, 128), 1)
    side = jnp.where(lane < 8, side, jnp.where(lane >= 120, turn(side, 112), 0.0))
    part[:, :128] = main
    part[:, 128:] = side
    high = lane >= 64
    to_east[ROWS:, :] = jnp.where(high, main, side)
    to_west[ROWS:, :] = jnp.where(high, side, main)


def level_scratch():
    sources = [pltpu.VMEM((plane_rows(level), 128), F32) for level in range(LEVELS + 1)]
    blacks = [pltpu.VMEM((plane_rows(level), 128), F32) for level in range(LEVELS)]
    return sources + blacks + [pltpu.VMEM((COEF_ROWS, 128), F32)]


def vmem():
    return pl.BlockSpec(memory_space=pltpu.VMEM)


def shaped(*dims):
    return jax.ShapeDtypeStruct(dims, F32)


def params(mebibytes):
    return dict(compiler_params=pltpu.CompilerParams(vmem_limit_bytes=mebibytes * 2**20))


def run_first(vort, swirl):
    return pl.pallas_call(
        first_kernel,
        grid=(1,),
        out_shape=(shaped(32, 256), shaped(ROWS + 32, 128), shaped(ROWS + 32, 128), shaped(64 * 24, 128)),
        in_specs=[
            pl.BlockSpec((ROWS, COLS), lambda t: (0, 0)),
            pl.BlockSpec((ROWS, 128), lambda t: (0, 0)),
            pl.BlockSpec((ROWS, 128), lambda t: (0, COLS // 128 - 1)),
        ],
        out_specs=[vmem()] * 4,
        scratch_shapes=level_scratch(),
        name="down_own",
        **params(40),
    )(vort, swirl, swirl)


def second_kernel(part, from_west, from_east, planes, vort_top, vort_end, swirl_top, swirl_end, base_top, base_end, whole, to_next, to_prev):
    high = iota((32, 128), 1) >= 64
    west, east = from_west[ROWS:, :], from_east[ROWS:, :]
    main = part[:, :128] + jnp.where(high, east, west)
    side = part[:, 128:] + jnp.where(high, west, east)
    whole[:, :128] = main
    whole[:, 128:] = side
    low = (iota((4, 128), 1) & 15) < 8
    ends = ((to_next, 20, 7, slice(16, 32), vort_end, swirl_end, base_end), (to_prev, 0, 0, slice(0, 16), vort_top, swirl_top, base_top))
    for dest, g, edge, rows, vort, swirl, back in ends:
        for b in range(8):
            for p in range(8):
                at = 4 * (9 * b + p)
                dest[at : at + 4, :] = planes[24 * (8 * b + p) + g : 24 * (8 * b + p) + g + 4, :]
            at = 4 * (9 * b + 8)
            beyond = (from_east[pl.ds(8 * g + b, 4, stride=8), :], from_west[pl.ds(8 * g + b, 4, stride=8), :])
            dest[at : at + 4, :] = jnp.where(low, beyond[0], beyond[1])
        for tile in range(COLS // 128):
            lanes = slice(128 * tile, 128 * tile + 128)
            row = swirl[edge : edge + 1, lanes]
            dest[320 + tile : 321 + tile, :] = row
            dest[328 + tile : 329 + tile, :] = 2.0 * back[edge : edge + 1, lanes] * row
            dest[336 + tile : 337 + tile, :] = vort[edge : edge + 1, lanes]
        dest[288:304, :] = main[rows]
        dest[304:320, :] = side[rows]


def run_second(part, from_west, from_east, planes, vort, swirl, back):
    top = pl.BlockSpec((8, COLS), lambda t: (0, 0))
    end = pl.BlockSpec((8, COLS), lambda t: (ROWS // 8 - 1, 0))
    return pl.pallas_call(
        second_kernel,
        grid=(1,),
        out_shape=(shaped(32, 256), shaped(344, 128), shaped(344, 128)),
        in_specs=[vmem()] * 4 + [top, end] * 3,
        out_specs=[vmem()] * 3,
        name="pack_gz",
        **params(40),
    )(part, from_west, from_east, planes, vort, vort, swirl, swirl, back, back)


def third_kernel(whole, from_prev, from_next, basis, message, grid, gram_high, gram_low):
    gz, row, gz_count, row_count = place()
    grid[...] = jnp.zeros((48, 256), F32)
    grid[8:40, :] = whole[...]
    grid[0:16, :128] += from_prev[288:304, :]
    grid[0:16, 128:] += from_prev[304:320, :]
    grid[32:48, :128] += from_next[288:304, :]
    grid[32:48, 128:] += from_next[304:320, :]

    lane = iota((48, 256), 1)
    cols = jnp.where(lane < 192, lane, lane - 256)
    width = COLS >> LEVELS
    at = iota((48, 256), 0) - 12
    inside = lanes_inside(cols, width, row, row_count)
    low = jnp.where(gz == 0, 0, -64)
    high = jnp.where(gz == gz_count - 1, ROWS >> LEVELS, 128)
    inside = inside & (at >= low) & (at < high)
    spacing = float(2**LEVELS)
    radius = spacing * ((cols + row * width).astype(F32) + 0.5) + 16.0
    term = (1.5 * spacing) / radius
    east = jnp.where(inside, 0.25 + 0.25 * term, 0.0)
    west = jnp.where(inside, 0.25 - 0.25 * term, 0.0)
    quarter = jnp.where(inside, 0.25, 0.0)

    def average(x):
        total = quarter * (pltpu.roll(x, 1, 0) + pltpu.roll(x, 47, 0))
        total = total + east * pltpu.roll(x, 255, 1)
        return total + west * pltpu.roll(x, 1, 1)

    source = jnp.where(inside, grid[...], 0.0)
    older = source - average(source)
    newer = average(older)
    vectors = [source, older, newer]
    for _ in range(BASIS - 3):
        older, newer = newer, 2.0 * average(newer) - older
        vectors.append(newer)
    at = iota((32, 128), 0)
    own = (at >= 4) & (at < 28)
    parts = []
    for k in range(BASIS):
        if k < ITERS:
            basis[32 * k : 32 * k + 32, :] = vectors[k][8:40]
        masked = jnp.where(own, vectors[k][8:40, :128], 0.0)
        parts.append((masked,) + halves(masked))
    for slot, (i, j) in enumerate(PAIRS):
        a, ah, al = parts[i]
        b, bh, bl = parts[j]
        product = a * b
        error = ((ah * bh - product) + ah * bl + al * bh) + al * bl
        top, first = two_sum(product[0:8], product[8:16])
        bottom, second = two_sum(product[16:24], product[24:32])
        total, third = two_sum(top, bottom)
        rest = (error[0:8] + error[8:16]) + (error[16:24] + error[24:32])
        gram_high[8 * slot : 8 * slot + 8, :] = total
        gram_low[8 * slot : 8 * slot + 8, :] = rest + (first + second + third)
    gram_high[8 * len(PAIRS) :, :] = jnp.zeros((8 * (SLOTS - len(PAIRS)), 128), F32)
    gram_low[8 * len(PAIRS) :, :] = jnp.zeros((8 * (SLOTS - len(PAIRS)), 128), F32)
    total = None
    for s in range(8):
        term = (gram_high[pl.ds(s, SLOTS, stride=8), :], gram_low[pl.ds(s, SLOTS, stride=8), :])
        total = term if total is None else dd_add(total, term)
    for by in (64, 32, 16, 8, 4, 2, 1):
        total = dd_add(total, tuple(pltpu.roll(t, by, 1) for t in total))
    slot = iota((SLOTS, 128), 0)
    lane = iota((SLOTS, 128), 1)
    keep = lane < 0
    for number, (i, j) in enumerate(PAIRS):
        keep = keep | ((slot == number) & ((lane == BASIS * i + j) | (lane == BASIS * j + i)))
    rows = [jnp.sum(jnp.where(keep, t, 0.0), axis=0, keepdims=True) for t in total]
    odd = (iota(message.shape, 0) & 1) == 1
    message[...] = jnp.where(odd, rows[1], rows[0])


def run_third(whole, from_prev, from_next, devices):
    return pl.pallas_call(
        third_kernel,
        out_shape=(shaped(32 * ITERS, 256), shaped(2 * devices, 128)),
        in_specs=[vmem()] * 3,
        out_specs=[vmem()] * 2,
        scratch_shapes=[pltpu.VMEM((48, 256), F32), pltpu.VMEM((8 * SLOTS, 128), F32), pltpu.VMEM((8 * SLOTS, 128), F32)],
        name="basis_gram",
        **params(40),
    )(whole, from_prev, from_next)


def coarse_coefs(grams, cells):
    devices = grams.shape[0] // 2
    gram = (grams[pl.ds(0, devices, stride=2), :], grams[pl.ds(1, devices, stride=2), :])
    while gram[0].shape[0] > 8:
        half = gram[0].shape[0] // 2
        gram = dd_add(tuple(g[:half] for g in gram), tuple(g[half:] for g in gram))
    for by in (4, 2, 1):
        gram = dd_add(gram, tuple(pltpu.roll(g, by, 0) for g in gram))

    lane = iota((8, 128), 1)
    i = lane // BASIS
    j = lane - BASIS * i
    used = lane < BASIS * BASIS

    def weights(index):
        below = jnp.where(index == 0, 0.0, jnp.where(index == 1, -1.0, jnp.where(index == 2, 1.0, 0.5)))
        above = jnp.where((index > 0) & (index < BASIS - 1), 0.5, 0.0)
        same = jnp.where(index > 0, 1.0, 0.0)
        return tuple(jnp.where(used, t, 0.0) for t in (below, above, same))

    def image(a, weight, step):
        below, above, same = weight
        moved = dd_add(
            tuple(below * pltpu.roll(t, step, 1) for t in a), tuple(above * pltpu.roll(t, 128 - step, 1) for t in a)
        )
        return dd_add(tuple(same * t for t in a), tuple(-t for t in moved))

    weight_i, weight_j = weights(i), weights(j)
    none = jnp.zeros((8, 128), F32)
    a_i = (jnp.where(used & (i == 0), 1.0, 0.0), none)
    a_j = (jnp.where(used & (j == 0), 1.0, 0.0), none)
    first = iota((8, 128), 0) == 0
    solved = none
    tiny = float(4 ** (2 * LEVELS)) / 16.0 * cells * 1e-12
    for _ in range(ITERS):
        b_i = image(a_i, weight_i, BASIS)
        b_j = image(a_j, weight_j, 1)
        left = tuple(jnp.where(first, a, b) for a, b in zip(a_i, b_i))
        form = dd_mul(dd_mul(left, b_j), gram)
        for by in (64, 32, 16, 8, 4, 2, 1):
            form = dd_add(form, tuple(pltpu.roll(t, by, 1) for t in form))
        alpha = form[0][0:1] / (form[0][1:2] + tiny)
        alpha = jnp.broadcast_to(alpha, (8, 128))
        solved = solved + alpha * a_j[0]

        def less(a, b):
            high, rest = two_prod(alpha, b[0])
            return dd_add(a, (-high, -(rest + alpha * b[1])))

        a_i, a_j = less(a_i, b_i), less(a_j, b_j)
    return solved * (float(4**LEVELS) * 0.25)


def fourth_kernel(
    grams, basis, planes, from_west, from_east, from_prev, from_next, out,
    s0, s1, s2, s3, b0, b1, b2, coef, *, cells,
):
    fill_coefs(coef)
    zero_pads(((0, s0), (1, s1), (2, s2), (0, b0), (1, b1), (2, b2)))
    low = (iota((24, 128), 1) & 15) < 8
    for b in range(8):
        for p in range(9):
            at = base(0, b, p) + PAD
            edge = 4 * (9 * b + p)
            s0[at : at + 4, :] = from_prev[edge : edge + 4, :]
            s0[at + 28 : at + 32, :] = from_next[edge : edge + 4, :]
            if p < 8:
                s0[at + 4 : at + 28, :] = planes[24 * (8 * b + p) : 24 * (8 * b + p) + 24, :]
            else:
                beyond = (from_east[pl.ds(b, 24, stride=8), :], from_west[pl.ds(b, 24, stride=8), :])
                s0[at + 4 : at + 28, :] = jnp.where(low, beyond[0], beyond[1])
    down_level(0, s0, b0, s1, coef)
    down_level(1, s1, b1, s2, coef)
    down_level(2, s2, b2, s3, coef)

    solved = coarse_coefs(grams, cells)
    value = jnp.zeros((32, 256), F32)
    for k in range(ITERS):
        value = value + solved[0:1, k : k + 1] * basis[32 * k : 32 * k + 32, :]
    lane = iota((SPAN, 128), 1)
    side = value[:, 128:]
    s3[PAD : PAD + SPAN, :] = value[:, :128]
    s3[TALL + PAD : TALL + PAD + SPAN, :] = jnp.where(lane < 8, side, turn(side, 16))
    up_level(2, s2, b2, s3, coef)
    up_level(1, s1, b1, b2, coef)
    up_level(0, s0, b0, b1, coef)
    for g in range(ROWS // 8):
        tiles = [b0[pl.ds(base(0, 0, p) + PAD + 4 + g, 8, stride=9 * TALL), :] for p in range(8)]
        for k, tile in enumerate(exchanged(tiles)):
            out[8 * g : 8 * g + 8, 128 * k : 128 * k + 128] = restored(tile)


def run_fourth(grams, basis, planes, from_west, from_east, from_prev, from_next):
    cells = float((ROWS >> LEVELS) * (COLS >> LEVELS) * lax.axis_size("gz") * lax.axis_size("row"))
    return pl.pallas_call(
        functools.partial(fourth_kernel, cells=cells),
        out_shape=shaped(ROWS, COLS),
        in_specs=[vmem()] * 7,
        out_specs=vmem(),
        scratch_shapes=level_scratch(),
        name="v_cycle",
        **params(40),
    )(grams, basis, planes, from_west, from_east, from_prev, from_next)


def rates_kernel(
    swirl, vort, back, from_west, from_east, from_prev, from_next, vel_r, vel_z, swirl_coef, vort_coef, swirl_out, vort_out
):
    tile = pl.program_id(0)
    lane = iota((ROWS, 128), 1)
    at = iota((ROWS, 128), 0)
    start = pl.multiple_of(128 * tile, 128)
    lanes = pl.ds(start, 128)
    before = pl.ds(pl.multiple_of(jnp.maximum(start - 128, 0), 128), 128)
    after = pl.ds(pl.multiple_of(jnp.minimum(start + 128, COLS - 128), 128), 128)

    def slope_r(ref, west, east):
        here = ref[:, lanes]
        left = jnp.where(tile == 0, west, pltpu.roll(ref[:, before], 1, 1))
        right = jnp.where(tile == COLS // 128 - 1, east, pltpu.roll(ref[:, after], 127, 1))
        ahead = jnp.where(lane == 127, right, pltpu.roll(here, 127, 1))
        behind = jnp.where(lane == 0, left, pltpu.roll(here, 1, 1))
        return (ahead - behind) * 0.5

    def slope_z(here, top, bottom):
        ahead = jnp.where(at == ROWS - 1, bottom, pltpu.roll(here, ROWS - 1, 0))
        behind = jnp.where(at == 0, top, pltpu.roll(here, 1, 0))
        return (ahead - behind) * 0.5

    west, east = from_west[:ROWS, :], from_east[:ROWS, :]
    u_r = slope_r(swirl, turn(west, 64), turn(east, 119))
    w_r = slope_r(vort, pltpu.roll(west, 1, 1), pltpu.roll(east, 127, 1))
    u, w = swirl[:, lanes], vort[:, lanes]
    product = 2.0 * back[:, lanes] * u
    u_z = slope_z(u, from_prev[pl.ds(320 + tile, 1), :], from_next[pl.ds(320 + tile, 1), :])
    p_z = slope_z(product, from_prev[pl.ds(328 + tile, 1), :], from_next[pl.ds(328 + tile, 1), :])
    w_z = slope_z(w, from_prev[pl.ds(336 + tile, 1), :], from_next[pl.ds(336 + tile, 1), :])
    swirl_out[...] = swirl_coef[...] * u - vel_r[...] * u_r - vel_z[...] * u_z
    vort_out[...] = vort_coef[...] * w - vel_r[...] * w_r - vel_z[...] * w_z + p_z


def run_rates(swirl, vort, back, from_west, from_east, from_prev, from_next, vel_r, vel_z, swirl_coef, vort_coef):
    block = pl.BlockSpec((ROWS, 128), lambda t: (0, t))

    def whole(shape):
        return pl.BlockSpec(shape, lambda t: (0, 0))

    big = whole((ROWS, COLS))
    return pl.pallas_call(
        rates_kernel,
        grid=(COLS // 128,),
        out_shape=(shaped(ROWS, COLS), shaped(ROWS, COLS)),
        in_specs=[big] * 3 + [whole((ROWS + 32, 128))] * 2 + [whole((344, 128))] * 2 + [block] * 4,
        out_specs=[block] * 2,
        name="rates",
        cost_estimate=pl.CostEstimate(flops=30 * ROWS * COLS, bytes_accessed=36 * ROWS * COLS, transcendentals=0),
        **params(60),
    )(swirl, vort, back, from_west, from_east, from_prev, from_next, vel_r, vel_z, swirl_coef, vort_coef)


def both_ways(axis, up, down):
    count = lax.axis_size(axis)
    ahead = [(i, i + 1) for i in range(count - 1)]
    back = [(i + 1, i) for i in range(count - 1)]
    return lax.ppermute(up, axis, ahead), lax.ppermute(down, axis, back)


def per_device(swirl, vorticity, base_swirl, vel_r, vel_z, swirl_coef, vort_coef):
    devices = lax.axis_size("gz") * lax.axis_size("row")
    part, to_east, to_west, planes = run_first(vorticity, swirl)
    from_west, from_east = both_ways("row", to_east, to_west)
    whole, to_next, to_prev = run_second(part, from_west, from_east, planes, vorticity, swirl, base_swirl)
    from_prev, from_next = both_ways("gz", to_next, to_prev)
    basis, message = run_third(whole, from_prev, from_next, devices)
    grams = lax.all_to_all(message, AXES, 0, 0, tiled=True)
    potential = run_fourth(grams, basis, planes, from_west, from_east, from_prev, from_next)
    swirl_rate, vort_rate = run_rates(
        swirl, vorticity, base_swirl, from_west, from_east, from_prev, from_next, vel_r, vel_z, swirl_coef, vort_coef
    )
    return swirl_rate, vort_rate, potential


def solution(mesh):
    spec = P("gz", "row")
    return jax.shard_map(per_device, mesh=mesh, in_specs=(spec,) * 7, out_specs=(spec,) * 3, check_vma=False)
```

time: 104 us -> 79.4 us (0.76)
  Pallas kernels: 60.7 us -> 39.1 us
  local copies, waits for them, and re-layouts: 6.8 us -> 2.83 us
  waiting for transfers between devices: 9.69 us -> 10.9 us
    pallas_call x1, Pallas kernels: 37.1 us -> 20.8 us  [run_fourth(): pl.pallas_call(functools.partial(fourth_kernel, cells=cells), out_shape=s...]
    pallas_call x2, Pallas kernels: 16.1 us -> 7.56 us  [the longest x1 7.47 us: run_first(): pl.pallas_call(first_kernel, grid=(1,), out_shape=(shaped(32, 256), shape...]
    unnamed x18 -> x22, local copies, waits for them, and re-layouts: 6.8 us -> 2.83 us
    pallas_call x1, Pallas kernels: 5.02 us -> 8.35 us  [run_rates(): pl.pallas_call(rates_kernel, grid=(COLS // 128,), out_shape=(shaped(ROWS,...]
    all_to_all x1, waiting for transfers between devices: 0.66 us -> 1.84 us  [per_device(): grams = lax.all_to_all(message, AXES, 0, 0, tiled=True)]
  transfers between devices with their start and end apart: 5 -> 5, of which waited for: 4 -> 4; matrix products, arithmetic and copies ran while one was open for 0% -> 0% of each run, Pallas kernels for 5% -> 11%
where the time goes in v2:
time: 79.4 us; the launch traced here: 78.9 us
  Pallas kernels  39.1 us (49%)
  starting transfers between devices  25.2 us (32%)
  waiting for transfers between devices  10.9 us (14%)
  local copies, waits for them, and re-layouts  2.83 us (4%)
    pallas_call x1, Pallas kernels, run_fourth(): pl.pallas_call(functools.partial(fourth_kernel, cells=cells), out_shape=s...  20.8 us
    all_to_all x1, starting transfers between devices, per_device(): grams = lax.all_to_all(message, AXES, 0, 0, tiled=True)  14.3 us
    ppermute x4, starting transfers between devices, both_ways(): return (lax.ppermute(up, axis, ahead), lax.ppermute(down, axis, back))  10.9 us
    ppermute x4, waiting for transfers between devices, both_ways(): return (lax.ppermute(up, axis, ahead), lax.ppermute(down, axis, back))  9.06 us
    pallas_call x1, Pallas kernels, run_rates(): pl.pallas_call(rates_kernel, grid=(COLS // 128,), out_shape=(shaped(ROWS,...  8.35 us
    pallas_call x1, Pallas kernels, run_first(): pl.pallas_call(first_kernel, grid=(1,), out_shape=(shaped(32, 256), shape...  7.47 us
    unnamed x22, local copies, waits for them, and re-layouts  2.83 us
    pallas_call x1, Pallas kernels, run_third(): pl.pallas_call(third_kernel, out_shape=(shaped(32 * ITERS, 256), shaped(2...  2.39 us
  transfers between devices with their start and end apart: 5, of which 4 were waited for; matrix products, arithmetic and copies ran while one was open for 0% of the time, Pallas kernels for 11%

profile of v2, /device:TPU:1, one launch (start us, length us, event | category | flops | bytes accessed | tf_op | source)
XLA Modules:
  0.0 78.9 jit_solution(8627407346064759159)
XLA Ops:
  0.6 0.0 copy-start
  0.6 1.1 %copy-done = f32[192,1024]{1,0:T(8,128)S(1)} copy-done((f32[192,1024]{1,0:T(8,128)S(1)}, f32[192,1024]{1,0:T(8,128)}, u32[]{:S(2)}) %copy-start) | copy-done | bytes 786456
  1.8 1.1 %copy-done.1 = f32[192,1024]{1,0:T(8,128)S(1)} copy-done((f32[192,1024]{1,0:T(8,128)S(1)}, f32[192,1024]{1,0:T(8,128)}, u32[]{:S(2)}) %copy-start.1) | copy-done | bytes 786456
  2.9 7.5 %down_own.1 = (f32[32,256]{1,0:T(8,128)S(1)}, f32[224,128]{1,0:T(8,128)S(1)}, f32[224,128]{1,0:T(8,128)S(1)}, f32[1536,128]{1,0:T(8,128)S(1)}) custom-call(f32[192,1024]{1,0:T(8,128)S(1)} %copy-done.1, f32[192,1024]{1,0:T(8,128)S(1)} %copy-done, f32[192,1024]{1,0:T(8,128)S(1)} %copy-done), custom_call_target="tpu_custom_call" | custom-call | tf_op jit(solution)/shard_map/down_own/pallas_call | solution.py:349
  10.4 4.5 %collective-permute-start = (f32[224,128]{1,0:T(8,128)S(1)}, f32[224,128]{1,0:T(8,128)S(1)}, u32[]{:S(2)}, u32[]{:S(2)}) collective-permute-start(f32[224,128]{1,0:T(8,128)S(1)} %get-tuple-element.14), channel_id=1, source_target_pairs={{0,1},{1,2},{2,3},{3,4},{4,5},{5,6},{6,7},{7,8},{8,9},{9,10},{10,1... | collective-permute-start | bytes 344072 | tf_op jit(solution)/shard_map/ppermute | solution.py:655
  14.9 1.9 %collective-permute-start.1 = (f32[224,128]{1,0:T(8,128)S(1)}, f32[224,128]{1,0:T(8,128)S(1)}, u32[]{:S(2)}, u32[]{:S(2)}) collective-permute-start(f32[224,128]{1,0:T(8,128)S(1)} %get-tuple-element.15), channel_id=1, source_target_pairs={{1,0},{2,1},{3,2},{4,3},{5,4},{6,5},{7,6},{8,7},{9,8},{10,9},{11,1... | collective-permute-start | bytes 344072 | tf_op jit(solution)/shard_map/ppermute | solution.py:655
  16.8 0.0 collective-permute-done.from_west
  16.8 4.2 %collective-permute-done.1.from_east = f32[224,128]{1,0:T(8,128)S(1)} collective-permute-done((f32[224,128]{1,0:T(8,128)S(1)}, f32[224,128]{1,0:T(8,128)S(1)}, u32[]{:S(2)}, u32[]{:S(2)}) %collective-permute-start.1) | collective-permute-done | bytes 114720 | tf_op jit(solution)/shard_map/ppermute | solution.py:655
  21.0 0.1 pack_gz.1
  21.1 0.5 copy-done.9
  21.6 3.2 %collective-permute-start.2 = (f32[344,128]{1,0:T(8,128)S(1)}, f32[344,128]{1,0:T(8,128)S(1)}, u32[]{:S(2)}, u32[]{:S(2)}) collective-permute-start(f32[344,128]{1,0:T(8,128)S(1)} %get-tuple-element.18), channel_id=1, source_target_pairs={{0,16},{16,32},{32,48},{48,64},{64,80},{80,96},{96,112},{1,17},{17... | collective-permute-start | bytes 528392 | tf_op jit(solution)/shard_map/ppermute | solution.py:655
  24.8 1.3 %collective-permute-start.3 = (f32[344,128]{1,0:T(8,128)S(1)}, f32[344,128]{1,0:T(8,128)S(1)}, u32[]{:S(2)}, u32[]{:S(2)}) collective-permute-start(f32[344,128]{1,0:T(8,128)S(1)} %get-tuple-element.19), channel_id=1, source_target_pairs={{16,0},{32,16},{48,32},{64,48},{80,64},{96,80},{112,96},{17,1},{33... | collective-permute-start | bytes 528392 | tf_op jit(solution)/shard_map/ppermute | solution.py:655
  26.1 1.1 %collective-permute-done.2.from_prev = f32[344,128]{1,0:T(8,128)S(1)} collective-permute-done((f32[344,128]{1,0:T(8,128)S(1)}, f32[344,128]{1,0:T(8,128)S(1)}, u32[]{:S(2)}, u32[]{:S(2)}) %collective-permute-start.2) | collective-permute-done | bytes 176160 | tf_op jit(solution)/shard_map/ppermute | solution.py:655
  27.2 3.8 %collective-permute-done.3.from_next = f32[344,128]{1,0:T(8,128)S(1)} collective-permute-done((f32[344,128]{1,0:T(8,128)S(1)}, f32[344,128]{1,0:T(8,128)S(1)}, u32[]{:S(2)}, u32[]{:S(2)}) %collective-permute-start.3) | collective-permute-done | bytes 176160 | tf_op jit(solution)/shard_map/ppermute | solution.py:655
  31.0 2.4 %basis_gram.1 = (f32[320,256]{1,0:T(8,128)S(1)}, f32[256,128]{1,0:T(8,128)}) custom-call(f32[32,256]{1,0:T(8,128)S(1)} %get-tuple-element.22.whole, f32[344,128]{1,0:T(8,128)S(1)} %collective-permute-done.2.from_prev, f32[344,128]{1,0:T(8,128)S(1)} %collective-permute-done.3.from_next), custom_call_target="tpu_custom_call" | custom-call | tf_op jit(solution)/shard_map/basis_gram/pallas_call | solution.py:480
  33.4 0.0 copy-done.3
  33.4 14.3 %all-to-all-start = ((f32[128,2,128]{2,1,0:T(2,128)}), f32[128,2,128]{2,1,0:T(2,128)S(1)}, u32[]{:S(2)}, u32[]{:S(2)}) async-start(f32[128,2,128]{2,1,0:T(2,128)} %bitcast), calls=%async_computation | async-start | bytes 262144 | tf_op jit(solution)/shard_map/all_to_all | solution.py:665
  47.7 0.0 copy-start.4
  47.8 0.0 copy-start.6
  47.8 0.0 copy-start.8
  47.8 0.0 copy-start.10
  47.8 8.4 %rates.1 = (f32[192,1024]{1,0:T(8,128)}, f32[192,1024]{1,0:T(8,128)}) custom-call(f32[192,1024]{1,0:T(8,128)} %swirl.1, f32[192,1024]{1,0:T(8,128)} %vort.3, f32[192,1024]{1,0:T(8,128)} %back.1, f32[224,128]{1,0:T(8,128)} %copy-done.7, f32[224,128]{1,0:T(8,128)} %copy-done.9, f32[344,128]{1,0:T(8,128)} %copy-done.3, f32[344,128]{1,0:T(8,128)} %copy-done.5, ...), custom_call_target="tpu_custom_call" | custom-call | flops 5898240 | bytes 7077888 | tf_op jit(solution)/shard_map/rates/pallas_call | solution.py:639
  56.1 1.8 %all-to-all-done = f32[128,2,128]{2,1,0:T(2,128)S(1)} async-done(((f32[128,2,128]{2,1,0:T(2,128)}), f32[128,2,128]{2,1,0:T(2,128)S(1)}, u32[]{:S(2)}, u32[]{:S(2)}) %all-to-all-start) | async-done | bytes 131104 | tf_op jit(solution)/shard_map/all_to_all | solution.py:665
  58.0 20.8 %v_cycle.1 = f32[192,1024]{1,0:T(8,128)} custom-call(f32[256,128]{1,0:T(8,128)S(1)} %bitcast.2, f32[320,256]{1,0:T(8,128)S(1)} %get-tuple-element.24.basis, f32[1536,128]{1,0:T(8,128)S(1)} %get-tuple-element.17.planes, f32[224,128]{1,0:T(8,128)S(1)} %copy-done.8, f32[224,128]{1,0:T(8,128)S(1)} %copy-done.10, f32[344,128]{1,0:T(8,128)S(1)} %copy-done.4, ...), custom_call_target="tpu_custom_call" | custom-call | tf_op jit(solution)/shard_map/v_cycle/pallas_call | solution.py:585
  (13 shorter events, 0.0 us)
Async XLA Ops:
  0.6 1.1 %copy-start = (f32[192,1024]{1,0:T(8,128)S(1)}, f32[192,1024]{1,0:T(8,128)}, u32[]{:S(2)}) copy-start(f32[192,1024]{1,0:T(8,128)} %swirl.1) | copy-start | bytes 2359300
  1.8 1.1 %copy-start.1 = (f32[192,1024]{1,0:T(8,128)S(1)}, f32[192,1024]{1,0:T(8,128)}, u32[]{:S(2)}) copy-start(f32[192,1024]{1,0:T(8,128)} %vort.3) | copy-start | bytes 2359300
  2.9 18.1 %copy-start.2 = (f32[192,1024]{1,0:T(8,128)S(1)}, f32[192,1024]{1,0:T(8,128)}, u32[]{:S(2)}) copy-start(f32[192,1024]{1,0:T(8,128)} %back.1) | copy-start | bytes 2359300
  10.4 6.4 %collective-permute-start = (f32[224,128]{1,0:T(8,128)S(1)}, f32[224,128]{1,0:T(8,128)S(1)}, u32[]{:S(2)}, u32[]{:S(2)}) collective-permute-start(f32[224,128]{1,0:T(8,128)S(1)} %get-tuple-element.14), channel_id=1, source_target_pairs={{0,1},{1,2},{2,3},{3,4},{4,5},{5,6},{6,7},{7,8},{8,9},{9,10},{10,1... | collective-permute-start | bytes 344072 | tf_op jit(solution)/shard_map/ppermute | solution.py:655
  14.9 6.1 %collective-permute-start.1 = (f32[224,128]{1,0:T(8,128)S(1)}, f32[224,128]{1,0:T(8,128)S(1)}, u32[]{:S(2)}, u32[]{:S(2)}) collective-permute-start(f32[224,128]{1,0:T(8,128)S(1)} %get-tuple-element.15), channel_id=1, source_target_pairs={{1,0},{2,1},{3,2},{4,3},{5,4},{6,5},{7,6},{8,7},{9,8},{10,9},{11,1... | collective-permute-start | bytes 344072 | tf_op jit(solution)/shard_map/ppermute | solution.py:655
  16.8 4.3 %copy-start.7 = (f32[224,128]{1,0:T(8,128)}, f32[224,128]{1,0:T(8,128)S(1)}, u32[]{:S(2)}) copy-start(f32[224,128]{1,0:T(8,128)S(1)} %collective-permute-done.from_west) | copy-start | bytes 344068
  21.0 0.6 copy-start.9
  21.6 5.6 %collective-permute-start.2 = (f32[344,128]{1,0:T(8,128)S(1)}, f32[344,128]{1,0:T(8,128)S(1)}, u32[]{:S(2)}, u32[]{:S(2)}) collective-permute-start(f32[344,128]{1,0:T(8,128)S(1)} %get-tuple-element.18), channel_id=1, source_target_pairs={{0,16},{16,32},{32,48},{48,64},{64,80},{80,96},{96,112},{1,17},{17... | collective-permute-start | bytes 528392 | tf_op jit(solution)/shard_map/ppermute | solution.py:655
  24.8 6.2 %collective-permute-start.3 = (f32[344,128]{1,0:T(8,128)S(1)}, f32[344,128]{1,0:T(8,128)S(1)}, u32[]{:S(2)}, u32[]{:S(2)}) collective-permute-start(f32[344,128]{1,0:T(8,128)S(1)} %get-tuple-element.19), channel_id=1, source_target_pairs={{16,0},{32,16},{48,32},{64,48},{80,64},{96,80},{112,96},{17,1},{33... | collective-permute-start | bytes 528392 | tf_op jit(solution)/shard_map/ppermute | solution.py:655
  27.2 6.2 %copy-start.3 = (f32[344,128]{1,0:T(8,128)}, f32[344,128]{1,0:T(8,128)S(1)}, u32[]{:S(2)}) copy-start(f32[344,128]{1,0:T(8,128)S(1)} %collective-permute-done.2.from_prev) | copy-start | bytes 528388
  31.0 2.4 %copy-start.5 = (f32[344,128]{1,0:T(8,128)}, f32[344,128]{1,0:T(8,128)S(1)}, u32[]{:S(2)}) copy-start(f32[344,128]{1,0:T(8,128)S(1)} %collective-permute-done.3.from_next) | copy-start | bytes 528388
  33.4 24.6 %all-to-all-start = ((f32[128,2,128]{2,1,0:T(2,128)}), f32[128,2,128]{2,1,0:T(2,128)S(1)}, u32[]{:S(2)}, u32[]{:S(2)}) async-start(f32[128,2,128]{2,1,0:T(2,128)} %bitcast), calls=%async_computation | async-start | bytes 262144 | tf_op jit(solution)/shard_map/all_to_all | solution.py:665
  47.7 10.2 %copy-start.4 = (f32[344,128]{1,0:T(8,128)S(1)}, f32[344,128]{1,0:T(8,128)}, u32[]{:S(2)}) copy-start(f32[344,128]{1,0:T(8,128)} %copy-done.3) | copy-start | bytes 528388
  47.8 10.2 %copy-start.6 = (f32[344,128]{1,0:T(8,128)S(1)}, f32[344,128]{1,0:T(8,128)}, u32[]{:S(2)}) copy-start(f32[344,128]{1,0:T(8,128)} %copy-done.5) | copy-start | bytes 528388
  47.8 10.2 %copy-start.8 = (f32[224,128]{1,0:T(8,128)S(1)}, f32[224,128]{1,0:T(8,128)}, u32[]{:S(2)}) copy-start(f32[224,128]{1,0:T(8,128)} %copy-done.7) | copy-start | bytes 344068
  47.8 10.2 %copy-start.10 = (f32[224,128]{1,0:T(8,128)S(1)}, f32[224,128]{1,0:T(8,128)}, u32[]{:S(2)}) copy-start(f32[224,128]{1,0:T(8,128)} %copy-done.9) | copy-start | bytes 344068

commit v3 on v2

--- a/solution.py
+++ b/solution.py
@@ -51,24 +51,26 @@
 COEF_ROWS = 2 * 8 * 17
 
 
-def side_place():
+def main_q():
     lane = iota((8, 128), 1)
-    h = lane & 15
-    return lax.shift_right_logical(lane, 4), h, jnp.where(h < 8, h + 128, h - 16)
+    return 16 * (lane & 7) + lax.shift_right_logical(lane, 3)
+
+
+def side_cols():
+    lane = iota((8, 128), 1)
+    return jnp.where(lane < 64, lane + COLS, lane - 128)
 
 
 def fill_coefs(coef):
     _, row, _, _ = place()
-    lane = iota((8, 128), 1)
-    p_side, _, q_side = side_place()
     for level in range(LEVELS):
         count = planes_of(level)
         spacing = float(2**level)
         for p in range(count + 1):
             if p < count:
-                cols = count * lane + p
+                cols = count * main_q() + p
             else:
-                cols = count * q_side + lax.shift_right_logical(p_side, level)
+                cols = lax.shift_right_arithmetic(side_cols(), level)
             cols = cols + row * (COLS >> level)
             term = (1.5 * spacing) / (spacing * (cols.astype(F32) + 0.5) + 16.0)
             at = 16 * (COEF_AT[level] + p)
@@ -109,17 +111,18 @@
     step = 2**level
     lane = iota((8, 128), 1)
     east, west = coefs_of(coef, level, p)
-    side = None
-    if p == 0 or p == count - 1:
-        side = here_of(ref, level, b, count, k)
     if p < count - 1:
         right = here_of(ref, level, b, p + 1, k)
     else:
-        right = jnp.where(lane == 127, turn(side, -1), turn(here_of(ref, level, b, 0, k), -1))
+        first, side = here_of(ref, level, b, 0, k), here_of(ref, level, b, count, k)
+        right = jnp.where(lane < 120, turn(first, -8), turn(first, -9))
+        right = jnp.where(lane == 127, turn(side, -1), right)
     if p > 0:
         left = here_of(ref, level, b, p - 1, k)
     else:
-        left = jnp.where(lane == 0, turn(side, 16 * step - 15), turn(here_of(ref, level, b, count - 1, k), 1))
+        last, side = here_of(ref, level, b, count - 1, k), here_of(ref, level, b, count, k)
+        left = jnp.where(lane >= 8, turn(last, 8), turn(last, 9))
+        left = jnp.where(lane == 0, turn(side, step), left)
     return (vertical(ref, level, b, p, k) + east * right) + west * left
 
 
@@ -130,17 +133,13 @@
     east, west = coefs_of(coef, level, count)
     side = here_of(ref, level, b, count, k)
     first, last = here_of(ref, level, b, 0, k), here_of(ref, level, b, count - 1, k)
-    edge = 16 * (8 - step)
-    right = jnp.where(lane >= edge, turn(side, -(16 * step + 1)), turn(side, -16 * step))
-    right = jnp.where(lane == edge + 15, turn(first, edge + 15), right)
-    left = jnp.where(lane < 16, turn(side, 16 * step + 1), turn(side, 16 * step))
-    left = jnp.where(lane == 0, turn(last, 1), left)
+    right = jnp.where(lane == 128 - step, turn(first, 128 - step), turn(side, -step))
+    left = jnp.where(lane == 0, turn(last, 1), turn(side, step))
     return (vertical(ref, level, b, count, k) + east * right) + west * left
 
 
 def odd_side(level, b):
-    p_side, _, _ = side_place()
-    return ((lax.shift_right_logical(p_side, level) + b) & 1) == 1
+    return ((lax.shift_right_logical(iota((8, 128), 1), level) + b) & 1) == 1
 
 
 def inside_factors(k):
@@ -149,78 +148,93 @@
     high = jnp.where(gz == gz_count - 1, SPAN - 4, SPAN)
     at = iota((8, 128), 0) + 8 * k
     main = jnp.where((at >= low) & (at < high), 1.0, 0.0).astype(F32)
-    _, h, _ = side_place()
-    first = jnp.where(row == row_count - 1, 8, 0)
-    after = jnp.where(row == 0, 8, 16)
-    return main, jnp.where((h >= first) & (h < after), main, 0.0)
-
-
-def chunks(body):
-    pl.loop(0, SPAN // 8)(body)
+    lane = iota((8, 128), 1)
+    first = jnp.where(row == row_count - 1, 64, 0)
+    after = jnp.where(row == 0, 64, 128)
+    return main, jnp.where((lane >= first) & (lane < after), main, 0.0)
+
+
+def chunks(level, body):
+    def write(stores):
+        for ref, at, b, p, k, value in stores:
+            put(ref, at, b, p, k, value)
+
+    if level == 0:
+        pl.loop(0, SPAN // 8)(lambda k: write(body(k)))
+    else:
+        write([store for k in range(SPAN // 8) for store in body(k)])
 
 
 def down_level(level, source, black, coarse, coef):
     count = planes_of(level)
-
-    @chunks
-    def _(k):
+    step = 2**level
+    keep = (lax.shift_right_logical(iota((8, 128), 1), level) & 1) == 0
+
+    def sweep(k):
         main, side = inside_factors(k)
         main, side = 0.25 * main, 0.25 * side
+        stores = []
         for b in range(count):
+            beside = beside_side(source, coef, level, b, k)
+            value = (here_of(source, level, b, count, k) + 0.25 * beside) * side
+            stores.append((black, level, b, count, k, jnp.where(odd_side(level, b), value, 0.0)))
             for p in range(1 - b % 2, count, 2):
                 beside = beside_main(source, coef, level, b, p, k)
-                put(black, level, b, p, k, (here_of(source, level, b, p, k) + 0.25 * beside) * main)
-            beside = beside_side(source, coef, level, b, k)
-            value = (here_of(source, level, b, count, k) + 0.25 * beside) * side
-            put(black, level, b, count, k, jnp.where(odd_side(level, b), value, 0.0))
-
-    step = 2**level
-    p_side, _, _ = side_place()
-    keep = (lax.shift_right_logical(p_side, level) & 1) == 0
-
-    @chunks
-    def _(k):
+                value = (here_of(source, level, b, p, k) + 0.25 * beside) * main
+                stores.append((black, level, b, p, k, value))
+        return stores
+
+    def restrict(k):
         main, side = inside_factors(k)
+        stores = []
         for b in range(0, count, 2):
+            even = beside_side(black, coef, level, b, k)
+            odd = turn(beside_side(black, coef, level, b + 1, k), -step)
+            value = jnp.where(keep, (even + odd) * side, 0.0)
+            stores.append((coarse, level + 1, b // 2, count // 2, k, value))
             for p in range(0, count, 2):
                 value = beside_main(black, coef, level, b, p, k) + beside_main(black, coef, level, b + 1, p + 1, k)
-                put(coarse, level + 1, b // 2, p // 2, k, value * main)
-            even = beside_side(black, coef, level, b, k)
-            odd = turn(beside_side(black, coef, level, b + 1, k), -16 * step)
-            put(coarse, level + 1, b // 2, count // 2, k, jnp.where(keep, (even + odd) * side, 0.0))
+                stores.append((coarse, level + 1, b // 2, p // 2, k, value * main))
+        return stores
+
+    chunks(level, sweep)
+    chunks(level, restrict)
 
 
 def up_level(level, source, black, error, coef):
     count = planes_of(level)
     step = 2**level
-    p_side, _, _ = side_place()
-    moved = (lax.shift_right_logical(p_side, level) & 1) == 1
-
-    @chunks
-    def _(k):
+    moved = (lax.shift_right_logical(iota((8, 128), 1), level) & 1) == 1
+
+    def correct(k):
+        stores = []
         for b in range(count):
+            value = here_of(error, level + 1, b // 2, count // 2, k)
+            value = jnp.where(moved, turn(value, step), value)
+            value = here_of(black, level, b, count, k) + value
+            stores.append((black, level, b, count, k, jnp.where(odd_side(level, b), value, 0.0)))
             for p in range(1 - b % 2, count, 2):
                 value = here_of(error, level + 1, b // 2, p // 2, k)
-                put(black, level, b, p, k, here_of(black, level, b, p, k) + value)
-            value = here_of(error, level + 1, b // 2, count // 2, k)
-            value = jnp.where(moved, turn(value, 16 * step), value)
-            value = here_of(black, level, b, count, k) + value
-            put(black, level, b, count, k, jnp.where(odd_side(level, b), value, 0.0))
-
-    for colour in (0, 1):
-
-        @chunks
-        def _(k):
-            main, side = inside_factors(k)
-            main, side = 0.25 * main, 0.25 * side
-            for b in range(count):
-                for p in range((b + colour) % 2, count, 2):
-                    beside = beside_main(black, coef, level, b, p, k)
-                    put(black, level, b, p, k, (here_of(source, level, b, p, k) + beside) * main)
-                beside = beside_side(black, coef, level, b, k)
-                value = (here_of(source, level, b, count, k) + beside) * side
-                mine = odd_side(level, b + 1 - colour)
-                put(black, level, b, count, k, jnp.where(mine, value, here_of(black, level, b, count, k)))
+                stores.append((black, level, b, p, k, here_of(black, level, b, p, k) + value))
+        return stores
+
+    def sweep(colour, k):
+        main, side = inside_factors(k)
+        main, side = 0.25 * main, 0.25 * side
+        stores = []
+        for b in range(count):
+            beside = beside_side(black, coef, level, b, k)
+            value = (here_of(source, level, b, count, k) + beside) * side
+            mine = odd_side(level, b + 1 - colour)
+            stores.append((black, level, b, count, k, jnp.where(mine, value, here_of(black, level, b, count, k))))
+            for p in range((b + colour) % 2, count, 2):
+                beside = beside_main(black, coef, level, b, p, k)
+                stores.append((black, level, b, p, k, (here_of(source, level, b, p, k) + beside) * main))
+        return stores
+
+    chunks(level, correct)
+    chunks(level, functools.partial(sweep, 0))
+    chunks(level, functools.partial(sweep, 1))
 
 
 def zero_pads(refs):
@@ -232,14 +246,8 @@
                 ref[at + PAD + SPAN : at + TALL, :] = jnp.zeros((PAD, 128), F32)
 
 
-def permuted(x):
-    lane = iota(x.shape, 1)
-    return jnp.take_along_axis(x, (lane & 15) * 8 + lax.shift_right_logical(lane, 4), axis=1)
-
-
-def restored(x):
-    lane = iota(x.shape, 1)
-    return jnp.take_along_axis(x, (lane & 7) * 16 + lax.shift_right_logical(lane, 3), axis=1)
+def picked(x, pick):
+    return jnp.take_along_axis(x, pick, axis=1)
 
 
 def exchanged(tiles):
@@ -247,12 +255,12 @@
     lane = iota(tiles[0].shape, 1)
     for bit in range(3):
         far = 2**bit
-        low = (lax.shift_right_logical(lane, 4 + bit) & 1) == 0
+        low = (lax.shift_right_logical(lane, bit) & 1) == 0
         for k in range(8):
             if not k & far:
                 a, c = tiles[k], tiles[k + far]
-                tiles[k] = jnp.where(low, a, turn(c, 16 * far))
-                tiles[k + far] = jnp.where(low, turn(a, -16 * far), c)
+                tiles[k] = jnp.where(low, a, turn(c, far))
+                tiles[k + far] = jnp.where(low, turn(a, -far), c)
     return tiles
 
 
@@ -289,10 +297,20 @@
     return high, rest - (high - total)
 
 
-def first_kernel(vort, swirl_first, swirl_last, part, to_east, to_west, planes, s0, s1, s2, s3, b0, b1, b2, coef):
+BAND = 32
+
+
+def first_kernel(
+    vort_hbm, swirl_first, swirl_last, part, to_east, to_west, planes, s0, s1, s2, s3, b0, b1, b2, coef, vort, arrived
+):
+    copies = []
+    for band in range(ROWS // BAND):
+        rows = pl.ds(BAND * band, BAND)
+        copies.append(pltpu.make_async_copy(vort_hbm.at[rows, :], vort.at[rows, :], arrived.at[band]))
+        copies[-1].start()
     fill_coefs(coef)
     zero_pads(((0, s0), (1, s1), (2, s2), (0, b0), (1, b1), (2, b2)))
-    low = (iota((8, 128), 1) & 15) < 8
+    low = iota((BAND, 128), 1) < 64
     for b in range(8):
         for p in range(8):
             at = base(0, b, p) + PAD
@@ -300,13 +318,16 @@
             s0[at + 28 : at + 32, :] = jnp.zeros((4, 128), F32)
         at = base(0, b, 8) + PAD
         s0[at : at + SPAN, :] = jnp.zeros((SPAN, 128), F32)
-    for g in range(ROWS // 8):
-        rows = slice(8 * g, 8 * g + 8)
-        tiles = [permuted(vort[rows, 128 * k : 128 * k + 128]) for k in range(8)]
-        to_east[rows, :] = jnp.where(low, turn(swirl_last[rows, :], 65), tiles[7])
-        to_west[rows, :] = jnp.where(low, tiles[0], turn(swirl_first[rows, :], 8))
+    for band in range(ROWS // BAND):
+        copies[band].wait()
+        rows = slice(BAND * band, BAND * band + BAND)
+        tiles = [vort[rows, 128 * k : 128 * k + 128] for k in range(8)]
+        to_east[rows, :] = jnp.where(low, turn(swirl_last[rows, :], 64), tiles[7])
+        to_west[rows, :] = jnp.where(low, tiles[0], turn(swirl_first[rows, :], 64))
         for p, tile in enumerate(exchanged(tiles)):
-            s0[pl.ds(base(0, 0, p) + PAD + 4 + g, 8, stride=9 * TALL), :] = tile
+            for part_of in range(BAND // 8):
+                g = BAND // 8 * band + part_of
+                s0[pl.ds(base(0, 0, p) + PAD + 4 + g, 8, stride=9 * TALL), :] = tile[8 * part_of : 8 * part_of + 8]
     for b in range(8):
         for p in range(8):
             at = base(0, b, p) + PAD + 4
@@ -319,7 +340,8 @@
     main = s3[PAD : PAD + SPAN, :] * scale
     side = s3[TALL + PAD : TALL + PAD + SPAN, :] * scale
     lane = iota((SPAN, 128), 1)
-    side = jnp.where(lane < 8, side, jnp.where(lane >= 120, turn(side, 112), 0.0))
+    main = picked(main, 8 * (lane & 15) + lax.shift_right_logical(lane, 4))
+    side = jnp.where((lane < 8) | (lane >= 120), picked(side, 8 * (lane & 15)), 0.0)
     part[:, :128] = main
     part[:, 128:] = side
     high = lane >= 64
@@ -351,14 +373,14 @@
         grid=(1,),
         out_shape=(shaped(32, 256), shaped(ROWS + 32, 128), shaped(ROWS + 32, 128), shaped(64 * 24, 128)),
         in_specs=[
-            pl.BlockSpec((ROWS, COLS), lambda t: (0, 0)),
+            pl.BlockSpec(memory_space=pl.ANY),
             pl.BlockSpec((ROWS, 128), lambda t: (0, 0)),
             pl.BlockSpec((ROWS, 128), lambda t: (0, COLS // 128 - 1)),
         ],
         out_specs=[vmem()] * 4,
-        scratch_shapes=level_scratch(),
+        scratch_shapes=level_scratch() + [pltpu.VMEM((ROWS, COLS), F32), pltpu.SemaphoreType.DMA((ROWS // BAND,))],
         name="down_own",
-        **params(40),
+        **params(56),
     )(vort, swirl, swirl)
 
 
@@ -369,7 +391,7 @@
     side = part[:, 128:] + jnp.where(high, west, east)
     whole[:, :128] = main
     whole[:, 128:] = side
-    low = (iota((4, 128), 1) & 15) < 8
+    low = iota((4, 128), 1) < 64
     ends = ((to_next, 20, 7, slice(16, 32), vort_end, swirl_end, base_end), (to_prev, 0, 0, slice(0, 16), vort_top, swirl_top, base_top))
     for dest, g, edge, rows, vort, swirl, back in ends:
         for b in range(8):
@@ -488,7 +510,23 @@
     )(whole, from_prev, from_next)
 
 
-def coarse_coefs(grams, cells):
+def sum_of(terms):
+    terms = list(terms)
+    while len(terms) > 1:
+        added = []
+        for left, right in zip(terms[::2], terms[1::2]):
+            total, rest = two_sum(left[0], right[0])
+            added.append((total, rest + (left[1] + right[1])))
+        terms = added + terms[len(terms) // 2 * 2 :]
+    return terms[0]
+
+
+def tidy(pair):
+    high = pair[0] + pair[1]
+    return high, pair[1] - (high - pair[0])
+
+
+def coarse_coefs(grams, held, cells):
     devices = grams.shape[0] // 2
     gram = (grams[pl.ds(0, devices, stride=2), :], grams[pl.ds(1, devices, stride=2), :])
     while gram[0].shape[0] > 8:
@@ -497,57 +535,63 @@
     for by in (4, 2, 1):
         gram = dd_add(gram, tuple(pltpu.roll(g, by, 0) for g in gram))
 
-    lane = iota((8, 128), 1)
-    i = lane // BASIS
-    j = lane - BASIS * i
-    used = lane < BASIS * BASIS
-
-    def weights(index):
-        below = jnp.where(index == 0, 0.0, jnp.where(index == 1, -1.0, jnp.where(index == 2, 1.0, 0.5)))
-        above = jnp.where((index > 0) & (index < BASIS - 1), 0.5, 0.0)
-        same = jnp.where(index > 0, 1.0, 0.0)
-        return tuple(jnp.where(used, t, 0.0) for t in (below, above, same))
-
-    def image(a, weight, step):
-        below, above, same = weight
-        moved = dd_add(
-            tuple(below * pltpu.roll(t, step, 1) for t in a), tuple(above * pltpu.roll(t, 128 - step, 1) for t in a)
-        )
-        return dd_add(tuple(same * t for t in a), tuple(-t for t in moved))
-
-    weight_i, weight_j = weights(i), weights(j)
-    none = jnp.zeros((8, 128), F32)
-    a_i = (jnp.where(used & (i == 0), 1.0, 0.0), none)
-    a_j = (jnp.where(used & (j == 0), 1.0, 0.0), none)
-    first = iota((8, 128), 0) == 0
-    solved = none
+    lane = iota((16, 128), 0)
+    gram = tuple(jnp.concatenate([g, g], axis=0) for g in gram)
+    columns = []
+    for j in range(BASIS):
+        pick = jnp.minimum(lane * BASIS + j, BASIS * BASIS - 1)
+        high, low = (jnp.where(lane < BASIS, picked(g, pick), 0.0) for g in gram)
+        columns.append((high, low) + halves(high))
+
+    index = iota((16, 128), 0)
+    below = jnp.where(index == 0, 0.0, jnp.where(index == 1, -1.0, jnp.where(index == 2, 1.0, 0.5)))
+    below = jnp.where(index < BASIS, below, 0.0)
+    above = jnp.where((index > 0) & (index < BASIS - 1), 0.5, 0.0)
+    same = jnp.where((index > 0) & (index < BASIS), 1.0, 0.0)
+
+    def image(a):
+        moved = sum_of([tuple(below * pltpu.roll(t, 1, 0) for t in a), tuple(above * pltpu.roll(t, 15, 0) for t in a)])
+        return tidy(sum_of([tuple(same * t for t in a), tuple(-t for t in moved)]))
+
+    a = (jnp.where(index == 0, 1.0, 0.0), jnp.zeros((16, 128), F32))
+    solved = jnp.zeros((16, 128), F32)
     tiny = float(4 ** (2 * LEVELS)) / 16.0 * cells * 1e-12
     for _ in range(ITERS):
-        b_i = image(a_i, weight_i, BASIS)
-        b_j = image(a_j, weight_j, 1)
-        left = tuple(jnp.where(first, a, b) for a, b in zip(a_i, b_i))
-        form = dd_mul(dd_mul(left, b_j), gram)
-        for by in (64, 32, 16, 8, 4, 2, 1):
-            form = dd_add(form, tuple(pltpu.roll(t, by, 1) for t in form))
-        alpha = form[0][0:1] / (form[0][1:2] + tiny)
-        alpha = jnp.broadcast_to(alpha, (8, 128))
-        solved = solved + alpha * a_j[0]
-
-        def less(a, b):
-            high, rest = two_prod(alpha, b[0])
-            return dd_add(a, (-high, -(rest + alpha * b[1])))
-
-        a_i, a_j = less(a_i, b_i), less(a_j, b_j)
+        b = image(a)
+        held[0:16, :] = b[0]
+        held[16:32, :] = b[1]
+        terms = []
+        for j, (high, low, upper, lower) in enumerate(columns):
+            at_j = jnp.broadcast_to(held[j : j + 1, :], (16, 128))
+            rest_j = jnp.broadcast_to(held[16 + j : 17 + j, :], (16, 128))
+            jh, jl = halves(at_j)
+            product = high * at_j
+            rest = ((upper * jh - product) + upper * jl + lower * jh) + lower * jl
+            terms.append((product, rest + (high * rest_j + low * at_j)))
+        image_gram = tidy(sum_of(terms))
+        forms = []
+        for left in (a, b):
+            high, rest = two_prod(left[0], image_gram[0])
+            form = (high, rest + (left[0] * image_gram[1] + left[1] * image_gram[0]))
+            form = sum_of([tuple(t[:8] for t in form), tuple(t[8:] for t in form)])
+            for by in (4, 2, 1):
+                form = sum_of([form, tuple(pltpu.roll(t, by, 0) for t in form)])
+            forms.append(form[0] + form[1])
+        alpha = forms[0] / (forms[1] + tiny)
+        alpha = jnp.concatenate([alpha, alpha], axis=0)
+        solved = solved + alpha * a[0]
+        high, rest = two_prod(alpha, b[0])
+        a = tidy(sum_of([a, (-high, -(rest + alpha * b[1]))]))
     return solved * (float(4**LEVELS) * 0.25)
 
 
 def fourth_kernel(
     grams, basis, planes, from_west, from_east, from_prev, from_next, out,
-    s0, s1, s2, s3, b0, b1, b2, coef, *, cells,
+    s0, s1, s2, s3, b0, b1, b2, coef, held, *, cells,
 ):
     fill_coefs(coef)
     zero_pads(((0, s0), (1, s1), (2, s2), (0, b0), (1, b1), (2, b2)))
-    low = (iota((24, 128), 1) & 15) < 8
+    low = iota((24, 128), 1) < 64
     for b in range(8):
         for p in range(9):
             at = base(0, b, p) + PAD
@@ -563,21 +607,25 @@
     down_level(1, s1, b1, s2, coef)
     down_level(2, s2, b2, s3, coef)
 
-    solved = coarse_coefs(grams, cells)
+    solved = coarse_coefs(grams, held, cells)
     value = jnp.zeros((32, 256), F32)
     for k in range(ITERS):
-        value = value + solved[0:1, k : k + 1] * basis[32 * k : 32 * k + 32, :]
+        value = value + solved[k : k + 1, 0:1] * basis[32 * k : 32 * k + 32, :]
     lane = iota((SPAN, 128), 1)
     side = value[:, 128:]
-    s3[PAD : PAD + SPAN, :] = value[:, :128]
-    s3[TALL + PAD : TALL + PAD + SPAN, :] = jnp.where(lane < 8, side, turn(side, 16))
+    far = lax.shift_right_logical(lane, 3)
+    s3[PAD : PAD + SPAN, :] = picked(value[:, :128], 16 * (lane & 7) + far)
+    s3[TALL + PAD : TALL + PAD + SPAN, :] = picked(side, jnp.where(lane < 64, far, far + 112))
     up_level(2, s2, b2, s3, coef)
     up_level(1, s1, b1, b2, coef)
     up_level(0, s0, b0, b1, coef)
-    for g in range(ROWS // 8):
-        tiles = [b0[pl.ds(base(0, 0, p) + PAD + 4 + g, 8, stride=9 * TALL), :] for p in range(8)]
+    for band in range(ROWS // BAND):
+        tiles = []
+        for p in range(8):
+            at = base(0, 0, p) + PAD + 4 + BAND // 8 * band
+            tiles.append(jnp.concatenate([b0[pl.ds(at + g, 8, stride=9 * TALL), :] for g in range(BAND // 8)], axis=0))
         for k, tile in enumerate(exchanged(tiles)):
-            out[8 * g : 8 * g + 8, 128 * k : 128 * k + 128] = restored(tile)
+            out[BAND * band : BAND * band + BAND, 128 * k : 128 * k + 128] = tile
 
 
 def run_fourth(grams, basis, planes, from_west, from_east, from_prev, from_next):
@@ -587,7 +635,7 @@
         out_shape=shaped(ROWS, COLS),
         in_specs=[vmem()] * 7,
         out_specs=vmem(),
-        scratch_shapes=level_scratch(),
+        scratch_shapes=level_scratch() + [pltpu.VMEM((32, 128), F32)],
         name="v_cycle",
         **params(40),
     )(grams, basis, planes, from_west, from_east, from_prev, from_next)
@@ -618,7 +666,7 @@
         return (ahead - behind) * 0.5
 
     west, east = from_west[:ROWS, :], from_east[:ROWS, :]
-    u_r = slope_r(swirl, turn(west, 64), turn(east, 119))
+    u_r = slope_r(swirl, turn(west, 65), turn(east, 63))
     w_r = slope_r(vort, pltpu.roll(west, 1, 1), pltpu.roll(east, 127, 1))
     u, w = swirl[:, lanes], vort[:, lanes]
     product = 2.0 * back[:, lanes] * u

time: 79.4 us -> 64.4 us (0.81)
  Pallas kernels: 39.1 us -> 24.5 us
  local copies, waits for them, and re-layouts: 2.83 us -> 1.98 us
    pallas_call x1, Pallas kernels: 20.8 us -> 7.3 us  [run_fourth(): pl.pallas_call(functools.partial(fourth_kernel, cells=cells), out_shape=s...]
    pallas_call x1, Pallas kernels: 7.47 us -> 6.36 us  [run_first(): pl.pallas_call(first_kernel, grid=(1,), out_shape=(shaped(32, 256), shape...]
    unnamed x22 -> x28, local copies, waits for them, and re-layouts: 2.83 us -> 1.98 us
  transfers between devices with their start and end apart: 5 -> 5, of which waited for: 4 -> 5; matrix products, arithmetic and copies ran while one was open for 0% -> 0% of each run, Pallas kernels for 11% -> 13%
where the time goes in v3:
time: 64.4 us; the launch traced here: 63.8 us
  starting transfers between devices  25.4 us (39%)
  Pallas kernels  24.5 us (38%)
  waiting for transfers between devices  11.1 us (17%)
  local copies, waits for them, and re-layouts  1.98 us (3%)
  between operations  0.8 us (1%)
    all_to_all x1, starting transfers between devices, per_device(): grams = lax.all_to_all(message, AXES, 0, 0, tiled=True)  14.5 us
    ppermute x4, starting transfers between devices, both_ways(): return (lax.ppermute(up, axis, ahead), lax.ppermute(down, axis, back))  10.9 us
    ppermute x4, waiting for transfers between devices, both_ways(): return (lax.ppermute(up, axis, ahead), lax.ppermute(down, axis, back))  9.28 us
    pallas_call x1, Pallas kernels, run_rates(): pl.pallas_call(rates_kernel, grid=(COLS // 128,), out_shape=(shaped(ROWS,...  8.34 us
    pallas_call x1, Pallas kernels, run_fourth(): pl.pallas_call(functools.partial(fourth_kernel, cells=cells), out_shape=s...  7.3 us
    pallas_call x1, Pallas kernels, run_first(): pl.pallas_call(first_kernel, grid=(1,), out_shape=(shaped(32, 256), shape...  6.36 us
    pallas_call x1, Pallas kernels, run_third(): pl.pallas_call(third_kernel, out_shape=(shaped(32 * ITERS, 256), shaped(2...  2.39 us
    unnamed x28, local copies, waits for them, and re-layouts  1.98 us
  transfers between devices with their start and end apart: 5, of which 5 were waited for; matrix products, arithmetic and copies ran while one was open for 0% of the time, Pallas kernels for 13%

profile of v3, /device:TPU:1, one launch (start us, length us, event | category | flops | bytes accessed | tf_op | source)
XLA Modules:
  0.0 63.8 jit_solution(1655207435551270945)
XLA Ops:
  0.6 0.0 copy-start.1
  0.6 0.0 copy-start
  0.7 0.0 copy-start.2
  0.7 6.4 %down_own.1 = (f32[32,256]{1,0:T(8,128)}, f32[224,128]{1,0:T(8,128)}, f32[224,128]{1,0:T(8,128)}, f32[1536,128]{1,0:T(8,128)}) custom-call(f32[192,1024]{1,0:T(8,128)} %vort.1, f32[192,1024]{1,0:T(8,128)} %swirl.1, f32[192,1024]{1,0:T(8,128)} %swirl.1), custom_call_target="tpu_custom_call" | custom-call | tf_op jit(solution)/shard_map/down_own/pallas_call | solution.py:371
  7.0 4.5 %collective-permute-start = (f32[224,128]{1,0:T(8,128)}, f32[224,128]{1,0:T(8,128)S(1)}, u32[]{:S(2)}, u32[]{:S(2)}) collective-permute-start(f32[224,128]{1,0:T(8,128)} %get-tuple-element.14), channel_id=1, source_target_pairs={{0,1},{1,2},{2,3},{3,4},{4,5},{5,6},{6,7},{7,8},{8,9},{9,10},{10,1... | collective-permute-start | bytes 344072 | tf_op jit(solution)/shard_map/ppermute | solution.py:703
  11.5 1.9 %collective-permute-start.1 = (f32[224,128]{1,0:T(8,128)}, f32[224,128]{1,0:T(8,128)S(1)}, u32[]{:S(2)}, u32[]{:S(2)}) collective-permute-start(f32[224,128]{1,0:T(8,128)} %get-tuple-element.15), channel_id=1, source_target_pairs={{1,0},{2,1},{3,2},{4,3},{5,4},{6,5},{7,6},{8,7},{9,8},{10,9},{11,1... | collective-permute-start | bytes 344072 | tf_op jit(solution)/shard_map/ppermute | solution.py:703
  13.5 0.2 collective-permute-done.from_west
  13.6 4.2 %collective-permute-done.1.from_east = f32[224,128]{1,0:T(8,128)S(1)} collective-permute-done((f32[224,128]{1,0:T(8,128)}, f32[224,128]{1,0:T(8,128)S(1)}, u32[]{:S(2)}, u32[]{:S(2)}) %collective-permute-start.1) | collective-permute-done | bytes 114720 | tf_op jit(solution)/shard_map/ppermute | solution.py:703
  17.9 0.0 copy-done.1
  17.9 0.0 copy-start.3
  17.9 1.2 %copy-done.3 = f32[1536,128]{1,0:T(8,128)S(1)} copy-done((f32[1536,128]{1,0:T(8,128)S(1)}, f32[1536,128]{1,0:T(8,128)}, u32[]{:S(2)}) %copy-start.3) | copy-done | bytes 786456
  19.1 0.8 %copy-done.13 = f32[32,256]{1,0:T(8,128)S(1)} copy-done((f32[32,256]{1,0:T(8,128)S(1)}, f32[32,256]{1,0:T(8,128)}, u32[]{:S(2)}) %copy-start.13) | copy-done | bytes 32792
  19.8 0.1 pack_gz.1
  19.9 0.0 copy-done.9
  19.9 3.2 %collective-permute-start.2 = (f32[344,128]{1,0:T(8,128)S(1)}, f32[344,128]{1,0:T(8,128)S(1)}, u32[]{:S(2)}, u32[]{:S(2)}) collective-permute-start(f32[344,128]{1,0:T(8,128)S(1)} %get-tuple-element.18), channel_id=1, source_target_pairs={{0,16},{16,32},{32,48},{48,64},{64,80},{80,96},{96,112},{1,17},{17... | collective-permute-start | bytes 528392 | tf_op jit(solution)/shard_map/ppermute | solution.py:703
  23.1 1.3 %collective-permute-start.3 = (f32[344,128]{1,0:T(8,128)S(1)}, f32[344,128]{1,0:T(8,128)S(1)}, u32[]{:S(2)}, u32[]{:S(2)}) collective-permute-start(f32[344,128]{1,0:T(8,128)S(1)} %get-tuple-element.19), channel_id=1, source_target_pairs={{16,0},{32,16},{48,32},{64,48},{80,64},{96,80},{112,96},{17,1},{33... | collective-permute-start | bytes 528392 | tf_op jit(solution)/shard_map/ppermute | solution.py:703
  24.4 1.1 %collective-permute-done.2.from_prev = f32[344,128]{1,0:T(8,128)S(1)} collective-permute-done((f32[344,128]{1,0:T(8,128)S(1)}, f32[344,128]{1,0:T(8,128)S(1)}, u32[]{:S(2)}, u32[]{:S(2)}) %collective-permute-start.2) | collective-permute-done | bytes 176160 | tf_op jit(solution)/shard_map/ppermute | solution.py:703
  25.5 3.8 %collective-permute-done.3.from_next = f32[344,128]{1,0:T(8,128)S(1)} collective-permute-done((f32[344,128]{1,0:T(8,128)S(1)}, f32[344,128]{1,0:T(8,128)S(1)}, u32[]{:S(2)}, u32[]{:S(2)}) %collective-permute-start.3) | collective-permute-done | bytes 176160 | tf_op jit(solution)/shard_map/ppermute | solution.py:703
  29.3 2.4 %basis_gram.1 = (f32[320,256]{1,0:T(8,128)S(1)}, f32[256,128]{1,0:T(8,128)}) custom-call(f32[32,256]{1,0:T(8,128)S(1)} %get-tuple-element.22.whole, f32[344,128]{1,0:T(8,128)S(1)} %collective-permute-done.2.from_prev, f32[344,128]{1,0:T(8,128)S(1)} %collective-permute-done.3.from_next), custom_call_target="tpu_custom_call" | custom-call | tf_op jit(solution)/shard_map/basis_gram/pallas_call | solution.py:502
  31.7 14.5 %all-to-all-start = ((f32[128,2,128]{2,1,0:T(2,128)}), f32[128,2,128]{2,1,0:T(2,128)S(1)}, u32[]{:S(2)}, u32[]{:S(2)}) async-start(f32[128,2,128]{2,1,0:T(2,128)} %bitcast), calls=%async_computation | async-start | bytes 262144 | tf_op jit(solution)/shard_map/all_to_all | solution.py:713
  46.3 0.0 copy-start.4
  46.3 8.3 %rates.1 = (f32[192,1024]{1,0:T(8,128)}, f32[192,1024]{1,0:T(8,128)}) custom-call(f32[192,1024]{1,0:T(8,128)} %swirl.1, f32[192,1024]{1,0:T(8,128)} %vort.1, f32[192,1024]{1,0:T(8,128)} %back.1, f32[224,128]{1,0:T(8,128)} %copy-done.9, f32[224,128]{1,0:T(8,128)} %copy-done.11, f32[344,128]{1,0:T(8,128)} %copy-done.5, f32[344,128]{1,0:T(8,128)} %copy-done.7, ...), custom_call_target="tpu_custom_call" | custom-call | flops 5898240 | bytes 7077888 | tf_op jit(solution)/shard_map/rates/pallas_call | solution.py:687
  54.7 1.8 %all-to-all-done = f32[128,2,128]{2,1,0:T(2,128)S(1)} async-done(((f32[128,2,128]{2,1,0:T(2,128)}), f32[128,2,128]{2,1,0:T(2,128)S(1)}, u32[]{:S(2)}, u32[]{:S(2)}) %all-to-all-start) | async-done | bytes 131104 | tf_op jit(solution)/shard_map/all_to_all | solution.py:713
  56.5 7.3 %v_cycle.1 = f32[192,1024]{1,0:T(8,128)} custom-call(f32[256,128]{1,0:T(8,128)S(1)} %bitcast.2, f32[320,256]{1,0:T(8,128)S(1)} %get-tuple-element.24.basis, f32[1536,128]{1,0:T(8,128)S(1)} %copy-done.4, f32[224,128]{1,0:T(8,128)S(1)} %copy-done.10, f32[224,128]{1,0:T(8,128)S(1)} %copy-done.12, f32[344,128]{1,0:T(8,128)S(1)} %copy-done.6, ...), custom_call_target="tpu_custom_call" | custom-call | tf_op jit(solution)/shard_map/v_cycle/pallas_call | solution.py:633
  (19 shorter events, 0.0 us)
Async XLA Ops:
  0.6 17.2 %copy-start.1 = (f32[192,1024]{1,0:T(8,128)S(1)}, f32[192,1024]{1,0:T(8,128)}, u32[]{:S(2)}) copy-start(f32[192,1024]{1,0:T(8,128)} %vort.1) | copy-start | bytes 2359300
  0.6 17.2 %copy-start = (f32[192,1024]{1,0:T(8,128)S(1)}, f32[192,1024]{1,0:T(8,128)}, u32[]{:S(2)}) copy-start(f32[192,1024]{1,0:T(8,128)} %swirl.1) | copy-start | bytes 2359300
  0.7 17.2 %copy-start.2 = (f32[192,1024]{1,0:T(8,128)S(1)}, f32[192,1024]{1,0:T(8,128)}, u32[]{:S(2)}) copy-start(f32[192,1024]{1,0:T(8,128)} %back.1) | copy-start | bytes 2359300
  7.0 6.6 %collective-permute-start = (f32[224,128]{1,0:T(8,128)}, f32[224,128]{1,0:T(8,128)S(1)}, u32[]{:S(2)}, u32[]{:S(2)}) collective-permute-start(f32[224,128]{1,0:T(8,128)} %get-tuple-element.14), channel_id=1, source_target_pairs={{0,1},{1,2},{2,3},{3,4},{4,5},{5,6},{6,7},{7,8},{8,9},{9,10},{10,1... | collective-permute-start | bytes 344072 | tf_op jit(solution)/shard_map/ppermute | solution.py:703
  11.5 6.3 %collective-permute-start.1 = (f32[224,128]{1,0:T(8,128)}, f32[224,128]{1,0:T(8,128)S(1)}, u32[]{:S(2)}, u32[]{:S(2)}) collective-permute-start(f32[224,128]{1,0:T(8,128)} %get-tuple-element.15), channel_id=1, source_target_pairs={{1,0},{2,1},{3,2},{4,3},{5,4},{6,5},{7,6},{8,7},{9,8},{10,9},{11,1... | collective-permute-start | bytes 344072 | tf_op jit(solution)/shard_map/ppermute | solution.py:703
  13.6 6.3 %copy-start.9 = (f32[224,128]{1,0:T(8,128)}, f32[224,128]{1,0:T(8,128)S(1)}, u32[]{:S(2)}) copy-start(f32[224,128]{1,0:T(8,128)S(1)} %collective-permute-done.from_west) | copy-start | bytes 344068
  17.9 2.0 %copy-start.11 = (f32[224,128]{1,0:T(8,128)}, f32[224,128]{1,0:T(8,128)S(1)}, u32[]{:S(2)}) copy-start(f32[224,128]{1,0:T(8,128)S(1)} %collective-permute-done.1.from_east) | copy-start | bytes 344068
  17.9 1.2 %copy-start.3 = (f32[1536,128]{1,0:T(8,128)S(1)}, f32[1536,128]{1,0:T(8,128)}, u32[]{:S(2)}) copy-start(f32[1536,128]{1,0:T(8,128)} %get-tuple-element.17.planes) | copy-start | bytes 2359300
  19.1 0.8 %copy-start.13 = (f32[32,256]{1,0:T(8,128)S(1)}, f32[32,256]{1,0:T(8,128)}, u32[]{:S(2)}) copy-start(f32[32,256]{1,0:T(8,128)} %get-tuple-element.16.part) | copy-start | bytes 98308
  19.9 5.6 %collective-permute-start.2 = (f32[344,128]{1,0:T(8,128)S(1)}, f32[344,128]{1,0:T(8,128)S(1)}, u32[]{:S(2)}, u32[]{:S(2)}) collective-permute-start(f32[344,128]{1,0:T(8,128)S(1)} %get-tuple-element.18), channel_id=1, source_target_pairs={{0,16},{16,32},{32,48},{48,64},{64,80},{80,96},{96,112},{1,17},{17... | collective-permute-start | bytes 528392 | tf_op jit(solution)/shard_map/ppermute | solution.py:703
  23.1 6.2 %collective-permute-start.3 = (f32[344,128]{1,0:T(8,128)S(1)}, f32[344,128]{1,0:T(8,128)S(1)}, u32[]{:S(2)}, u32[]{:S(2)}) collective-permute-start(f32[344,128]{1,0:T(8,128)S(1)} %get-tuple-element.19), channel_id=1, source_target_pairs={{16,0},{32,16},{48,32},{64,48},{80,64},{96,80},{112,96},{17,1},{33... | collective-permute-start | bytes 528392 | tf_op jit(solution)/shard_map/ppermute | solution.py:703
  25.5 6.2 %copy-start.5 = (f32[344,128]{1,0:T(8,128)}, f32[344,128]{1,0:T(8,128)S(1)}, u32[]{:S(2)}) copy-start(f32[344,128]{1,0:T(8,128)S(1)} %collective-permute-done.2.from_prev) | copy-start | bytes 528388
  29.3 2.4 %copy-start.7 = (f32[344,128]{1,0:T(8,128)}, f32[344,128]{1,0:T(8,128)S(1)}, u32[]{:S(2)}) copy-start(f32[344,128]{1,0:T(8,128)S(1)} %collective-permute-done.3.from_next) | copy-start | bytes 528388
  31.7 24.8 %all-to-all-start = ((f32[128,2,128]{2,1,0:T(2,128)}), f32[128,2,128]{2,1,0:T(2,128)S(1)}, u32[]{:S(2)}, u32[]{:S(2)}) async-start(f32[128,2,128]{2,1,0:T(2,128)} %bitcast), calls=%async_computation | async-start | bytes 262144 | tf_op jit(solution)/shard_map/all_to_all | solution.py:713
  46.3 10.2 %copy-start.4 = (f32[1536,128]{1,0:T(8,128)S(1)}, f32[1536,128]{1,0:T(8,128)}, u32[]{:S(2)}) copy-start(f32[1536,128]{1,0:T(8,128)} %get-tuple-element.17.planes) | copy-start | bytes 2359300
  46.3 10.2 %copy-start.6 = (f32[344,128]{1,0:T(8,128)S(1)}, f32[344,128]{1,0:T(8,128)}, u32[]{:S(2)}) copy-start(f32[344,128]{1,0:T(8,128)} %copy-done.5) | copy-start | bytes 528388
  46.3 10.2 %copy-start.8 = (f32[344,128]{1,0:T(8,128)S(1)}, f32[344,128]{1,0:T(8,128)}, u32[]{:S(2)}) copy-start(f32[344,128]{1,0:T(8,128)} %copy-done.7) | copy-start | bytes 528388
  46.3 10.2 %copy-start.10 = (f32[224,128]{1,0:T(8,128)S(1)}, f32[224,128]{1,0:T(8,128)}, u32[]{:S(2)}) copy-start(f32[224,128]{1,0:T(8,128)} %copy-done.9) | copy-start | bytes 344068
  46.3 10.2 %copy-start.12 = (f32[224,128]{1,0:T(8,128)S(1)}, f32[224,128]{1,0:T(8,128)}, u32[]{:S(2)}) copy-start(f32[224,128]{1,0:T(8,128)} %copy-done.11) | copy-start | bytes 344068

commit v4 on v3

--- a/solution.py
+++ b/solution.py
@@ -201,7 +201,7 @@
     chunks(level, restrict)
 
 
-def up_level(level, source, black, error, coef):
+def up_level(level, source, black, error, field, coef):
     count = planes_of(level)
     step = 2**level
     moved = (lax.shift_right_logical(iota((8, 128), 1), level) & 1) == 1
@@ -212,10 +212,10 @@
             value = here_of(error, level + 1, b // 2, count // 2, k)
             value = jnp.where(moved, turn(value, step), value)
             value = here_of(black, level, b, count, k) + value
-            stores.append((black, level, b, count, k, jnp.where(odd_side(level, b), value, 0.0)))
+            stores.append((field, level, b, count, k, jnp.where(odd_side(level, b), value, 0.0)))
             for p in range(1 - b % 2, count, 2):
                 value = here_of(error, level + 1, b // 2, p // 2, k)
-                stores.append((black, level, b, p, k, here_of(black, level, b, p, k) + value))
+                stores.append((field, level, b, p, k, here_of(black, level, b, p, k) + value))
         return stores
 
     def sweep(colour, k):
@@ -223,13 +223,13 @@
         main, side = 0.25 * main, 0.25 * side
         stores = []
         for b in range(count):
-            beside = beside_side(black, coef, level, b, k)
+            beside = beside_side(field, coef, level, b, k)
             value = (here_of(source, level, b, count, k) + beside) * side
             mine = odd_side(level, b + 1 - colour)
-            stores.append((black, level, b, count, k, jnp.where(mine, value, here_of(black, level, b, count, k))))
+            stores.append((field, level, b, count, k, jnp.where(mine, value, here_of(field, level, b, count, k))))
             for p in range((b + colour) % 2, count, 2):
-                beside = beside_main(black, coef, level, b, p, k)
-                stores.append((black, level, b, p, k, (here_of(source, level, b, p, k) + beside) * main))
+                beside = beside_main(field, coef, level, b, p, k)
+                stores.append((field, level, b, p, k, (here_of(source, level, b, p, k) + beside) * main))
         return stores
 
     chunks(level, correct)
@@ -298,19 +298,50 @@
 
 
 BAND = 32
+FOLD = ROWS // 4
+
+
+def pack_edges(vort, swirl_first, swirl_last, to_east, to_west):
+    lane = iota((FOLD, 128), 1)
+    eastward = westward = None
+    for run in range(4):
+        rows = slice(FOLD * run, FOLD * run + FOLD)
+        last = jnp.where(lane == 96, turn(swirl_last[rows, :], 97), vort[rows, COLS - 128 :])
+        first = jnp.where(lane == 31, turn(swirl_first[rows, :], 31), vort[rows, :128])
+        last, first = turn(last, 32 * run + 32), turn(first, 32 * run)
+        mine = lax.shift_right_logical(lane, 5) == run
+        eastward = last if run == 0 else jnp.where(mine, last, eastward)
+        westward = first if run == 0 else jnp.where(mine, first, westward)
+    to_east[:FOLD, :] = eastward
+    to_west[:FOLD, :] = westward
+
+
+def unpack_edges(from_west, from_east, beyond):
+    lane = iota((FOLD, 128), 1)
+    west, east = from_west[:FOLD, :], from_east[:FOLD, :]
+    for run in range(4):
+        value = jnp.where(lane >= 96, turn(west, 96 - 32 * run), 0.0)
+        beyond[FOLD * run : FOLD * run + FOLD, :] = jnp.where(lane < 32, turn(east, -32 * run), value)
 
 
 def first_kernel(
-    vort_hbm, swirl_first, swirl_last, part, to_east, to_west, planes, s0, s1, s2, s3, b0, b1, b2, coef, vort, arrived
+    vort_hbm, swirl_hbm, back_hbm, part, to_east, to_west, planes, row_top, row_end,
+    s0, s1, s2, s3, b0, b1, b2, coef, vort, arrived, swirl_first, swirl_last, ends, ends_arrived,
 ):
-    copies = []
+    copies, extras = [], []
     for band in range(ROWS // BAND):
         rows = pl.ds(BAND * band, BAND)
         copies.append(pltpu.make_async_copy(vort_hbm.at[rows, :], vort.at[rows, :], arrived.at[band]))
         copies[-1].start()
+    pieces = [(swirl_hbm.at[:, pl.ds(0, 128)], swirl_first), (swirl_hbm.at[:, pl.ds(COLS - 128, 128)], swirl_last)]
+    for number, array in enumerate((swirl_hbm, back_hbm)):
+        for end, first in enumerate((0, ROWS - 8)):
+            pieces.append((array.at[pl.ds(first, 8), :], ends.at[2 * number + end]))
+    for number, (src, dst) in enumerate(pieces):
+        extras.append(pltpu.make_async_copy(src, dst, ends_arrived.at[number]))
+        extras[-1].start()
     fill_coefs(coef)
     zero_pads(((0, s0), (1, s1), (2, s2), (0, b0), (1, b1), (2, b2)))
-    low = iota((BAND, 128), 1) < 64
     for b in range(8):
         for p in range(8):
             at = base(0, b, p) + PAD
@@ -322,12 +353,20 @@
         copies[band].wait()
         rows = slice(BAND * band, BAND * band + BAND)
         tiles = [vort[rows, 128 * k : 128 * k + 128] for k in range(8)]
-        to_east[rows, :] = jnp.where(low, turn(swirl_last[rows, :], 64), tiles[7])
-        to_west[rows, :] = jnp.where(low, tiles[0], turn(swirl_first[rows, :], 64))
         for p, tile in enumerate(exchanged(tiles)):
             for part_of in range(BAND // 8):
                 g = BAND // 8 * band + part_of
                 s0[pl.ds(base(0, 0, p) + PAD + 4 + g, 8, stride=9 * TALL), :] = tile[8 * part_of : 8 * part_of + 8]
+    for extra in extras:
+        extra.wait()
+    pack_edges(vort, swirl_first, swirl_last, to_east, to_west)
+    for end, (dest, row, edge) in enumerate(((row_top, 0, 0), (row_end, ROWS - 1, 7))):
+        for tile in range(COLS // 128):
+            lanes = slice(128 * tile, 128 * tile + 128)
+            swirl = ends[end, edge : edge + 1, lanes]
+            dest[tile : tile + 1, :] = swirl
+            dest[8 + tile : 9 + tile, :] = 2.0 * ends[2 + end, edge : edge + 1, lanes] * swirl
+            dest[16 + tile : 17 + tile, :] = vort[row : row + 1, lanes]
     for b in range(8):
         for p in range(8):
             at = base(0, b, p) + PAD + 4
@@ -345,8 +384,8 @@
     part[:, :128] = main
     part[:, 128:] = side
     high = lane >= 64
-    to_east[ROWS:, :] = jnp.where(high, main, side)
-    to_west[ROWS:, :] = jnp.where(high, side, main)
+    to_east[FOLD:, :] = jnp.where(high, main, side)
+    to_west[FOLD:, :] = jnp.where(high, side, main)
 
 
 def level_scratch():
@@ -359,6 +398,14 @@
     return pl.BlockSpec(memory_space=pltpu.VMEM)
 
 
+def hbm():
+    return pl.BlockSpec(memory_space=pltpu.HBM)
+
+
+def fixed(x):
+    return pltpu.with_memory_space_constraint(x, pltpu.HBM)
+
+
 def shaped(*dims):
     return jax.ShapeDtypeStruct(dims, F32)
 
@@ -367,72 +414,64 @@
     return dict(compiler_params=pltpu.CompilerParams(vmem_limit_bytes=mebibytes * 2**20))
 
 
-def run_first(vort, swirl):
+def run_first(vort, swirl, back):
     return pl.pallas_call(
         first_kernel,
-        grid=(1,),
-        out_shape=(shaped(32, 256), shaped(ROWS + 32, 128), shaped(ROWS + 32, 128), shaped(64 * 24, 128)),
-        in_specs=[
-            pl.BlockSpec(memory_space=pl.ANY),
-            pl.BlockSpec((ROWS, 128), lambda t: (0, 0)),
-            pl.BlockSpec((ROWS, 128), lambda t: (0, COLS // 128 - 1)),
-        ],
-        out_specs=[vmem()] * 4,
-        scratch_shapes=level_scratch() + [pltpu.VMEM((ROWS, COLS), F32), pltpu.SemaphoreType.DMA((ROWS // BAND,))],
+        out_shape=(shaped(32, 256), shaped(FOLD + 32, 128), shaped(FOLD + 32, 128), shaped(64 * 24, 128))
+        + (shaped(24, 128),) * 2,
+        in_specs=[hbm()] * 3,
+        out_specs=[vmem()] * 6,
+        scratch_shapes=level_scratch()
+        + [pltpu.VMEM((ROWS, COLS), F32), pltpu.SemaphoreType.DMA((ROWS // BAND,))]
+        + [pltpu.VMEM((ROWS, 128), F32)] * 2
+        + [pltpu.VMEM((4, 8, COLS), F32), pltpu.SemaphoreType.DMA((6,))],
         name="down_own",
-        **params(56),
-    )(vort, swirl, swirl)
-
-
-def second_kernel(part, from_west, from_east, planes, vort_top, vort_end, swirl_top, swirl_end, base_top, base_end, whole, to_next, to_prev):
+        **params(24),
+    )(fixed(vort), fixed(swirl), fixed(back))
+
+
+OUTER = 288
+
+
+def second_kernel(part, from_west, from_east, planes, row_top, row_end, whole, beyond, to_next, to_prev):
     high = iota((32, 128), 1) >= 64
-    west, east = from_west[ROWS:, :], from_east[ROWS:, :]
+    west, east = from_west[FOLD:, :], from_east[FOLD:, :]
     main = part[:, :128] + jnp.where(high, east, west)
     side = part[:, 128:] + jnp.where(high, west, east)
     whole[:, :128] = main
     whole[:, 128:] = side
-    low = iota((4, 128), 1) < 64
-    ends = ((to_next, 20, 7, slice(16, 32), vort_end, swirl_end, base_end), (to_prev, 0, 0, slice(0, 16), vort_top, swirl_top, base_top))
-    for dest, g, edge, rows, vort, swirl, back in ends:
+    unpack_edges(from_west, from_east, beyond)
+    for dest, g, rows, row in ((to_next, 20, slice(16, 32), row_end), (to_prev, 0, slice(0, 16), row_top)):
         for b in range(8):
             for p in range(8):
                 at = 4 * (9 * b + p)
                 dest[at : at + 4, :] = planes[24 * (8 * b + p) + g : 24 * (8 * b + p) + g + 4, :]
             at = 4 * (9 * b + 8)
-            beyond = (from_east[pl.ds(8 * g + b, 4, stride=8), :], from_west[pl.ds(8 * g + b, 4, stride=8), :])
-            dest[at : at + 4, :] = jnp.where(low, beyond[0], beyond[1])
-        for tile in range(COLS // 128):
-            lanes = slice(128 * tile, 128 * tile + 128)
-            row = swirl[edge : edge + 1, lanes]
-            dest[320 + tile : 321 + tile, :] = row
-            dest[328 + tile : 329 + tile, :] = 2.0 * back[edge : edge + 1, lanes] * row
-            dest[336 + tile : 337 + tile, :] = vort[edge : edge + 1, lanes]
-        dest[288:304, :] = main[rows]
-        dest[304:320, :] = side[rows]
-
-
-def run_second(part, from_west, from_east, planes, vort, swirl, back):
-    top = pl.BlockSpec((8, COLS), lambda t: (0, 0))
-    end = pl.BlockSpec((8, COLS), lambda t: (ROWS // 8 - 1, 0))
+            dest[at : at + 4, :] = beyond[pl.ds(8 * g + b, 4, stride=8), :]
+        dest[OUTER : OUTER + 16, :] = main[rows]
+        dest[OUTER + 16 : OUTER + 32, :] = side[rows]
+        dest[OUTER + 32 :, :] = row[...]
+
+
+def run_second(part, from_west, from_east, planes, row_top, row_end):
     return pl.pallas_call(
         second_kernel,
-        grid=(1,),
-        out_shape=(shaped(32, 256), shaped(344, 128), shaped(344, 128)),
-        in_specs=[vmem()] * 4 + [top, end] * 3,
-        out_specs=[vmem()] * 3,
+        out_shape=(shaped(32, 256), shaped(ROWS, 128), shaped(OUTER + 56, 128), shaped(OUTER + 56, 128)),
+        in_specs=[vmem()] * 6,
+        out_specs=[vmem()] * 4,
         name="pack_gz",
-        **params(40),
-    )(part, from_west, from_east, planes, vort, vort, swirl, swirl, back, back)
-
-
-def third_kernel(whole, from_prev, from_next, basis, message, grid, gram_high, gram_low):
+        **params(24),
+    )(part, from_west, from_east, planes, row_top, row_end)
+
+
+def third_kernel(whole, from_prev, from_next, basis_out, message, grid, gram_high, gram_low, basis, moved):
     gz, row, gz_count, row_count = place()
     grid[...] = jnp.zeros((48, 256), F32)
     grid[8:40, :] = whole[...]
-    grid[0:16, :128] += from_prev[288:304, :]
-    grid[0:16, 128:] += from_prev[304:320, :]
-    grid[32:48, :128] += from_next[288:304, :]
-    grid[32:48, 128:] += from_next[304:320, :]
+    grid[0:16, :128] += from_prev[OUTER : OUTER + 16, :]
+    grid[0:16, 128:] += from_prev[OUTER + 16 : OUTER + 32, :]
+    grid[32:48, :128] += from_next[OUTER : OUTER + 16, :]
+    grid[32:48, 128:] += from_next[OUTER + 16 : OUTER + 32, :]
 
     lane = iota((48, 256), 1)
     cols = jnp.where(lane < 192, lane, lane - 256)
@@ -469,6 +508,8 @@
             basis[32 * k : 32 * k + 32, :] = vectors[k][8:40]
         masked = jnp.where(own, vectors[k][8:40, :128], 0.0)
         parts.append((masked,) + halves(masked))
+    copy = pltpu.make_async_copy(basis, basis_out, moved)
+    copy.start()
     for slot, (i, j) in enumerate(PAIRS):
         a, ah, al = parts[i]
         b, bh, bl = parts[j]
@@ -496,17 +537,20 @@
     rows = [jnp.sum(jnp.where(keep, t, 0.0), axis=0, keepdims=True) for t in total]
     odd = (iota(message.shape, 0) & 1) == 1
     message[...] = jnp.where(odd, rows[1], rows[0])
+    copy.wait()
 
 
 def run_third(whole, from_prev, from_next, devices):
     return pl.pallas_call(
         third_kernel,
-        out_shape=(shaped(32 * ITERS, 256), shaped(2 * devices, 128)),
+        out_shape=(pltpu.HBM((32 * ITERS, 256), F32), shaped(2 * devices, 128)),
         in_specs=[vmem()] * 3,
-        out_specs=[vmem()] * 2,
-        scratch_shapes=[pltpu.VMEM((48, 256), F32), pltpu.VMEM((8 * SLOTS, 128), F32), pltpu.VMEM((8 * SLOTS, 128), F32)],
+        out_specs=[hbm(), vmem()],
+        scratch_shapes=[pltpu.VMEM((48, 256), F32)]
+        + [pltpu.VMEM((8 * SLOTS, 128), F32)] * 2
+        + [pltpu.VMEM((32 * ITERS, 256), F32), pltpu.SemaphoreType.DMA],
         name="basis_gram",
-        **params(40),
+        **params(24),
     )(whole, from_prev, from_next)
 
 
@@ -585,13 +629,29 @@
     return solved * (float(4**LEVELS) * 0.25)
 
 
-def fourth_kernel(
-    grams, basis, planes, from_west, from_east, from_prev, from_next, out,
-    s0, s1, s2, s3, b0, b1, b2, coef, held, *, cells,
+def out_copies(pairs, moved):
+    return [pltpu.make_async_copy(src, dst, moved.at[at]) for at, (src, dst) in enumerate(pairs)]
+
+
+LEVEL_ROWS = [plane_rows(level) for level in range(LEVELS)]
+
+
+def down_kernel(
+    planes_hbm, beyond_hbm, prev_hbm, next_hbm, s0_out, b0_out, s1_out, b1_out, s2_out, b2_out,
+    s0, s1, s2, s3, b0, b1, b2, coef, planes, beyond, from_prev, from_next, arrived, moved,
 ):
+    outer = pl.ds(0, OUTER)
+    reads = out_copies(
+        [(planes_hbm, planes), (beyond_hbm, beyond), (prev_hbm.at[outer, :], from_prev), (next_hbm.at[outer, :], from_next)],
+        arrived,
+    )
+    writes = out_copies([(s0, s0_out), (b0, b0_out), (s1, s1_out), (b1, b1_out), (s2, s2_out), (b2, b2_out)], moved)
+    for read in reads:
+        read.start()
     fill_coefs(coef)
     zero_pads(((0, s0), (1, s1), (2, s2), (0, b0), (1, b1), (2, b2)))
-    low = iota((24, 128), 1) < 64
+    for read in reads:
+        read.wait()
     for b in range(8):
         for p in range(9):
             at = base(0, b, p) + PAD
@@ -601,13 +661,49 @@
             if p < 8:
                 s0[at + 4 : at + 28, :] = planes[24 * (8 * b + p) : 24 * (8 * b + p) + 24, :]
             else:
-                beyond = (from_east[pl.ds(b, 24, stride=8), :], from_west[pl.ds(b, 24, stride=8), :])
-                s0[at + 4 : at + 28, :] = jnp.where(low, beyond[0], beyond[1])
+                s0[at + 4 : at + 28, :] = beyond[pl.ds(b, 24, stride=8), :]
+    writes[0].start()
     down_level(0, s0, b0, s1, coef)
+    writes[1].start()
+    writes[2].start()
     down_level(1, s1, b1, s2, coef)
+    writes[3].start()
+    writes[4].start()
     down_level(2, s2, b2, s3, coef)
-
+    writes[5].start()
+    for write in writes:
+        write.wait()
+
+
+def run_down(planes, beyond, from_prev, from_next):
+    held = [(64 * 24, 128), (ROWS, 128), (OUTER, 128), (OUTER, 128)]
+    return pl.pallas_call(
+        down_kernel,
+        out_shape=tuple(pltpu.HBM((LEVEL_ROWS[level], 128), F32) for level in (0, 0, 1, 1, 2, 2)),
+        in_specs=[hbm()] * 4,
+        out_specs=[hbm()] * 6,
+        scratch_shapes=level_scratch()
+        + [pltpu.VMEM(dims, F32) for dims in held]
+        + [pltpu.SemaphoreType.DMA((4,)), pltpu.SemaphoreType.DMA((6,))],
+        name="down_all",
+        cost_estimate=pl.CostEstimate(flops=40 * ROWS * COLS, bytes_accessed=30 * ROWS * COLS, transcendentals=0),
+        **params(24),
+    )(*[fixed(x) for x in (planes, beyond, from_prev, from_next)])
+
+
+def fourth_kernel(
+    grams, basis_hbm, s0_hbm, b0_hbm, s1_hbm, b1_hbm, s2_hbm, b2_hbm, out,
+    s0, s1, s2, s3, b0, b1, b2, coef, held, basis, moved, *, cells,
+):
+    reads = out_copies(
+        [(basis_hbm, basis), (s2_hbm, s2), (b2_hbm, b2), (s1_hbm, s1), (b1_hbm, b1), (s0_hbm, s0), (b0_hbm, b0)], moved
+    )
+    for read in reads:
+        read.start()
+    fill_coefs(coef)
     solved = coarse_coefs(grams, held, cells)
+    for read in reads[:3]:
+        read.wait()
     value = jnp.zeros((32, 256), F32)
     for k in range(ITERS):
         value = value + solved[k : k + 1, 0:1] * basis[32 * k : 32 * k + 32, :]
@@ -616,9 +712,13 @@
     far = lax.shift_right_logical(lane, 3)
     s3[PAD : PAD + SPAN, :] = picked(value[:, :128], 16 * (lane & 7) + far)
     s3[TALL + PAD : TALL + PAD + SPAN, :] = picked(side, jnp.where(lane < 64, far, far + 112))
-    up_level(2, s2, b2, s3, coef)
-    up_level(1, s1, b1, b2, coef)
-    up_level(0, s0, b0, b1, coef)
+    up_level(2, s2, b2, s3, b2, coef)
+    for read in reads[3:5]:
+        read.wait()
+    up_level(1, s1, b1, b2, b1, coef)
+    for read in reads[5:]:
+        read.wait()
+    up_level(0, s0, b0, b1, b0, coef)
     for band in range(ROWS // BAND):
         tiles = []
         for p in range(8):
@@ -628,72 +728,80 @@
             out[BAND * band : BAND * band + BAND, 128 * k : 128 * k + 128] = tile
 
 
-def run_fourth(grams, basis, planes, from_west, from_east, from_prev, from_next):
+def run_fourth(grams, basis, levels):
     cells = float((ROWS >> LEVELS) * (COLS >> LEVELS) * lax.axis_size("gz") * lax.axis_size("row"))
+    held = [(32, 128), (32 * ITERS, 256)]
     return pl.pallas_call(
         functools.partial(fourth_kernel, cells=cells),
         out_shape=shaped(ROWS, COLS),
-        in_specs=[vmem()] * 7,
+        in_specs=[vmem()] + [hbm()] * 7,
         out_specs=vmem(),
-        scratch_shapes=level_scratch() + [pltpu.VMEM((32, 128), F32)],
+        scratch_shapes=level_scratch() + [pltpu.VMEM(dims, F32) for dims in held] + [pltpu.SemaphoreType.DMA((7,))],
         name="v_cycle",
-        **params(40),
-    )(grams, basis, planes, from_west, from_east, from_prev, from_next)
+        **params(24),
+    )(grams, *[fixed(x) for x in (basis, *levels)])
+
+
+STRIP = 32
 
 
 def rates_kernel(
-    swirl, vort, back, from_west, from_east, from_prev, from_next, vel_r, vel_z, swirl_coef, vort_coef, swirl_out, vort_out
+    swirl, swirl_up, swirl_down, vort, vort_up, vort_down, back, back_up, back_down, beyond,
+    u_prev, p_prev, w_prev, u_next, p_next, w_next, vel_r, vel_z, swirl_coef, vort_coef, swirl_out, vort_out,
 ):
-    tile = pl.program_id(0)
-    lane = iota((ROWS, 128), 1)
-    at = iota((ROWS, 128), 0)
-    start = pl.multiple_of(128 * tile, 128)
-    lanes = pl.ds(start, 128)
-    before = pl.ds(pl.multiple_of(jnp.maximum(start - 128, 0), 128), 128)
-    after = pl.ds(pl.multiple_of(jnp.minimum(start + 128, COLS - 128), 128), 128)
-
-    def slope_r(ref, west, east):
+    strip = pl.program_id(0)
+    lane = iota((STRIP, 128), 1)
+    at = iota((STRIP, 128), 0)
+    tiles = COLS // 128
+    outside = beyond[...]
+
+    above, below = strip > 0, strip < ROWS // STRIP - 1
+
+    def slopes(ref, top, bottom, west, east, tile):
+        lanes = slice(128 * tile, 128 * tile + 128)
         here = ref[:, lanes]
-        left = jnp.where(tile == 0, west, pltpu.roll(ref[:, before], 1, 1))
-        right = jnp.where(tile == COLS // 128 - 1, east, pltpu.roll(ref[:, after], 127, 1))
-        ahead = jnp.where(lane == 127, right, pltpu.roll(here, 127, 1))
-        behind = jnp.where(lane == 0, left, pltpu.roll(here, 1, 1))
-        return (ahead - behind) * 0.5
+        left = west if tile == 0 else turn(ref[:, 128 * tile - 128 : 128 * tile], 1)
+        right = east if tile == tiles - 1 else turn(ref[:, 128 * tile + 128 : 128 * tile + 256], -1)
+        along_r = jnp.where(lane == 127, right, turn(here, -1)) - jnp.where(lane == 0, left, turn(here, 1))
+        return here, along_r * 0.5, slope_z(here, top, bottom)
 
     def slope_z(here, top, bottom):
-        ahead = jnp.where(at == ROWS - 1, bottom, pltpu.roll(here, ROWS - 1, 0))
+        ahead = jnp.where(at == STRIP - 1, bottom, pltpu.roll(here, STRIP - 1, 0))
         behind = jnp.where(at == 0, top, pltpu.roll(here, 1, 0))
         return (ahead - behind) * 0.5
 
-    west, east = from_west[:ROWS, :], from_east[:ROWS, :]
-    u_r = slope_r(swirl, turn(west, 65), turn(east, 63))
-    w_r = slope_r(vort, pltpu.roll(west, 1, 1), pltpu.roll(east, 127, 1))
-    u, w = swirl[:, lanes], vort[:, lanes]
-    product = 2.0 * back[:, lanes] * u
-    u_z = slope_z(u, from_prev[pl.ds(320 + tile, 1), :], from_next[pl.ds(320 + tile, 1), :])
-    p_z = slope_z(product, from_prev[pl.ds(328 + tile, 1), :], from_next[pl.ds(328 + tile, 1), :])
-    w_z = slope_z(w, from_prev[pl.ds(336 + tile, 1), :], from_next[pl.ds(336 + tile, 1), :])
-    swirl_out[...] = swirl_coef[...] * u - vel_r[...] * u_r - vel_z[...] * u_z
-    vort_out[...] = vort_coef[...] * w - vel_r[...] * w_r - vel_z[...] * w_z + p_z
-
-
-def run_rates(swirl, vort, back, from_west, from_east, from_prev, from_next, vel_r, vel_z, swirl_coef, vort_coef):
-    block = pl.BlockSpec((ROWS, 128), lambda t: (0, t))
-
-    def whole(shape):
-        return pl.BlockSpec(shape, lambda t: (0, 0))
-
-    big = whole((ROWS, COLS))
+    for tile in range(tiles):
+        lanes = slice(128 * tile, 128 * tile + 128)
+        own = slice(tile, tile + 1)
+        u_top = jnp.where(above, swirl_up[7:8, lanes], u_prev[own, :])
+        u_bottom = jnp.where(below, swirl_down[0:1, lanes], u_next[own, :])
+        w_top = jnp.where(above, vort_up[7:8, lanes], w_prev[own, :])
+        w_bottom = jnp.where(below, vort_down[0:1, lanes], w_next[own, :])
+        p_top = jnp.where(above, 2.0 * back_up[7:8, lanes] * u_top, p_prev[own, :])
+        p_bottom = jnp.where(below, 2.0 * back_down[0:1, lanes] * u_bottom, p_next[own, :])
+        u, u_r, u_z = slopes(swirl, u_top, u_bottom, turn(outside, 32), turn(outside, 96), tile)
+        w, w_r, w_z = slopes(vort, w_top, w_bottom, turn(outside, 1), turn(outside, -1), tile)
+        p_z = slope_z(2.0 * back[:, lanes] * u, p_top, p_bottom)
+        swirl_out[:, lanes] = swirl_coef[:, lanes] * u - vel_r[:, lanes] * u_r - vel_z[:, lanes] * u_z
+        vort_out[:, lanes] = vort_coef[:, lanes] * w - vel_r[:, lanes] * w_r - vel_z[:, lanes] * w_z + p_z
+
+
+def run_rates(swirl, vort, back, beyond, from_prev, from_next, vel_r, vel_z, swirl_coef, vort_coef):
+    per = STRIP // 8
+    block = pl.BlockSpec((STRIP, COLS), lambda t: (t, 0))
+    up = pl.BlockSpec((8, COLS), lambda t: (jnp.maximum(per * t - 1, 0), 0))
+    down = pl.BlockSpec((8, COLS), lambda t: (jnp.minimum(per * t + per, ROWS // 8 - 1), 0))
+    singles = [pl.BlockSpec((8, 128), functools.partial(lambda at, t: (at, 0), OUTER // 8 + 4 + k)) for k in range(3)]
     return pl.pallas_call(
         rates_kernel,
-        grid=(COLS // 128,),
+        grid=(ROWS // STRIP,),
         out_shape=(shaped(ROWS, COLS), shaped(ROWS, COLS)),
-        in_specs=[big] * 3 + [whole((ROWS + 32, 128))] * 2 + [whole((344, 128))] * 2 + [block] * 4,
+        in_specs=[block, up, down] * 3 + [pl.BlockSpec((STRIP, 128), lambda t: (t, 0))] + singles * 2 + [block] * 4,
         out_specs=[block] * 2,
         name="rates",
         cost_estimate=pl.CostEstimate(flops=30 * ROWS * COLS, bytes_accessed=36 * ROWS * COLS, transcendentals=0),
-        **params(60),
-    )(swirl, vort, back, from_west, from_east, from_prev, from_next, vel_r, vel_z, swirl_coef, vort_coef)
+        **params(16),
+    )(*[fixed(x) for x in (swirl,) * 3 + (vort,) * 3 + (back,) * 3], fixed(beyond), *[fixed(x) for x in (from_prev,) * 3 + (from_next,) * 3 + (vel_r, vel_z, swirl_coef, vort_coef)])
 
 
 def both_ways(axis, up, down):
@@ -705,16 +813,17 @@
 
 def per_device(swirl, vorticity, base_swirl, vel_r, vel_z, swirl_coef, vort_coef):
     devices = lax.axis_size("gz") * lax.axis_size("row")
-    part, to_east, to_west, planes = run_first(vorticity, swirl)
+    part, to_east, to_west, planes, row_top, row_end = run_first(vorticity, swirl, base_swirl)
     from_west, from_east = both_ways("row", to_east, to_west)
-    whole, to_next, to_prev = run_second(part, from_west, from_east, planes, vorticity, swirl, base_swirl)
+    whole, beyond, to_next, to_prev = run_second(part, from_west, from_east, planes, row_top, row_end)
     from_prev, from_next = both_ways("gz", to_next, to_prev)
     basis, message = run_third(whole, from_prev, from_next, devices)
     grams = lax.all_to_all(message, AXES, 0, 0, tiled=True)
-    potential = run_fourth(grams, basis, planes, from_west, from_east, from_prev, from_next)
+    levels = run_down(planes, beyond, from_prev, from_next)
     swirl_rate, vort_rate = run_rates(
-        swirl, vorticity, base_swirl, from_west, from_east, from_prev, from_next, vel_r, vel_z, swirl_coef, vort_coef
+        swirl, vorticity, base_swirl, beyond, from_prev, from_next, vel_r, vel_z, swirl_coef, vort_coef
     )
+    potential = run_fourth(grams, basis, levels)
     return swirl_rate, vort_rate, potential
 
 

time: 64.4 us -> 59.6 us (0.925)
  waiting for transfers between devices: 11.1 us -> 8.71 us
  local copies, waits for them, and re-layouts: 1.98 us -> 0.66 us
    all_to_all x1, waiting for transfers between devices: 1.84 us -> 0.01 us  [per_device(): grams = lax.all_to_all(message, AXES, 0, 0, tiled=True)]
    unnamed x28 -> x8, local copies, waits for them, and re-layouts: 1.98 us -> 0.66 us
    pallas_call x1, Pallas kernels: 7.3 us -> 6.09 us  [run_fourth(): pl.pallas_call(functools.partial(fourth_kernel, cells=cells), out_shape=s...]
    pallas_call x4 -> x5, Pallas kernels: 17.2 us -> 17.9 us  [the longest x1 6.63 us: run_rates(): pl.pallas_call(rates_kernel, grid=(ROWS // STRIP,), out_shape=(shaped(ROW...]
  transfers between devices with their start and end apart: 5 -> 5, of which waited for: 5 -> 3; matrix products, arithmetic and copies ran while one was open for 0% -> 0% of each run, Pallas kernels for 13% -> 18%
where the time goes in v4:
time: 59.6 us; the launch traced here: 59.2 us
  starting transfers between devices  25 us (42%)
  Pallas kernels  24 us (40%)
  waiting for transfers between devices  8.71 us (15%)
  between operations  0.76 us (1%)
  local copies, waits for them, and re-layouts  0.66 us (1%)
    all_to_all x1, starting transfers between devices, per_device(): grams = lax.all_to_all(message, AXES, 0, 0, tiled=True)  14.1 us
    ppermute x4, starting transfers between devices, both_ways(): return (lax.ppermute(up, axis, ahead), lax.ppermute(down, axis, back))  10.9 us
    ppermute x4, waiting for transfers between devices, both_ways(): return (lax.ppermute(up, axis, ahead), lax.ppermute(down, axis, back))  8.71 us
    pallas_call x1, Pallas kernels, run_rates(): pl.pallas_call(rates_kernel, grid=(ROWS // STRIP,), out_shape=(shaped(ROW...  6.63 us
    pallas_call x1, Pallas kernels, run_fourth(): pl.pallas_call(functools.partial(fourth_kernel, cells=cells), out_shape=s...  6.09 us
    pallas_call x1, Pallas kernels, run_first(): pl.pallas_call(first_kernel, out_shape=(shaped(32, 256), shaped(FOLD + 32...  4.69 us
    pallas_call x1, Pallas kernels, run_down(): pl.pallas_call(down_kernel, out_shape=tuple((pltpu.HBM((LEVEL_ROWS[level]...  4.06 us
    pallas_call x1, Pallas kernels, run_third(): pl.pallas_call(third_kernel, out_shape=(pltpu.HBM((32 * ITERS, 256), F32)...  2.42 us
  transfers between devices with their start and end apart: 5, of which 3 were waited for; matrix products, arithmetic and copies ran while one was open for 0% of the time, Pallas kernels for 18%

profile of v4, /device:TPU:1, one launch (start us, length us, event | category | flops | bytes accessed | tf_op | source)
XLA Modules:
  0.0 59.2 jit_solution(13209903139228517268)
XLA Ops:
  0.6 4.7 %down_own.1 = (f32[32,256]{1,0:T(8,128)S(1)}, f32[80,128]{1,0:T(8,128)S(1)}, f32[80,128]{1,0:T(8,128)S(1)}, f32[1536,128]{1,0:T(8,128)S(1)}, f32[24,128]{1,0:T(8,128)S(1)}, /*index=5*/f32[24,128]{1,0:T(8,128)S(1)}) custom-call(f32[192,1024]{1,0:T(8,128)} %vort_down.1, f32[192,1024]{1,0:T(8,128)} %swirl_down.1, f32[192,1024]{1,0:T(8,128)} %back_down.1), custom_call_target="tpu_custom_call" | custom-call | tf_op jit(solution)/shard_map/down_own/pallas_call | solution.py:418
  5.3 0.0 copy-start.2
  5.3 4.5 %collective-permute-start = (f32[80,128]{1,0:T(8,128)S(1)}, f32[80,128]{1,0:T(8,128)S(1)}, u32[]{:S(2)}, u32[]{:S(2)}) collective-permute-start(f32[80,128]{1,0:T(8,128)S(1)} %get-tuple-element.24), channel_id=1, source_target_pairs={{0,1},{1,2},{2,3},{3,4},{4,5},{5,6},{6,7},{7,8},{8,9},{9,10},{10,1... | collective-permute-start | bytes 122888 | tf_op jit(solution)/shard_map/ppermute | solution.py:811
  9.9 1.9 %collective-permute-start.1 = (f32[80,128]{1,0:T(8,128)S(1)}, f32[80,128]{1,0:T(8,128)S(1)}, u32[]{:S(2)}, u32[]{:S(2)}) collective-permute-start(f32[80,128]{1,0:T(8,128)S(1)} %get-tuple-element.25), channel_id=1, source_target_pairs={{1,0},{2,1},{3,2},{4,3},{5,4},{6,5},{7,6},{8,7},{9,8},{10,9},{11,1... | collective-permute-start | bytes 122888 | tf_op jit(solution)/shard_map/ppermute | solution.py:811
  11.8 0.0 collective-permute-done.from_west
  11.8 3.4 %collective-permute-done.1.from_east = f32[80,128]{1,0:T(8,128)S(1)} collective-permute-done((f32[80,128]{1,0:T(8,128)S(1)}, f32[80,128]{1,0:T(8,128)S(1)}, u32[]{:S(2)}, u32[]{:S(2)}) %collective-permute-start.1) | collective-permute-done | bytes 40992 | tf_op jit(solution)/shard_map/ppermute | solution.py:811
  15.2 0.1 pack_gz.1
  15.3 0.0 copy-start.3
  15.3 0.6 %copy-done.3 = f32[192,128]{1,0:T(8,128)} copy-done((f32[192,128]{1,0:T(8,128)}, f32[192,128]{1,0:T(8,128)S(1)}, u32[]{:S(2)}) %copy-start.3) | copy-done | bytes 98328
  16.0 3.2 %collective-permute-start.2 = (f32[344,128]{1,0:T(8,128)S(1)}, f32[344,128]{1,0:T(8,128)S(1)}, u32[]{:S(2)}, u32[]{:S(2)}) collective-permute-start(f32[344,128]{1,0:T(8,128)S(1)} %get-tuple-element.30), channel_id=1, source_target_pairs={{0,16},{16,32},{32,48},{48,64},{64,80},{80,96},{96,112},{1,17},{17... | collective-permute-start | bytes 528392 | tf_op jit(solution)/shard_map/ppermute | solution.py:811
  19.2 1.3 %collective-permute-start.3 = (f32[344,128]{1,0:T(8,128)S(1)}, f32[344,128]{1,0:T(8,128)S(1)}, u32[]{:S(2)}, u32[]{:S(2)}) collective-permute-start(f32[344,128]{1,0:T(8,128)S(1)} %get-tuple-element.31), channel_id=1, source_target_pairs={{16,0},{32,16},{48,32},{64,48},{80,64},{96,80},{112,96},{17,1},{33... | collective-permute-start | bytes 528392 | tf_op jit(solution)/shard_map/ppermute | solution.py:811
  20.5 1.2 %collective-permute-done.2.u_prev.p_prev.w_prev.from_prev.prev_hbm = f32[344,128]{1,0:T(8,128)S(1)} collective-permute-done((f32[344,128]{1,0:T(8,128)S(1)}, f32[344,128]{1,0:T(8,128)S(1)}, u32[]{:S(2)}, u32[]{:S(2)}) %collective-permute-start.2) | collective-permute-done | bytes 176160 | tf_op jit(solution)/shard_map/ppermute | solution.py:811
  21.7 0.0 copy-start
  21.7 4.1 %collective-permute-done.3.u_next.p_next.w_next.from_next.next_hbm = f32[344,128]{1,0:T(8,128)S(1)} collective-permute-done((f32[344,128]{1,0:T(8,128)S(1)}, f32[344,128]{1,0:T(8,128)S(1)}, u32[]{:S(2)}, u32[]{:S(2)}) %collective-permute-start.3) | collective-permute-done | bytes 176160 | tf_op jit(solution)/shard_map/ppermute | solution.py:811
  25.8 0.0 copy-start.1
  25.8 2.4 %basis_gram.1 = (f32[320,256]{1,0:T(8,128)}, f32[256,128]{1,0:T(8,128)}) custom-call(f32[32,256]{1,0:T(8,128)S(1)} %get-tuple-element.34.whole, f32[344,128]{1,0:T(8,128)S(1)} %collective-permute-done.2.u_prev.p_prev.w_prev.from_prev.prev_hbm, f32[344,128]{1,0:T(8,128)S(1)} %collective-permute-done.3.u_next.p_next.w_next.from_next.next_hbm), custom_call_target="tpu_custom_call" | custom-call | tf_op jit(solution)/shard_map/basis_gram/pallas_call | solution.py:544
  28.3 14.1 %all-to-all-start = ((f32[128,2,128]{2,1,0:T(2,128)}), f32[128,2,128]{2,1,0:T(2,128)S(1)}, u32[]{:S(2)}, u32[]{:S(2)}) async-start(f32[128,2,128]{2,1,0:T(2,128)} %bitcast), calls=%async_computation | async-start | bytes 262144 | tf_op jit(solution)/shard_map/all_to_all | solution.py:821
  42.3 0.0 copy-done
  42.3 0.0 copy-done.1
  42.4 6.6 %rates.1 = (f32[192,1024]{1,0:T(8,128)}, f32[192,1024]{1,0:T(8,128)}) custom-call(f32[192,1024]{1,0:T(8,128)} %swirl_down.1, f32[192,1024]{1,0:T(8,128)} %swirl_down.1, f32[192,1024]{1,0:T(8,128)} %swirl_down.1, f32[192,1024]{1,0:T(8,128)} %vort_down.1, f32[192,1024]{1,0:T(8,128)} %vort_down.1, f32[192,1024]{1,0:T(8,128)} %vort_down.1, ...), custom_call_target="tpu_custom_call" | custom-call | flops 5898240 | bytes 7077888 | tf_op jit(solution)/shard_map/rates/pallas_call | solution.py:795
  49.0 0.0 copy-done.2
  49.0 4.1 %down_all.1 = (f32[3456,128]{1,0:T(8,128)}, f32[3456,128]{1,0:T(8,128)}, f32[960,128]{1,0:T(8,128)}, f32[960,128]{1,0:T(8,128)}, f32[288,128]{1,0:T(8,128)}, /*index=5*/f32[288,128]{1,0:T(8,128)}) custom-call(f32[1536,128]{1,0:T(8,128)} %copy-done.2, f32[192,128]{1,0:T(8,128)} %copy-done.3, f32[344,128]{1,0:T(8,128)} %copy-done, f32[344,128]{1,0:T(8,128)} %copy-done.1), custom_call_target="tpu_custom_call" | custom-call | flops 7864320 | bytes 5898240 | tf_op jit(solution)/shard_map/down_all/pallas_call | solution.py:680
  53.1 0.0 all-to-all-done
  53.1 6.1 %v_cycle.1 = f32[192,1024]{1,0:T(8,128)} custom-call(f32[256,128]{1,0:T(8,128)S(1)} %bitcast.2, f32[320,256]{1,0:T(8,128)} %get-tuple-element.36.basis_hbm, f32[3456,128]{1,0:T(8,128)} %get-tuple-element.37.s0_hbm, f32[3456,128]{1,0:T(8,128)} %get-tuple-element.38.b0_hbm, f32[960,128]{1,0:T(8,128)} %get-tuple-element.39.s1_hbm, ...), custom_call_target="tpu_custom_call" | custom-call | tf_op jit(solution)/shard_map/v_cycle/pallas_call | solution.py:734
Async XLA Ops:
  5.3 43.7 %copy-start.2 = (f32[1536,128]{1,0:T(8,128)}, f32[1536,128]{1,0:T(8,128)S(1)}, u32[]{:S(2)}) copy-start(f32[1536,128]{1,0:T(8,128)S(1)} %get-tuple-element.26.planes.planes_hbm) | copy-start | bytes 2359300
  5.3 6.4 %collective-permute-start = (f32[80,128]{1,0:T(8,128)S(1)}, f32[80,128]{1,0:T(8,128)S(1)}, u32[]{:S(2)}, u32[]{:S(2)}) collective-permute-start(f32[80,128]{1,0:T(8,128)S(1)} %get-tuple-element.24), channel_id=1, source_target_pairs={{0,1},{1,2},{2,3},{3,4},{4,5},{5,6},{6,7},{7,8},{8,9},{9,10},{10,1... | collective-permute-start | bytes 122888 | tf_op jit(solution)/shard_map/ppermute | solution.py:811
  9.9 5.3 %collective-permute-start.1 = (f32[80,128]{1,0:T(8,128)S(1)}, f32[80,128]{1,0:T(8,128)S(1)}, u32[]{:S(2)}, u32[]{:S(2)}) collective-permute-start(f32[80,128]{1,0:T(8,128)S(1)} %get-tuple-element.25), channel_id=1, source_target_pairs={{1,0},{2,1},{3,2},{4,3},{5,4},{6,5},{7,6},{8,7},{9,8},{10,9},{11,1... | collective-permute-start | bytes 122888 | tf_op jit(solution)/shard_map/ppermute | solution.py:811
  15.3 0.7 %copy-start.3 = (f32[192,128]{1,0:T(8,128)}, f32[192,128]{1,0:T(8,128)S(1)}, u32[]{:S(2)}) copy-start(f32[192,128]{1,0:T(8,128)S(1)} %get-tuple-element.29.beyond.beyond_hbm) | copy-start | bytes 294916
  16.0 5.7 %collective-permute-start.2 = (f32[344,128]{1,0:T(8,128)S(1)}, f32[344,128]{1,0:T(8,128)S(1)}, u32[]{:S(2)}, u32[]{:S(2)}) collective-permute-start(f32[344,128]{1,0:T(8,128)S(1)} %get-tuple-element.30), channel_id=1, source_target_pairs={{0,16},{16,32},{32,48},{48,64},{64,80},{80,96},{96,112},{1,17},{17... | collective-permute-start | bytes 528392 | tf_op jit(solution)/shard_map/ppermute | solution.py:811
  19.2 6.6 %collective-permute-start.3 = (f32[344,128]{1,0:T(8,128)S(1)}, f32[344,128]{1,0:T(8,128)S(1)}, u32[]{:S(2)}, u32[]{:S(2)}) collective-permute-start(f32[344,128]{1,0:T(8,128)S(1)} %get-tuple-element.31), channel_id=1, source_target_pairs={{16,0},{32,16},{48,32},{64,48},{80,64},{96,80},{112,96},{17,1},{33... | collective-permute-start | bytes 528392 | tf_op jit(solution)/shard_map/ppermute | solution.py:811
  21.7 20.6 %copy-start = (f32[344,128]{1,0:T(8,128)}, f32[344,128]{1,0:T(8,128)S(1)}, u32[]{:S(2)}) copy-start(f32[344,128]{1,0:T(8,128)S(1)} %collective-permute-done.2.u_prev.p_prev.w_prev.from_prev.prev_hbm) | copy-start | bytes 528388
  25.8 16.5 %copy-start.1 = (f32[344,128]{1,0:T(8,128)}, f32[344,128]{1,0:T(8,128)S(1)}, u32[]{:S(2)}) copy-start(f32[344,128]{1,0:T(8,128)S(1)} %collective-permute-done.3.u_next.p_next.w_next.from_next.next_hbm) | copy-start | bytes 528388
  28.3 24.8 %all-to-all-start = ((f32[128,2,128]{2,1,0:T(2,128)}), f32[128,2,128]{2,1,0:T(2,128)S(1)}, u32[]{:S(2)}, u32[]{:S(2)}) async-start(f32[128,2,128]{2,1,0:T(2,128)} %bitcast), calls=%async_computation | async-start | bytes 262144 | tf_op jit(solution)/shard_map/all_to_all | solution.py:821

commit v5 on v4

--- a/solution.py
+++ b/solution.py
@@ -27,6 +27,16 @@
 
 def place():
     return lax.axis_index("gz"), lax.axis_index("row"), lax.axis_size("gz"), lax.axis_size("row")
+
+
+def is_odd(axis):
+    return lax.axis_index(axis) % 2 == 1
+
+
+def chosen(axis, first, second):
+    at, count, odd = lax.axis_index(axis), lax.axis_size(axis), is_odd(axis)
+    before = jnp.where(at > 0, jnp.where(odd, first, second), 0.0)
+    return before, jnp.where(at < count - 1, jnp.where(odd, second, first), 0.0)
 
 
 def lanes_inside(cols, width, row, row_count):
@@ -301,7 +311,7 @@
 FOLD = ROWS // 4
 
 
-def pack_edges(vort, swirl_first, swirl_last, to_east, to_west):
+def pack_edges(vort, swirl_first, swirl_last):
     lane = iota((FOLD, 128), 1)
     eastward = westward = None
     for run in range(4):
@@ -312,20 +322,18 @@
         mine = lax.shift_right_logical(lane, 5) == run
         eastward = last if run == 0 else jnp.where(mine, last, eastward)
         westward = first if run == 0 else jnp.where(mine, first, westward)
-    to_east[:FOLD, :] = eastward
-    to_west[:FOLD, :] = westward
-
-
-def unpack_edges(from_west, from_east, beyond):
+    return eastward, westward
+
+
+def unpack_edges(west, east, beyond):
     lane = iota((FOLD, 128), 1)
-    west, east = from_west[:FOLD, :], from_east[:FOLD, :]
     for run in range(4):
         value = jnp.where(lane >= 96, turn(west, 96 - 32 * run), 0.0)
         beyond[FOLD * run : FOLD * run + FOLD, :] = jnp.where(lane < 32, turn(east, -32 * run), value)
 
 
 def first_kernel(
-    vort_hbm, swirl_hbm, back_hbm, part, to_east, to_west, planes, row_top, row_end,
+    vort_hbm, swirl_hbm, back_hbm, part, swap_a, swap_b, planes, row_top, row_end,
     s0, s1, s2, s3, b0, b1, b2, coef, vort, arrived, swirl_first, swirl_last, ends, ends_arrived,
 ):
     copies, extras = [], []
@@ -359,7 +367,10 @@
                 s0[pl.ds(base(0, 0, p) + PAD + 4 + g, 8, stride=9 * TALL), :] = tile[8 * part_of : 8 * part_of + 8]
     for extra in extras:
         extra.wait()
-    pack_edges(vort, swirl_first, swirl_last, to_east, to_west)
+    odd = is_odd("row")
+    eastward, westward = pack_edges(vort, swirl_first, swirl_last)
+    swap_a[:FOLD, :] = jnp.where(odd, westward, eastward)
+    swap_b[:FOLD, :] = jnp.where(odd, eastward, westward)
     for end, (dest, row, edge) in enumerate(((row_top, 0, 0), (row_end, ROWS - 1, 7))):
         for tile in range(COLS // 128):
             lanes = slice(128 * tile, 128 * tile + 128)
@@ -384,8 +395,9 @@
     part[:, :128] = main
     part[:, 128:] = side
     high = lane >= 64
-    to_east[FOLD:, :] = jnp.where(high, main, side)
-    to_west[FOLD:, :] = jnp.where(high, side, main)
+    eastward, westward = jnp.where(high, main, side), jnp.where(high, side, main)
+    swap_a[FOLD:, :] = jnp.where(odd, westward, eastward)
+    swap_b[FOLD:, :] = jnp.where(odd, eastward, westward)
 
 
 def level_scratch():
@@ -433,14 +445,15 @@
 OUTER = 288
 
 
-def second_kernel(part, from_west, from_east, planes, row_top, row_end, whole, beyond, to_next, to_prev):
+def second_kernel(part, swap_a, swap_b, planes, row_top, row_end, whole, beyond, out_a, out_b, to_next, to_prev):
     high = iota((32, 128), 1) >= 64
-    west, east = from_west[FOLD:, :], from_east[FOLD:, :]
+    from_west, from_east = chosen("row", swap_a[...], swap_b[...])
+    west, east = from_west[FOLD:], from_east[FOLD:]
     main = part[:, :128] + jnp.where(high, east, west)
     side = part[:, 128:] + jnp.where(high, west, east)
     whole[:, :128] = main
     whole[:, 128:] = side
-    unpack_edges(from_west, from_east, beyond)
+    unpack_edges(from_west[:FOLD], from_east[:FOLD], beyond)
     for dest, g, rows, row in ((to_next, 20, slice(16, 32), row_end), (to_prev, 0, slice(0, 16), row_top)):
         for b in range(8):
             for p in range(8):
@@ -451,27 +464,32 @@
         dest[OUTER : OUTER + 16, :] = main[rows]
         dest[OUTER + 16 : OUTER + 32, :] = side[rows]
         dest[OUTER + 32 :, :] = row[...]
-
-
-def run_second(part, from_west, from_east, planes, row_top, row_end):
+    odd = is_odd("gz")
+    out_a[...] = jnp.where(odd, to_prev[...], to_next[...])
+    out_b[...] = jnp.where(odd, to_next[...], to_prev[...])
+
+
+def run_second(part, swap_a, swap_b, planes, row_top, row_end):
     return pl.pallas_call(
         second_kernel,
         out_shape=(shaped(32, 256), shaped(ROWS, 128), shaped(OUTER + 56, 128), shaped(OUTER + 56, 128)),
         in_specs=[vmem()] * 6,
         out_specs=[vmem()] * 4,
+        scratch_shapes=[pltpu.VMEM((OUTER + 56, 128), F32)] * 2,
         name="pack_gz",
         **params(24),
-    )(part, from_west, from_east, planes, row_top, row_end)
-
-
-def third_kernel(whole, from_prev, from_next, basis_out, message, grid, gram_high, gram_low, basis, moved):
+    )(part, swap_a, swap_b, planes, row_top, row_end)
+
+
+def third_kernel(whole, swap_a, swap_b, basis_out, message, grid, gram_high, gram_low, basis, moved):
     gz, row, gz_count, row_count = place()
     grid[...] = jnp.zeros((48, 256), F32)
     grid[8:40, :] = whole[...]
-    grid[0:16, :128] += from_prev[OUTER : OUTER + 16, :]
-    grid[0:16, 128:] += from_prev[OUTER + 16 : OUTER + 32, :]
-    grid[32:48, :128] += from_next[OUTER : OUTER + 16, :]
-    grid[32:48, 128:] += from_next[OUTER + 16 : OUTER + 32, :]
+    from_prev, from_next = chosen("gz", swap_a[OUTER : OUTER + 32, :], swap_b[OUTER : OUTER + 32, :])
+    grid[0:16, :128] += from_prev[:16]
+    grid[0:16, 128:] += from_prev[16:]
+    grid[32:48, :128] += from_next[:16]
+    grid[32:48, 128:] += from_next[16:]
 
     lane = iota((48, 256), 1)
     cols = jnp.where(lane < 192, lane, lane - 256)
@@ -529,18 +547,18 @@
         total = term if total is None else dd_add(total, term)
     for by in (64, 32, 16, 8, 4, 2, 1):
         total = dd_add(total, tuple(pltpu.roll(t, by, 1) for t in total))
-    slot = iota((SLOTS, 128), 0)
     lane = iota((SLOTS, 128), 1)
-    keep = lane < 0
-    for number, (i, j) in enumerate(PAIRS):
-        keep = keep | ((slot == number) & ((lane == BASIS * i + j) | (lane == BASIS * j + i)))
+    i = lane // BASIS
+    j = lane - BASIS * i
+    i, j = jnp.minimum(i, j), jnp.maximum(i, j)
+    keep = (iota((SLOTS, 128), 0) == BASIS * i - i * (i - 1) // 2 + j - i) & (lane < BASIS * BASIS)
     rows = [jnp.sum(jnp.where(keep, t, 0.0), axis=0, keepdims=True) for t in total]
     odd = (iota(message.shape, 0) & 1) == 1
     message[...] = jnp.where(odd, rows[1], rows[0])
     copy.wait()
 
 
-def run_third(whole, from_prev, from_next, devices):
+def run_third(whole, swap_a, swap_b, devices):
     return pl.pallas_call(
         third_kernel,
         out_shape=(pltpu.HBM((32 * ITERS, 256), F32), shaped(2 * devices, 128)),
@@ -551,7 +569,7 @@
         + [pltpu.VMEM((32 * ITERS, 256), F32), pltpu.SemaphoreType.DMA],
         name="basis_gram",
         **params(24),
-    )(whole, from_prev, from_next)
+    )(whole, swap_a, swap_b)
 
 
 def sum_of(terms):
@@ -637,12 +655,12 @@
 
 
 def down_kernel(
-    planes_hbm, beyond_hbm, prev_hbm, next_hbm, s0_out, b0_out, s1_out, b1_out, s2_out, b2_out,
-    s0, s1, s2, s3, b0, b1, b2, coef, planes, beyond, from_prev, from_next, arrived, moved,
+    planes_hbm, beyond_hbm, a_hbm, b_hbm, s0_out, b0_out, s1_out, b1_out, s2_out, b2_out,
+    s0, s1, s2, s3, b0, b1, b2, coef, planes, beyond, swap_a, swap_b, arrived, moved,
 ):
     outer = pl.ds(0, OUTER)
     reads = out_copies(
-        [(planes_hbm, planes), (beyond_hbm, beyond), (prev_hbm.at[outer, :], from_prev), (next_hbm.at[outer, :], from_next)],
+        [(planes_hbm, planes), (beyond_hbm, beyond), (a_hbm.at[outer, :], swap_a), (b_hbm.at[outer, :], swap_b)],
         arrived,
     )
     writes = out_copies([(s0, s0_out), (b0, b0_out), (s1, s1_out), (b1, b1_out), (s2, s2_out), (b2, b2_out)], moved)
@@ -656,8 +674,9 @@
         for p in range(9):
             at = base(0, b, p) + PAD
             edge = 4 * (9 * b + p)
-            s0[at : at + 4, :] = from_prev[edge : edge + 4, :]
-            s0[at + 28 : at + 32, :] = from_next[edge : edge + 4, :]
+            from_prev, from_next = chosen("gz", swap_a[edge : edge + 4, :], swap_b[edge : edge + 4, :])
+            s0[at : at + 4, :] = from_prev
+            s0[at + 28 : at + 32, :] = from_next
             if p < 8:
                 s0[at + 4 : at + 28, :] = planes[24 * (8 * b + p) : 24 * (8 * b + p) + 24, :]
             else:
@@ -675,7 +694,7 @@
         write.wait()
 
 
-def run_down(planes, beyond, from_prev, from_next):
+def run_down(planes, beyond, swap_a, swap_b):
     held = [(64 * 24, 128), (ROWS, 128), (OUTER, 128), (OUTER, 128)]
     return pl.pallas_call(
         down_kernel,
@@ -688,7 +707,7 @@
         name="down_all",
         cost_estimate=pl.CostEstimate(flops=40 * ROWS * COLS, bytes_accessed=30 * ROWS * COLS, transcendentals=0),
         **params(24),
-    )(*[fixed(x) for x in (planes, beyond, from_prev, from_next)])
+    )(*[fixed(x) for x in (planes, beyond, swap_a, swap_b)])
 
 
 def fourth_kernel(
@@ -747,7 +766,7 @@
 
 def rates_kernel(
     swirl, swirl_up, swirl_down, vort, vort_up, vort_down, back, back_up, back_down, beyond,
-    u_prev, p_prev, w_prev, u_next, p_next, w_next, vel_r, vel_z, swirl_coef, vort_coef, swirl_out, vort_out,
+    u_a, p_a, w_a, u_b, p_b, w_b, vel_r, vel_z, swirl_coef, vort_coef, swirl_out, vort_out,
 ):
     strip = pl.program_id(0)
     lane = iota((STRIP, 128), 1)
@@ -755,6 +774,9 @@
     tiles = COLS // 128
     outside = beyond[...]
 
+    u_prev, u_next = chosen("gz", u_a[...], u_b[...])
+    p_prev, p_next = chosen("gz", p_a[...], p_b[...])
+    w_prev, w_next = chosen("gz", w_a[...], w_b[...])
     above, below = strip > 0, strip < ROWS // STRIP - 1
 
     def slopes(ref, top, bottom, west, east, tile):
@@ -773,12 +795,12 @@
     for tile in range(tiles):
         lanes = slice(128 * tile, 128 * tile + 128)
         own = slice(tile, tile + 1)
-        u_top = jnp.where(above, swirl_up[7:8, lanes], u_prev[own, :])
-        u_bottom = jnp.where(below, swirl_down[0:1, lanes], u_next[own, :])
-        w_top = jnp.where(above, vort_up[7:8, lanes], w_prev[own, :])
-        w_bottom = jnp.where(below, vort_down[0:1, lanes], w_next[own, :])
-        p_top = jnp.where(above, 2.0 * back_up[7:8, lanes] * u_top, p_prev[own, :])
-        p_bottom = jnp.where(below, 2.0 * back_down[0:1, lanes] * u_bottom, p_next[own, :])
+        u_top = jnp.where(above, swirl_up[7:8, lanes], u_prev[own])
+        u_bottom = jnp.where(below, swirl_down[0:1, lanes], u_next[own])
+        w_top = jnp.where(above, vort_up[7:8, lanes], w_prev[own])
+        w_bottom = jnp.where(below, vort_down[0:1, lanes], w_next[own])
+        p_top = jnp.where(above, 2.0 * back_up[7:8, lanes] * u_top, p_prev[own])
+        p_bottom = jnp.where(below, 2.0 * back_down[0:1, lanes] * u_bottom, p_next[own])
         u, u_r, u_z = slopes(swirl, u_top, u_bottom, turn(outside, 32), turn(outside, 96), tile)
         w, w_r, w_z = slopes(vort, w_top, w_bottom, turn(outside, 1), turn(outside, -1), tile)
         p_z = slope_z(2.0 * back[:, lanes] * u, p_top, p_bottom)
@@ -786,7 +808,7 @@
         vort_out[:, lanes] = vort_coef[:, lanes] * w - vel_r[:, lanes] * w_r - vel_z[:, lanes] * w_z + p_z
 
 
-def run_rates(swirl, vort, back, beyond, from_prev, from_next, vel_r, vel_z, swirl_coef, vort_coef):
+def run_rates(swirl, vort, back, beyond, swap_a, swap_b, vel_r, vel_z, swirl_coef, vort_coef):
     per = STRIP // 8
     block = pl.BlockSpec((STRIP, COLS), lambda t: (t, 0))
     up = pl.BlockSpec((8, COLS), lambda t: (jnp.maximum(per * t - 1, 0), 0))
@@ -801,28 +823,26 @@
         name="rates",
         cost_estimate=pl.CostEstimate(flops=30 * ROWS * COLS, bytes_accessed=36 * ROWS * COLS, transcendentals=0),
         **params(16),
-    )(*[fixed(x) for x in (swirl,) * 3 + (vort,) * 3 + (back,) * 3], fixed(beyond), *[fixed(x) for x in (from_prev,) * 3 + (from_next,) * 3 + (vel_r, vel_z, swirl_coef, vort_coef)])
-
-
-def both_ways(axis, up, down):
+    )(*[fixed(x) for x in (swirl,) * 3 + (vort,) * 3 + (back,) * 3], fixed(beyond), *[fixed(x) for x in (swap_a,) * 3 + (swap_b,) * 3 + (vel_r, vel_z, swirl_coef, vort_coef)])
+
+
+def swapped(axis, first, second):
     count = lax.axis_size(axis)
-    ahead = [(i, i + 1) for i in range(count - 1)]
-    back = [(i + 1, i) for i in range(count - 1)]
-    return lax.ppermute(up, axis, ahead), lax.ppermute(down, axis, back)
+    pairs = [(i, i ^ 1) for i in range(count)]
+    others = [(i, (i + 1) % count if i % 2 else (i - 1) % count) for i in range(count)]
+    return lax.ppermute(first, axis, pairs), lax.ppermute(second, axis, others)
 
 
 def per_device(swirl, vorticity, base_swirl, vel_r, vel_z, swirl_coef, vort_coef):
     devices = lax.axis_size("gz") * lax.axis_size("row")
-    part, to_east, to_west, planes, row_top, row_end = run_first(vorticity, swirl, base_swirl)
-    from_west, from_east = both_ways("row", to_east, to_west)
-    whole, beyond, to_next, to_prev = run_second(part, from_west, from_east, planes, row_top, row_end)
-    from_prev, from_next = both_ways("gz", to_next, to_prev)
-    basis, message = run_third(whole, from_prev, from_next, devices)
+    part, *swaps, planes, row_top, row_end = run_first(vorticity, swirl, base_swirl)
+    swaps = swapped("row", *swaps)
+    whole, beyond, *swaps = run_second(part, *swaps, planes, row_top, row_end)
+    swaps = swapped("gz", *swaps)
+    basis, message = run_third(whole, *swaps, devices)
     grams = lax.all_to_all(message, AXES, 0, 0, tiled=True)
-    levels = run_down(planes, beyond, from_prev, from_next)
-    swirl_rate, vort_rate = run_rates(
-        swirl, vorticity, base_swirl, beyond, from_prev, from_next, vel_r, vel_z, swirl_coef, vort_coef
-    )
+    levels = run_down(planes, beyond, *swaps)
+    swirl_rate, vort_rate = run_rates(swirl, vorticity, base_swirl, beyond, *swaps, vel_r, vel_z, swirl_coef, vort_coef)
     potential = run_fourth(grams, basis, levels)
     return swirl_rate, vort_rate, potential
 

time: 59.6 us -> 51.6 us (0.87)
  starting transfers between devices: 25 us -> 20.8 us
  waiting for transfers between devices: 8.71 us -> 4.99 us
    ppermute x4, waiting for transfers between devices: 8.71 us -> 4.99 us  [the longest x2 4.98 us: swapped(): lax.ppermute(second, axis, others)]
    all_to_all x1, starting transfers between devices: 14.1 us -> 11.4 us  [per_device(): grams = lax.all_to_all(message, AXES, 0, 0, tiled=True)]
    ppermute x4, starting transfers between devices: 10.9 us -> 9.37 us  [the longest x2 6.49 us: swapped(): lax.ppermute(second, axis, others)]
  transfers between devices with their start and end apart: 5 -> 5, of which waited for: 3 -> 2; matrix products, arithmetic and copies ran while one was open for 0% -> 0% of each run, Pallas kernels for 18% -> 21%
where the time goes in v5:
time: 51.6 us; the launch traced here: 51.3 us
  Pallas kernels  24.1 us (47%)
  starting transfers between devices  20.8 us (40%)
  waiting for transfers between devices  4.99 us (10%)
  between operations  0.73 us (1%)
  local copies, waits for them, and re-layouts  0.66 us (1%)
    all_to_all x1, starting transfers between devices, per_device(): grams = lax.all_to_all(message, AXES, 0, 0, tiled=True)  11.4 us
    pallas_call x1, Pallas kernels, run_rates(): pl.pallas_call(rates_kernel, grid=(ROWS // STRIP,), out_shape=(shaped(ROW...  6.63 us
    ppermute x2, starting transfers between devices, swapped(): lax.ppermute(second, axis, others)  6.49 us
    pallas_call x1, Pallas kernels, run_fourth(): pl.pallas_call(functools.partial(fourth_kernel, cells=cells), out_shape=s...  6.09 us
    ppermute x2, waiting for transfers between devices, swapped(): lax.ppermute(second, axis, others)  4.98 us
    pallas_call x1, Pallas kernels, run_first(): pl.pallas_call(first_kernel, out_shape=(shaped(32, 256), shaped(FOLD + 32...  4.69 us
    pallas_call x1, Pallas kernels, run_down(): pl.pallas_call(down_kernel, out_shape=tuple((pltpu.HBM((LEVEL_ROWS[level]...  4.06 us
    ppermute x2, starting transfers between devices, swapped(): lax.ppermute(first, axis, pairs)  2.88 us
  transfers between devices with their start and end apart: 5, of which 2 were waited for; matrix products, arithmetic and copies ran while one was open for 0% of the time, Pallas kernels for 21%

profile of v5, /device:TPU:1, one launch (start us, length us, event | category | flops | bytes accessed | tf_op | source)
XLA Modules:
  0.0 51.3 jit_solution(2991421916764662224)
XLA Ops:
  0.6 4.7 %down_own.1 = (f32[32,256]{1,0:T(8,128)S(1)}, f32[80,128]{1,0:T(8,128)S(1)}, f32[80,128]{1,0:T(8,128)S(1)}, f32[1536,128]{1,0:T(8,128)S(1)}, f32[24,128]{1,0:T(8,128)S(1)}, /*index=5*/f32[24,128]{1,0:T(8,128)S(1)}) custom-call(f32[192,1024]{1,0:T(8,128)} %vort_down.1, f32[192,1024]{1,0:T(8,128)} %swirl_down.1, f32[192,1024]{1,0:T(8,128)} %back_down.1), custom_call_target="tpu_custom_call" | custom-call | tf_op jit(solution)/shard_map/down_own/pallas_call | solution.py:430
  5.3 0.0 copy-start.2
  5.3 1.5 %collective-permute-start = (f32[80,128]{1,0:T(8,128)S(1)}, f32[80,128]{1,0:T(8,128)S(1)}, u32[]{:S(2)}, u32[]{:S(2)}) collective-permute-start(f32[80,128]{1,0:T(8,128)S(1)} %get-tuple-element.24), channel_id=1, source_target_pairs={{0,1},{1,0},{2,3},{3,2},{4,5},{5,4},{6,7},{7,6},{8,9},{9,8},{10,11... | collective-permute-start | bytes 122888 | tf_op jit(solution)/shard_map/ppermute | solution.py:833
  6.8 1.3 %collective-permute-start.1 = (f32[80,128]{1,0:T(8,128)S(1)}, f32[80,128]{1,0:T(8,128)S(1)}, u32[]{:S(2)}, u32[]{:S(2)}) collective-permute-start(f32[80,128]{1,0:T(8,128)S(1)} %get-tuple-element.25), channel_id=1, source_target_pairs={{0,15},{1,2},{2,1},{3,4},{4,3},{5,6},{6,5},{7,8},{8,7},{9,10},{10,... | collective-permute-start | bytes 122888 | tf_op jit(solution)/shard_map/ppermute | solution.py:833
  8.1 0.0 collective-permute-done.swap_a
  8.1 2.2 %collective-permute-done.1.swap_b = f32[80,128]{1,0:T(8,128)S(1)} collective-permute-done((f32[80,128]{1,0:T(8,128)S(1)}, f32[80,128]{1,0:T(8,128)S(1)}, u32[]{:S(2)}, u32[]{:S(2)}) %collective-permute-start.1) | collective-permute-done | bytes 40992 | tf_op jit(solution)/shard_map/ppermute | solution.py:833
  10.3 0.2 pack_gz.1
  10.4 0.0 copy-start.3
  10.5 0.6 %copy-done.3 = f32[192,128]{1,0:T(8,128)} copy-done((f32[192,128]{1,0:T(8,128)}, f32[192,128]{1,0:T(8,128)S(1)}, u32[]{:S(2)}) %copy-start.3) | copy-done | bytes 98328
  11.1 1.4 %collective-permute-start.2 = (f32[344,128]{1,0:T(8,128)S(1)}, f32[344,128]{1,0:T(8,128)S(1)}, u32[]{:S(2)}, u32[]{:S(2)}) collective-permute-start(f32[344,128]{1,0:T(8,128)S(1)} %get-tuple-element.30), channel_id=1, source_target_pairs={{0,16},{16,0},{32,48},{48,32},{64,80},{80,64},{96,112},{112,96},{1... | collective-permute-start | bytes 528392 | tf_op jit(solution)/shard_map/ppermute | solution.py:833
  12.5 5.2 %collective-permute-start.3 = (f32[344,128]{1,0:T(8,128)S(1)}, f32[344,128]{1,0:T(8,128)S(1)}, u32[]{:S(2)}, u32[]{:S(2)}) collective-permute-start(f32[344,128]{1,0:T(8,128)S(1)} %get-tuple-element.31), channel_id=1, source_target_pairs={{0,112},{16,32},{32,16},{48,64},{64,48},{80,96},{96,80},{112,0},{1... | collective-permute-start | bytes 528392 | tf_op jit(solution)/shard_map/ppermute | solution.py:833
  17.7 0.0 collective-permute-done.2.u_a.p_a.w_a.swap_a.a_hbm
  17.7 0.0 copy-start
  17.7 2.8 %collective-permute-done.3.u_b.p_b.w_b.swap_b.b_hbm = f32[344,128]{1,0:T(8,128)S(1)} collective-permute-done((f32[344,128]{1,0:T(8,128)S(1)}, f32[344,128]{1,0:T(8,128)S(1)}, u32[]{:S(2)}, u32[]{:S(2)}) %collective-permute-start.3) | collective-permute-done | bytes 176160 | tf_op jit(solution)/shard_map/ppermute | solution.py:833
  20.5 0.0 copy-start.1
  20.5 2.4 %basis_gram.1 = (f32[320,256]{1,0:T(8,128)}, f32[256,128]{1,0:T(8,128)}) custom-call(f32[32,256]{1,0:T(8,128)S(1)} %get-tuple-element.34.whole, f32[344,128]{1,0:T(8,128)S(1)} %collective-permute-done.2.u_a.p_a.w_a.swap_a.a_hbm, f32[344,128]{1,0:T(8,128)S(1)} %collective-permute-done.3.u_b.p_b.w_b.swap_b.b_hbm), custom_call_target="tpu_custom_call" | custom-call | tf_op jit(solution)/shard_map/basis_gram/pallas_call | solution.py:562
  23.0 11.4 %all-to-all-start = ((f32[128,2,128]{2,1,0:T(2,128)}), f32[128,2,128]{2,1,0:T(2,128)S(1)}, u32[]{:S(2)}, u32[]{:S(2)}) async-start(f32[128,2,128]{2,1,0:T(2,128)} %bitcast), calls=%async_computation | async-start | bytes 262144 | tf_op jit(solution)/shard_map/all_to_all | solution.py:843
  34.4 0.0 copy-done
  34.4 0.0 copy-done.1
  34.4 6.6 %rates.1 = (f32[192,1024]{1,0:T(8,128)}, f32[192,1024]{1,0:T(8,128)}) custom-call(f32[192,1024]{1,0:T(8,128)} %swirl_down.1, f32[192,1024]{1,0:T(8,128)} %swirl_down.1, f32[192,1024]{1,0:T(8,128)} %swirl_down.1, f32[192,1024]{1,0:T(8,128)} %vort_down.1, f32[192,1024]{1,0:T(8,128)} %vort_down.1, f32[192,1024]{1,0:T(8,128)} %vort_down.1, ...), custom_call_target="tpu_custom_call" | custom-call | flops 5898240 | bytes 7077888 | tf_op jit(solution)/shard_map/rates/pallas_call | solution.py:817
  41.1 0.0 copy-done.2
  41.1 4.1 %down_all.1 = (f32[3456,128]{1,0:T(8,128)}, f32[3456,128]{1,0:T(8,128)}, f32[960,128]{1,0:T(8,128)}, f32[960,128]{1,0:T(8,128)}, f32[288,128]{1,0:T(8,128)}, /*index=5*/f32[288,128]{1,0:T(8,128)}) custom-call(f32[1536,128]{1,0:T(8,128)} %copy-done.2, f32[192,128]{1,0:T(8,128)} %copy-done.3, f32[344,128]{1,0:T(8,128)} %copy-done, f32[344,128]{1,0:T(8,128)} %copy-done.1), custom_call_target="tpu_custom_call" | custom-call | flops 7864320 | bytes 5898240 | tf_op jit(solution)/shard_map/down_all/pallas_call | solution.py:699
  45.2 0.0 all-to-all-done
  45.2 6.1 %v_cycle.1 = f32[192,1024]{1,0:T(8,128)} custom-call(f32[256,128]{1,0:T(8,128)S(1)} %bitcast.2, f32[320,256]{1,0:T(8,128)} %get-tuple-element.36.basis_hbm, f32[3456,128]{1,0:T(8,128)} %get-tuple-element.37.s0_hbm, f32[3456,128]{1,0:T(8,128)} %get-tuple-element.38.b0_hbm, f32[960,128]{1,0:T(8,128)} %get-tuple-element.39.s1_hbm, ...), custom_call_target="tpu_custom_call" | custom-call | tf_op jit(solution)/shard_map/v_cycle/pallas_call | solution.py:753
Async XLA Ops:
  5.3 35.7 %copy-start.2 = (f32[1536,128]{1,0:T(8,128)}, f32[1536,128]{1,0:T(8,128)S(1)}, u32[]{:S(2)}) copy-start(f32[1536,128]{1,0:T(8,128)S(1)} %get-tuple-element.26.planes.planes_hbm) | copy-start | bytes 2359300
  5.3 2.8 %collective-permute-start = (f32[80,128]{1,0:T(8,128)S(1)}, f32[80,128]{1,0:T(8,128)S(1)}, u32[]{:S(2)}, u32[]{:S(2)}) collective-permute-start(f32[80,128]{1,0:T(8,128)S(1)} %get-tuple-element.24), channel_id=1, source_target_pairs={{0,1},{1,0},{2,3},{3,2},{4,5},{5,4},{6,7},{7,6},{8,9},{9,8},{10,11... | collective-permute-start | bytes 122888 | tf_op jit(solution)/shard_map/ppermute | solution.py:833
  6.8 3.4 %collective-permute-start.1 = (f32[80,128]{1,0:T(8,128)S(1)}, f32[80,128]{1,0:T(8,128)S(1)}, u32[]{:S(2)}, u32[]{:S(2)}) collective-permute-start(f32[80,128]{1,0:T(8,128)S(1)} %get-tuple-element.25), channel_id=1, source_target_pairs={{0,15},{1,2},{2,1},{3,4},{4,3},{5,6},{6,5},{7,8},{8,7},{9,10},{10,... | collective-permute-start | bytes 122888 | tf_op jit(solution)/shard_map/ppermute | solution.py:833
  10.4 0.7 %copy-start.3 = (f32[192,128]{1,0:T(8,128)}, f32[192,128]{1,0:T(8,128)S(1)}, u32[]{:S(2)}) copy-start(f32[192,128]{1,0:T(8,128)S(1)} %get-tuple-element.29.beyond.beyond_hbm) | copy-start | bytes 294916
  11.1 6.6 %collective-permute-start.2 = (f32[344,128]{1,0:T(8,128)S(1)}, f32[344,128]{1,0:T(8,128)S(1)}, u32[]{:S(2)}, u32[]{:S(2)}) collective-permute-start(f32[344,128]{1,0:T(8,128)S(1)} %get-tuple-element.30), channel_id=1, source_target_pairs={{0,16},{16,0},{32,48},{48,32},{64,80},{80,64},{96,112},{112,96},{1... | collective-permute-start | bytes 528392 | tf_op jit(solution)/shard_map/ppermute | solution.py:833
  12.5 8.1 %collective-permute-start.3 = (f32[344,128]{1,0:T(8,128)S(1)}, f32[344,128]{1,0:T(8,128)S(1)}, u32[]{:S(2)}, u32[]{:S(2)}) collective-permute-start(f32[344,128]{1,0:T(8,128)S(1)} %get-tuple-element.31), channel_id=1, source_target_pairs={{0,112},{16,32},{32,16},{48,64},{64,48},{80,96},{96,80},{112,0},{1... | collective-permute-start | bytes 528392 | tf_op jit(solution)/shard_map/ppermute | solution.py:833
  17.7 16.7 %copy-start = (f32[344,128]{1,0:T(8,128)}, f32[344,128]{1,0:T(8,128)S(1)}, u32[]{:S(2)}) copy-start(f32[344,128]{1,0:T(8,128)S(1)} %collective-permute-done.2.u_a.p_a.w_a.swap_a.a_hbm) | copy-start | bytes 528388
  20.5 13.9 %copy-start.1 = (f32[344,128]{1,0:T(8,128)}, f32[344,128]{1,0:T(8,128)S(1)}, u32[]{:S(2)}) copy-start(f32[344,128]{1,0:T(8,128)S(1)} %collective-permute-done.3.u_b.p_b.w_b.swap_b.b_hbm) | copy-start | bytes 528388
  23.0 22.2 %all-to-all-start = ((f32[128,2,128]{2,1,0:T(2,128)}), f32[128,2,128]{2,1,0:T(2,128)S(1)}, u32[]{:S(2)}, u32[]{:S(2)}) async-start(f32[128,2,128]{2,1,0:T(2,128)} %bitcast), calls=%async_computation | async-start | bytes 262144 | tf_op jit(solution)/shard_map/all_to_all | solution.py:843

commit v6 on v5

--- a/solution.py
+++ b/solution.py
@@ -211,21 +211,43 @@
     chunks(level, restrict)
 
 
+PACKED_SOURCE = 72 * SPAN
+PACKED_BLACK = 40 * SPAN
+
+
+def packed_source(b, p):
+    return (9 * b + p) * SPAN
+
+
+def packed_black(b, p):
+    return (5 * b + (p // 2 if p < 8 else 4)) * SPAN
+
+
 def up_level(level, source, black, error, field, coef):
     count = planes_of(level)
     step = 2**level
     moved = (lax.shift_right_logical(iota((8, 128), 1), level) & 1) == 1
+
+    def source_at(b, p, k):
+        if level > 0:
+            return here_of(source, level, b, p, k)
+        return source[pl.ds(pl.multiple_of(packed_source(b, p) + 8 * k, 8), 8), :]
+
+    def black_at(b, p, k):
+        if level > 0:
+            return here_of(black, level, b, p, k)
+        return black[pl.ds(pl.multiple_of(packed_black(b, p) + 8 * k, 8), 8), :]
 
     def correct(k):
         stores = []
         for b in range(count):
             value = here_of(error, level + 1, b // 2, count // 2, k)
             value = jnp.where(moved, turn(value, step), value)
-            value = here_of(black, level, b, count, k) + value
+            value = black_at(b, count, k) + value
             stores.append((field, level, b, count, k, jnp.where(odd_side(level, b), value, 0.0)))
             for p in range(1 - b % 2, count, 2):
                 value = here_of(error, level + 1, b // 2, p // 2, k)
-                stores.append((field, level, b, p, k, here_of(black, level, b, p, k) + value))
+                stores.append((field, level, b, p, k, black_at(b, p, k) + value))
         return stores
 
     def sweep(colour, k):
@@ -234,12 +256,12 @@
         stores = []
         for b in range(count):
             beside = beside_side(field, coef, level, b, k)
-            value = (here_of(source, level, b, count, k) + beside) * side
+            value = (source_at(b, count, k) + beside) * side
             mine = odd_side(level, b + 1 - colour)
             stores.append((field, level, b, count, k, jnp.where(mine, value, here_of(field, level, b, count, k))))
             for p in range((b + colour) % 2, count, 2):
                 beside = beside_main(field, coef, level, b, p, k)
-                stores.append((field, level, b, p, k, (here_of(source, level, b, p, k) + beside) * main))
+                stores.append((field, level, b, p, k, (source_at(b, p, k) + beside) * main))
         return stores
 
     chunks(level, correct)
@@ -410,6 +432,10 @@
     return pl.BlockSpec(memory_space=pltpu.VMEM)
 
 
+def out_copies(pairs, moved):
+    return [pltpu.make_async_copy(src, dst, moved.at[at]) for at, (src, dst) in enumerate(pairs)]
+
+
 def hbm():
     return pl.BlockSpec(memory_space=pltpu.HBM)
 
@@ -445,7 +471,7 @@
 OUTER = 288
 
 
-def second_kernel(part, swap_a, swap_b, planes, row_top, row_end, whole, beyond, out_a, out_b, to_next, to_prev):
+def second_kernel(part, swap_a, swap_b, planes, row_top, row_end, whole, out_a, out_b, to_next, to_prev, beyond):
     high = iota((32, 128), 1) >= 64
     from_west, from_east = chosen("row", swap_a[...], swap_b[...])
     west, east = from_west[FOLD:], from_east[FOLD:]
@@ -472,16 +498,19 @@
 def run_second(part, swap_a, swap_b, planes, row_top, row_end):
     return pl.pallas_call(
         second_kernel,
-        out_shape=(shaped(32, 256), shaped(ROWS, 128), shaped(OUTER + 56, 128), shaped(OUTER + 56, 128)),
+        out_shape=(shaped(32, 256), shaped(OUTER + 56, 128), shaped(OUTER + 56, 128)),
         in_specs=[vmem()] * 6,
-        out_specs=[vmem()] * 4,
-        scratch_shapes=[pltpu.VMEM((OUTER + 56, 128), F32)] * 2,
+        out_specs=[vmem()] * 3,
+        scratch_shapes=[pltpu.VMEM((OUTER + 56, 128), F32)] * 2 + [pltpu.VMEM((ROWS, 128), F32)],
         name="pack_gz",
         **params(24),
     )(part, swap_a, swap_b, planes, row_top, row_end)
 
 
-def third_kernel(whole, swap_a, swap_b, basis_out, message, grid, gram_high, gram_low, basis, moved):
+def third_kernel(
+    whole, swap_a, swap_b, basis_out, message, grid, gram_high, gram_low, basis, moved
+):
+    copies = out_copies([(basis, basis_out)], moved)
     gz, row, gz_count, row_count = place()
     grid[...] = jnp.zeros((48, 256), F32)
     grid[8:40, :] = whole[...]
@@ -526,8 +555,7 @@
             basis[32 * k : 32 * k + 32, :] = vectors[k][8:40]
         masked = jnp.where(own, vectors[k][8:40, :128], 0.0)
         parts.append((masked,) + halves(masked))
-    copy = pltpu.make_async_copy(basis, basis_out, moved)
-    copy.start()
+    copies[0].start()
     for slot, (i, j) in enumerate(PAIRS):
         a, ah, al = parts[i]
         b, bh, bl = parts[j]
@@ -555,10 +583,11 @@
     rows = [jnp.sum(jnp.where(keep, t, 0.0), axis=0, keepdims=True) for t in total]
     odd = (iota(message.shape, 0) & 1) == 1
     message[...] = jnp.where(odd, rows[1], rows[0])
-    copy.wait()
-
-
-def run_third(whole, swap_a, swap_b, devices):
+    for copy in copies:
+        copy.wait()
+
+
+def run_third(whole, swaps, devices):
     return pl.pallas_call(
         third_kernel,
         out_shape=(pltpu.HBM((32 * ITERS, 256), F32), shaped(2 * devices, 128)),
@@ -566,10 +595,10 @@
         out_specs=[hbm(), vmem()],
         scratch_shapes=[pltpu.VMEM((48, 256), F32)]
         + [pltpu.VMEM((8 * SLOTS, 128), F32)] * 2
-        + [pltpu.VMEM((32 * ITERS, 256), F32), pltpu.SemaphoreType.DMA],
+        + [pltpu.VMEM((32 * ITERS, 256), F32), pltpu.SemaphoreType.DMA((1,))],
         name="basis_gram",
         **params(24),
-    )(whole, swap_a, swap_b)
+    )(whole, *swaps)
 
 
 def sum_of(terms):
@@ -647,29 +676,26 @@
     return solved * (float(4**LEVELS) * 0.25)
 
 
-def out_copies(pairs, moved):
-    return [pltpu.make_async_copy(src, dst, moved.at[at]) for at, (src, dst) in enumerate(pairs)]
-
-
-LEVEL_ROWS = [plane_rows(level) for level in range(LEVELS)]
+LEVEL_ROWS = [PACKED_SOURCE, PACKED_BLACK] + [plane_rows(level) for level in (1, 1, 2, 2)]
 
 
 def down_kernel(
-    planes_hbm, beyond_hbm, a_hbm, b_hbm, s0_out, b0_out, s1_out, b1_out, s2_out, b2_out,
-    s0, s1, s2, s3, b0, b1, b2, coef, planes, beyond, swap_a, swap_b, arrived, moved,
+    planes_hbm, row_a_hbm, row_b_hbm, a_hbm, b_hbm, s0_out, b0_out, s1_out, b1_out, s2_out, b2_out,
+    s0, s1, s2, s3, b0, b1, b2, coef, planes, row_a, row_b, swap_a, swap_b, beyond, s0_packed, b0_packed, arrived, moved,
 ):
     outer = pl.ds(0, OUTER)
     reads = out_copies(
-        [(planes_hbm, planes), (beyond_hbm, beyond), (a_hbm.at[outer, :], swap_a), (b_hbm.at[outer, :], swap_b)],
+        [(row_a_hbm, row_a), (row_b_hbm, row_b), (planes_hbm, planes), (a_hbm.at[outer, :], swap_a), (b_hbm.at[outer, :], swap_b)],
         arrived,
     )
-    writes = out_copies([(s0, s0_out), (b0, b0_out), (s1, s1_out), (b1, b1_out), (s2, s2_out), (b2, b2_out)], moved)
+    writes = out_copies([(s0_packed, s0_out), (b0_packed, b0_out), (s1, s1_out), (b1, b1_out), (s2, s2_out), (b2, b2_out)], moved)
     for read in reads:
         read.start()
     fill_coefs(coef)
     zero_pads(((0, s0), (1, s1), (2, s2), (0, b0), (1, b1), (2, b2)))
     for read in reads:
         read.wait()
+    unpack_edges(*chosen("row", row_a[:FOLD, :], row_b[:FOLD, :]), beyond)
     for b in range(8):
         for p in range(9):
             at = base(0, b, p) + PAD
@@ -681,8 +707,13 @@
                 s0[at + 4 : at + 28, :] = planes[24 * (8 * b + p) : 24 * (8 * b + p) + 24, :]
             else:
                 s0[at + 4 : at + 28, :] = beyond[pl.ds(b, 24, stride=8), :]
+            s0_packed[packed_source(b, p) : packed_source(b, p) + SPAN, :] = s0[at : at + SPAN, :]
     writes[0].start()
     down_level(0, s0, b0, s1, coef)
+    for b in range(8):
+        for p in list(range(1 - b % 2, 8, 2)) + [8]:
+            at = base(0, b, p) + PAD
+            b0_packed[packed_black(b, p) : packed_black(b, p) + SPAN, :] = b0[at : at + SPAN, :]
     writes[1].start()
     writes[2].start()
     down_level(1, s1, b1, s2, coef)
@@ -694,25 +725,25 @@
         write.wait()
 
 
-def run_down(planes, beyond, swap_a, swap_b):
-    held = [(64 * 24, 128), (ROWS, 128), (OUTER, 128), (OUTER, 128)]
+def run_down(planes, rows, swaps):
+    held = [(64 * 24, 128), (FOLD + 32, 128), (FOLD + 32, 128), (OUTER, 128), (OUTER, 128), (ROWS, 128), (PACKED_SOURCE, 128), (PACKED_BLACK, 128)]
     return pl.pallas_call(
         down_kernel,
-        out_shape=tuple(pltpu.HBM((LEVEL_ROWS[level], 128), F32) for level in (0, 0, 1, 1, 2, 2)),
-        in_specs=[hbm()] * 4,
+        out_shape=tuple(pltpu.HBM((rows, 128), F32) for rows in LEVEL_ROWS),
+        in_specs=[hbm()] * 5,
         out_specs=[hbm()] * 6,
         scratch_shapes=level_scratch()
         + [pltpu.VMEM(dims, F32) for dims in held]
-        + [pltpu.SemaphoreType.DMA((4,)), pltpu.SemaphoreType.DMA((6,))],
+        + [pltpu.SemaphoreType.DMA((5,)), pltpu.SemaphoreType.DMA((6,))],
         name="down_all",
         cost_estimate=pl.CostEstimate(flops=40 * ROWS * COLS, bytes_accessed=30 * ROWS * COLS, transcendentals=0),
         **params(24),
-    )(*[fixed(x) for x in (planes, beyond, swap_a, swap_b)])
+    )(*[fixed(x) for x in (planes, *rows, *swaps)])
 
 
 def fourth_kernel(
     grams, basis_hbm, s0_hbm, b0_hbm, s1_hbm, b1_hbm, s2_hbm, b2_hbm, out,
-    s0, s1, s2, s3, b0, b1, b2, coef, held, basis, moved, *, cells,
+    s0, s1, s2, s3, b0, b1, b2, v0, coef, held, basis, moved, final, left, *, cells,
 ):
     reads = out_copies(
         [(basis_hbm, basis), (s2_hbm, s2), (b2_hbm, b2), (s1_hbm, s1), (b1_hbm, b1), (s0_hbm, s0), (b0_hbm, b0)], moved
@@ -720,6 +751,7 @@
     for read in reads:
         read.start()
     fill_coefs(coef)
+    zero_pads(((0, v0),))
     solved = coarse_coefs(grams, held, cells)
     for read in reads[:3]:
         read.wait()
@@ -737,42 +769,53 @@
     up_level(1, s1, b1, b2, b1, coef)
     for read in reads[5:]:
         read.wait()
-    up_level(0, s0, b0, b1, b0, coef)
+    up_level(0, s0, b0, b1, v0, coef)
+    writes = []
     for band in range(ROWS // BAND):
         tiles = []
         for p in range(8):
             at = base(0, 0, p) + PAD + 4 + BAND // 8 * band
-            tiles.append(jnp.concatenate([b0[pl.ds(at + g, 8, stride=9 * TALL), :] for g in range(BAND // 8)], axis=0))
+            tiles.append(jnp.concatenate([v0[pl.ds(at + g, 8, stride=9 * TALL), :] for g in range(BAND // 8)], axis=0))
         for k, tile in enumerate(exchanged(tiles)):
-            out[BAND * band : BAND * band + BAND, 128 * k : 128 * k + 128] = tile
+            final[BAND * band : BAND * band + BAND, 128 * k : 128 * k + 128] = tile
+        rows = pl.ds(BAND * band, BAND)
+        writes.append(pltpu.make_async_copy(final.at[rows, :], out.at[rows, :], left.at[band]))
+        writes[-1].start()
+    for write in writes:
+        write.wait()
 
 
 def run_fourth(grams, basis, levels):
     cells = float((ROWS >> LEVELS) * (COLS >> LEVELS) * lax.axis_size("gz") * lax.axis_size("row"))
+    tall = [PACKED_SOURCE, *(plane_rows(level) for level in (1, 2, 3)), PACKED_BLACK]
+    tall += [plane_rows(level) for level in (1, 2, 0)] + [COEF_ROWS]
+    fields = [pltpu.VMEM((rows, 128), F32) for rows in tall]
     held = [(32, 128), (32 * ITERS, 256)]
     return pl.pallas_call(
         functools.partial(fourth_kernel, cells=cells),
         out_shape=shaped(ROWS, COLS),
         in_specs=[vmem()] + [hbm()] * 7,
-        out_specs=vmem(),
-        scratch_shapes=level_scratch() + [pltpu.VMEM(dims, F32) for dims in held] + [pltpu.SemaphoreType.DMA((7,))],
+        out_specs=hbm(),
+        scratch_shapes=fields + [pltpu.VMEM(dims, F32) for dims in held]
+        + [pltpu.SemaphoreType.DMA((7,)), pltpu.VMEM((ROWS, COLS), F32), pltpu.SemaphoreType.DMA((ROWS // BAND,))],
         name="v_cycle",
         **params(24),
     )(grams, *[fixed(x) for x in (basis, *levels)])
 
 
-STRIP = 32
+STRIP = FOLD
 
 
 def rates_kernel(
-    swirl, swirl_up, swirl_down, vort, vort_up, vort_down, back, back_up, back_down, beyond,
+    swirl, swirl_up, swirl_down, vort, vort_up, vort_down, back, back_up, back_down, row_a, row_b,
     u_a, p_a, w_a, u_b, p_b, w_b, vel_r, vel_z, swirl_coef, vort_coef, swirl_out, vort_out,
 ):
     strip = pl.program_id(0)
     lane = iota((STRIP, 128), 1)
     at = iota((STRIP, 128), 0)
     tiles = COLS // 128
-    outside = beyond[...]
+    west, east = chosen("row", row_a[...], row_b[...])
+    west, east = pltpu.roll(west, (224 - 32 * strip) % 128, 1), pltpu.roll(east, (128 - 32 * strip) % 128, 1)
 
     u_prev, u_next = chosen("gz", u_a[...], u_b[...])
     p_prev, p_next = chosen("gz", p_a[...], p_b[...])
@@ -801,14 +844,14 @@
         w_bottom = jnp.where(below, vort_down[0:1, lanes], w_next[own])
         p_top = jnp.where(above, 2.0 * back_up[7:8, lanes] * u_top, p_prev[own])
         p_bottom = jnp.where(below, 2.0 * back_down[0:1, lanes] * u_bottom, p_next[own])
-        u, u_r, u_z = slopes(swirl, u_top, u_bottom, turn(outside, 32), turn(outside, 96), tile)
-        w, w_r, w_z = slopes(vort, w_top, w_bottom, turn(outside, 1), turn(outside, -1), tile)
+        u, u_r, u_z = slopes(swirl, u_top, u_bottom, turn(west, 32), turn(east, 96), tile)
+        w, w_r, w_z = slopes(vort, w_top, w_bottom, turn(west, 1), turn(east, -1), tile)
         p_z = slope_z(2.0 * back[:, lanes] * u, p_top, p_bottom)
         swirl_out[:, lanes] = swirl_coef[:, lanes] * u - vel_r[:, lanes] * u_r - vel_z[:, lanes] * u_z
         vort_out[:, lanes] = vort_coef[:, lanes] * w - vel_r[:, lanes] * w_r - vel_z[:, lanes] * w_z + p_z
 
 
-def run_rates(swirl, vort, back, beyond, swap_a, swap_b, vel_r, vel_z, swirl_coef, vort_coef):
+def run_rates(swirl, vort, back, rows, swap_a, swap_b, vel_r, vel_z, swirl_coef, vort_coef):
     per = STRIP // 8
     block = pl.BlockSpec((STRIP, COLS), lambda t: (t, 0))
     up = pl.BlockSpec((8, COLS), lambda t: (jnp.maximum(per * t - 1, 0), 0))
@@ -818,12 +861,12 @@
         rates_kernel,
         grid=(ROWS // STRIP,),
         out_shape=(shaped(ROWS, COLS), shaped(ROWS, COLS)),
-        in_specs=[block, up, down] * 3 + [pl.BlockSpec((STRIP, 128), lambda t: (t, 0))] + singles * 2 + [block] * 4,
+        in_specs=[block, up, down] * 3 + [pl.BlockSpec((FOLD, 128), lambda t: (0, 0))] * 2 + singles * 2 + [block] * 4,
         out_specs=[block] * 2,
         name="rates",
         cost_estimate=pl.CostEstimate(flops=30 * ROWS * COLS, bytes_accessed=36 * ROWS * COLS, transcendentals=0),
         **params(16),
-    )(*[fixed(x) for x in (swirl,) * 3 + (vort,) * 3 + (back,) * 3], fixed(beyond), *[fixed(x) for x in (swap_a,) * 3 + (swap_b,) * 3 + (vel_r, vel_z, swirl_coef, vort_coef)])
+    )(*[fixed(x) for x in (swirl,) * 3 + (vort,) * 3 + (back,) * 3], *[fixed(x) for x in (*rows,) + (swap_a,) * 3 + (swap_b,) * 3 + (vel_r, vel_z, swirl_coef, vort_coef)])
 
 
 def swapped(axis, first, second):
@@ -836,13 +879,13 @@
 def per_device(swirl, vorticity, base_swirl, vel_r, vel_z, swirl_coef, vort_coef):
     devices = lax.axis_size("gz") * lax.axis_size("row")
     part, *swaps, planes, row_top, row_end = run_first(vorticity, swirl, base_swirl)
-    swaps = swapped("row", *swaps)
-    whole, beyond, *swaps = run_second(part, *swaps, planes, row_top, row_end)
+    rows = swapped("row", *swaps)
+    whole, *swaps = run_second(part, *rows, planes, row_top, row_end)
     swaps = swapped("gz", *swaps)
-    basis, message = run_third(whole, *swaps, devices)
+    basis, message = run_third(whole, swaps, devices)
     grams = lax.all_to_all(message, AXES, 0, 0, tiled=True)
-    levels = run_down(planes, beyond, *swaps)
-    swirl_rate, vort_rate = run_rates(swirl, vorticity, base_swirl, beyond, *swaps, vel_r, vel_z, swirl_coef, vort_coef)
+    levels = run_down(planes, rows, swaps)
+    swirl_rate, vort_rate = run_rates(swirl, vorticity, base_swirl, rows, *swaps, vel_r, vel_z, swirl_coef, vort_coef)
     potential = run_fourth(grams, basis, levels)
     return swirl_rate, vort_rate, potential
 

time: 51.6 us -> 49.9 us (0.967)
  Pallas kernels: 24.1 us -> 22.9 us
  local copies, waits for them, and re-layouts: 0.66 us -> 0.02 us
    pallas_call x1, Pallas kernels: 6.63 us -> 5.68 us  [run_rates(): pl.pallas_call(rates_kernel, grid=(ROWS // STRIP,), out_shape=(shaped(ROW...]
    unnamed x8 -> x10, local copies, waits for them, and re-layouts: 0.66 us -> 0.02 us
    pallas_call x1, Pallas kernels: 6.09 us -> 5.54 us  [run_fourth(): pl.pallas_call(functools.partial(fourth_kernel, cells=cells), out_shape=s...]
  transfers between devices with their start and end apart: 5 -> 5, of which waited for: 2 -> 2; matrix products, arithmetic and copies ran while one was open for 0% -> 0% of each run, Pallas kernels for 21% -> 20%
where the time goes in v6:
time: 49.9 us; the launch traced here: 49.6 us
  Pallas kernels  22.9 us (46%)
  starting transfers between devices  20.9 us (42%)
  waiting for transfers between devices  5.02 us (10%)
  between operations  0.73 us (1%)
    all_to_all x1, starting transfers between devices, per_device(): grams = lax.all_to_all(message, AXES, 0, 0, tiled=True)  11.4 us
    ppermute x2, starting transfers between devices, swapped(): lax.ppermute(second, axis, others)  6.49 us
    pallas_call x1, Pallas kernels, run_rates(): pl.pallas_call(rates_kernel, grid=(ROWS // STRIP,), out_shape=(shaped(ROW...  5.68 us
    pallas_call x1, Pallas kernels, run_fourth(): pl.pallas_call(functools.partial(fourth_kernel, cells=cells), out_shape=s...  5.54 us
    ppermute x2, waiting for transfers between devices, swapped(): lax.ppermute(second, axis, others)  4.98 us
    pallas_call x1, Pallas kernels, run_first(): pl.pallas_call(first_kernel, out_shape=(shaped(32, 256), shaped(FOLD + 32...  4.69 us
    pallas_call x1, Pallas kernels, run_down(): pl.pallas_call(down_kernel, out_shape=tuple((pltpu.HBM((rows, 128), F32)...  4.46 us
    ppermute x2, starting transfers between devices, swapped(): lax.ppermute(first, axis, pairs)  2.96 us
  transfers between devices with their start and end apart: 5, of which 2 were waited for; matrix products, arithmetic and copies ran while one was open for 0% of the time, Pallas kernels for 20%

profile of v6, /device:TPU:1, one launch (start us, length us, event | category | flops | bytes accessed | tf_op | source)
XLA Modules:
  0.0 49.6 jit_solution(1102744675502029267)
XLA Ops:
  0.6 4.7 %down_own.1 = (f32[32,256]{1,0:T(8,128)S(1)}, f32[80,128]{1,0:T(8,128)S(1)}, f32[80,128]{1,0:T(8,128)S(1)}, f32[1536,128]{1,0:T(8,128)S(1)}, f32[24,128]{1,0:T(8,128)S(1)}, /*index=5*/f32[24,128]{1,0:T(8,128)S(1)}) custom-call(f32[192,1024]{1,0:T(8,128)} %vort_down.1, f32[192,1024]{1,0:T(8,128)} %swirl_down.1, f32[192,1024]{1,0:T(8,128)} %back_down.1), custom_call_target="tpu_custom_call" | custom-call | tf_op jit(solution)/shard_map/down_own/pallas_call | solution.py:456
  5.3 0.0 copy-start.2
  5.3 1.5 %collective-permute-start = (f32[80,128]{1,0:T(8,128)S(1)}, f32[80,128]{1,0:T(8,128)S(1)}, u32[]{:S(2)}, u32[]{:S(2)}) collective-permute-start(f32[80,128]{1,0:T(8,128)S(1)} %get-tuple-element.22), channel_id=1, source_target_pairs={{0,1},{1,0},{2,3},{3,2},{4,5},{5,4},{6,7},{7,6},{8,9},{9,8},{10,11... | collective-permute-start | bytes 122888 | tf_op jit(solution)/shard_map/ppermute | solution.py:876
  6.8 1.3 %collective-permute-start.1 = (f32[80,128]{1,0:T(8,128)S(1)}, f32[80,128]{1,0:T(8,128)S(1)}, u32[]{:S(2)}, u32[]{:S(2)}) collective-permute-start(f32[80,128]{1,0:T(8,128)S(1)} %get-tuple-element.23), channel_id=1, source_target_pairs={{0,15},{1,2},{2,1},{3,4},{4,3},{5,6},{6,5},{7,8},{8,7},{9,10},{10,... | collective-permute-start | bytes 122888 | tf_op jit(solution)/shard_map/ppermute | solution.py:876
  8.1 0.0 collective-permute-done.swap_a.row_a.row_a_hbm
  8.1 0.0 copy-start.3
  8.1 2.1 %collective-permute-done.1.swap_b.row_b.row_b_hbm = f32[80,128]{1,0:T(8,128)S(1)} collective-permute-done((f32[80,128]{1,0:T(8,128)S(1)}, f32[80,128]{1,0:T(8,128)S(1)}, u32[]{:S(2)}, u32[]{:S(2)}) %collective-permute-start.1) | collective-permute-done | bytes 40992 | tf_op jit(solution)/shard_map/ppermute | solution.py:876
  10.3 0.0 copy-start.4
  10.3 0.2 pack_gz.1
  10.4 1.5 %collective-permute-start.2 = (f32[344,128]{1,0:T(8,128)S(1)}, f32[344,128]{1,0:T(8,128)S(1)}, u32[]{:S(2)}, u32[]{:S(2)}) collective-permute-start(f32[344,128]{1,0:T(8,128)S(1)} %get-tuple-element.28), channel_id=1, source_target_pairs={{0,16},{16,0},{32,48},{48,32},{64,80},{80,64},{96,112},{112,96},{1... | collective-permute-start | bytes 528392 | tf_op jit(solution)/shard_map/ppermute | solution.py:876
  11.9 5.2 %collective-permute-start.3 = (f32[344,128]{1,0:T(8,128)S(1)}, f32[344,128]{1,0:T(8,128)S(1)}, u32[]{:S(2)}, u32[]{:S(2)}) collective-permute-start(f32[344,128]{1,0:T(8,128)S(1)} %get-tuple-element.29), channel_id=1, source_target_pairs={{0,112},{16,32},{32,16},{48,64},{64,48},{80,96},{96,80},{112,0},{1... | collective-permute-start | bytes 528392 | tf_op jit(solution)/shard_map/ppermute | solution.py:876
  17.1 0.0 collective-permute-done.2.u_a.p_a.w_a.swap_a.a_hbm
  17.1 2.8 %collective-permute-done.3.u_b.p_b.w_b.swap_b.b_hbm = f32[344,128]{1,0:T(8,128)S(1)} collective-permute-done((f32[344,128]{1,0:T(8,128)S(1)}, f32[344,128]{1,0:T(8,128)S(1)}, u32[]{:S(2)}, u32[]{:S(2)}) %collective-permute-start.3) | collective-permute-done | bytes 176160 | tf_op jit(solution)/shard_map/ppermute | solution.py:876
  20.0 2.4 %basis_gram.1 = (f32[320,256]{1,0:T(8,128)}, f32[256,128]{1,0:T(8,128)}) custom-call(f32[32,256]{1,0:T(8,128)S(1)} %get-tuple-element.32.whole, f32[344,128]{1,0:T(8,128)S(1)} %collective-permute-done.2.u_a.p_a.w_a.swap_a.a_hbm, f32[344,128]{1,0:T(8,128)S(1)} %collective-permute-done.3.u_b.p_b.w_b.swap_b.b_hbm), custom_call_target="tpu_custom_call" | custom-call | tf_op jit(solution)/shard_map/basis_gram/pallas_call | solution.py:591
  22.4 11.4 %all-to-all-start = ((f32[128,2,128]{2,1,0:T(2,128)}), f32[128,2,128]{2,1,0:T(2,128)S(1)}, u32[]{:S(2)}, u32[]{:S(2)}) async-start(f32[128,2,128]{2,1,0:T(2,128)} %bitcast), calls=%async_computation | async-start | bytes 262144 | tf_op jit(solution)/shard_map/all_to_all | solution.py:886
  33.8 0.0 copy-done.3
  33.8 0.0 copy-done.4
  33.8 0.0 copy-done
  33.9 0.0 copy-done.1
  33.9 5.7 %rates.1 = (f32[192,1024]{1,0:T(8,128)}, f32[192,1024]{1,0:T(8,128)}) custom-call(f32[192,1024]{1,0:T(8,128)} %swirl_down.1, f32[192,1024]{1,0:T(8,128)} %swirl_down.1, f32[192,1024]{1,0:T(8,128)} %swirl_down.1, f32[192,1024]{1,0:T(8,128)} %vort_down.1, f32[192,1024]{1,0:T(8,128)} %vort_down.1, f32[192,1024]{1,0:T(8,128)} %vort_down.1, ...), custom_call_target="tpu_custom_call" | custom-call | flops 5898240 | bytes 7077888 | tf_op jit(solution)/shard_map/rates/pallas_call | solution.py:860
  39.5 0.0 copy-done.2
  39.6 4.5 %down_all.1 = (f32[2304,128]{1,0:T(8,128)}, f32[1280,128]{1,0:T(8,128)}, f32[960,128]{1,0:T(8,128)}, f32[960,128]{1,0:T(8,128)}, f32[288,128]{1,0:T(8,128)}, /*index=5*/f32[288,128]{1,0:T(8,128)}) custom-call(f32[1536,128]{1,0:T(8,128)} %copy-done.2, f32[80,128]{1,0:T(8,128)} %copy-done.3, f32[80,128]{1,0:T(8,128)} %copy-done.4, f32[344,128]{1,0:T(8,128)} %copy-done, ...), custom_call_target="tpu_custom_call" | custom-call | flops 7864320 | bytes 5898240 | tf_op jit(solution)/shard_map/down_all/pallas_call | solution.py:730
  44.0 0.0 all-to-all-done
  44.1 5.5 %v_cycle.1 = f32[192,1024]{1,0:T(8,128)} custom-call(f32[256,128]{1,0:T(8,128)S(1)} %bitcast.2, f32[320,256]{1,0:T(8,128)} %get-tuple-element.34.basis_hbm, f32[2304,128]{1,0:T(8,128)} %get-tuple-element.35.s0_hbm, f32[1280,128]{1,0:T(8,128)} %get-tuple-element.36.b0_hbm, f32[960,128]{1,0:T(8,128)} %get-tuple-element.37.s1_hbm, ...), custom_call_target="tpu_custom_call" | custom-call | tf_op jit(solution)/shard_map/v_cycle/pallas_call | solution.py:794
  (2 shorter events, 0.0 us)
Async XLA Ops:
  5.3 34.2 %copy-start.2 = (f32[1536,128]{1,0:T(8,128)}, f32[1536,128]{1,0:T(8,128)S(1)}, u32[]{:S(2)}) copy-start(f32[1536,128]{1,0:T(8,128)S(1)} %get-tuple-element.25.planes.planes_hbm) | copy-start | bytes 2359300
  5.3 2.8 %collective-permute-start = (f32[80,128]{1,0:T(8,128)S(1)}, f32[80,128]{1,0:T(8,128)S(1)}, u32[]{:S(2)}, u32[]{:S(2)}) collective-permute-start(f32[80,128]{1,0:T(8,128)S(1)} %get-tuple-element.22), channel_id=1, source_target_pairs={{0,1},{1,0},{2,3},{3,2},{4,5},{5,4},{6,7},{7,6},{8,9},{9,8},{10,11... | collective-permute-start | bytes 122888 | tf_op jit(solution)/shard_map/ppermute | solution.py:876
  6.8 3.4 %collective-permute-start.1 = (f32[80,128]{1,0:T(8,128)S(1)}, f32[80,128]{1,0:T(8,128)S(1)}, u32[]{:S(2)}, u32[]{:S(2)}) collective-permute-start(f32[80,128]{1,0:T(8,128)S(1)} %get-tuple-element.23), channel_id=1, source_target_pairs={{0,15},{1,2},{2,1},{3,4},{4,3},{5,6},{6,5},{7,8},{8,7},{9,10},{10,... | collective-permute-start | bytes 122888 | tf_op jit(solution)/shard_map/ppermute | solution.py:876
  8.1 25.7 %copy-start.3 = (f32[80,128]{1,0:T(8,128)}, f32[80,128]{1,0:T(8,128)S(1)}, u32[]{:S(2)}) copy-start(f32[80,128]{1,0:T(8,128)S(1)} %collective-permute-done.swap_a.row_a.row_a_hbm) | copy-start | bytes 122884
  10.3 23.6 %copy-start.4 = (f32[80,128]{1,0:T(8,128)}, f32[80,128]{1,0:T(8,128)S(1)}, u32[]{:S(2)}) copy-start(f32[80,128]{1,0:T(8,128)S(1)} %collective-permute-done.1.swap_b.row_b.row_b_hbm) | copy-start | bytes 122884
  10.4 6.7 %collective-permute-start.2 = (f32[344,128]{1,0:T(8,128)S(1)}, f32[344,128]{1,0:T(8,128)S(1)}, u32[]{:S(2)}, u32[]{:S(2)}) collective-permute-start(f32[344,128]{1,0:T(8,128)S(1)} %get-tuple-element.28), channel_id=1, source_target_pairs={{0,16},{16,0},{32,48},{48,32},{64,80},{80,64},{96,112},{112,96},{1... | collective-permute-start | bytes 528392 | tf_op jit(solution)/shard_map/ppermute | solution.py:876
  11.9 8.1 %collective-permute-start.3 = (f32[344,128]{1,0:T(8,128)S(1)}, f32[344,128]{1,0:T(8,128)S(1)}, u32[]{:S(2)}, u32[]{:S(2)}) collective-permute-start(f32[344,128]{1,0:T(8,128)S(1)} %get-tuple-element.29), channel_id=1, source_target_pairs={{0,112},{16,32},{32,16},{48,64},{64,48},{80,96},{96,80},{112,0},{1... | collective-permute-start | bytes 528392 | tf_op jit(solution)/shard_map/ppermute | solution.py:876
  17.1 16.7 %copy-start = (f32[344,128]{1,0:T(8,128)}, f32[344,128]{1,0:T(8,128)S(1)}, u32[]{:S(2)}) copy-start(f32[344,128]{1,0:T(8,128)S(1)} %collective-permute-done.2.u_a.p_a.w_a.swap_a.a_hbm) | copy-start | bytes 528388
  20.0 13.9 %copy-start.1 = (f32[344,128]{1,0:T(8,128)}, f32[344,128]{1,0:T(8,128)S(1)}, u32[]{:S(2)}) copy-start(f32[344,128]{1,0:T(8,128)S(1)} %collective-permute-done.3.u_b.p_b.w_b.swap_b.b_hbm) | copy-start | bytes 528388
  22.4 21.7 %all-to-all-start = ((f32[128,2,128]{2,1,0:T(2,128)}), f32[128,2,128]{2,1,0:T(2,128)S(1)}, u32[]{:S(2)}, u32[]{:S(2)}) async-start(f32[128,2,128]{2,1,0:T(2,128)} %bitcast), calls=%async_computation | async-start | bytes 262144 | tf_op jit(solution)/shard_map/all_to_all | solution.py:886

commit v7 on v6

--- a/solution.py
+++ b/solution.py
@@ -329,7 +329,7 @@
     return high, rest - (high - total)
 
 
-BAND = 32
+BAND = 16
 FOLD = ROWS // 4
 
 

time: 49.9 us -> 51.7 us (1.036)
  Pallas kernels: 22.9 us -> 24.7 us
    pallas_call x1, Pallas kernels: 4.69 us -> 5.95 us  [run_first(): pl.pallas_call(first_kernel, out_shape=(shaped(32, 256), shaped(FOLD + 32...]
    pallas_call x1, Pallas kernels: 5.54 us -> 6.06 us  [run_fourth(): pl.pallas_call(functools.partial(fourth_kernel, cells=cells), out_shape=s...]
where the time goes in v7:
time: 51.7 us; the launch traced here: 51.4 us
  Pallas kernels  24.7 us (48%)
  starting transfers between devices  20.9 us (40%)
  waiting for transfers between devices  5.02 us (10%)
  between operations  0.73 us (1%)
    all_to_all x1, starting transfers between devices, per_device(): grams = lax.all_to_all(message, AXES, 0, 0, tiled=True)  11.4 us
    ppermute x2, starting transfers between devices, swapped(): lax.ppermute(second, axis, others)  6.49 us
    pallas_call x1, Pallas kernels, run_fourth(): pl.pallas_call(functools.partial(fourth_kernel, cells=cells), out_shape=s...  6.06 us
    pallas_call x1, Pallas kernels, run_first(): pl.pallas_call(first_kernel, out_shape=(shaped(32, 256), shaped(FOLD + 32...  5.95 us
    pallas_call x1, Pallas kernels, run_rates(): pl.pallas_call(rates_kernel, grid=(ROWS // STRIP,), out_shape=(shaped(ROW...  5.68 us
    ppermute x2, waiting for transfers between devices, swapped(): lax.ppermute(second, axis, others)  4.98 us
    pallas_call x1, Pallas kernels, run_down(): pl.pallas_call(down_kernel, out_shape=tuple((pltpu.HBM((rows, 128), F32)...  4.46 us
    ppermute x2, starting transfers between devices, swapped(): lax.ppermute(first, axis, pairs)  2.96 us
  transfers between devices with their start and end apart: 5, of which 2 were waited for; matrix products, arithmetic and copies ran while one was open for 0% of the time, Pallas kernels for 20%

profile of v7, /device:TPU:1, one launch (start us, length us, event | category | flops | bytes accessed | tf_op | source)
XLA Modules:
  0.0 51.4 jit_solution(4229479465123287342)
XLA Ops:
  0.6 6.0 %down_own.1 = (f32[32,256]{1,0:T(8,128)S(1)}, f32[80,128]{1,0:T(8,128)S(1)}, f32[80,128]{1,0:T(8,128)S(1)}, f32[1536,128]{1,0:T(8,128)S(1)}, f32[24,128]{1,0:T(8,128)S(1)}, /*index=5*/f32[24,128]{1,0:T(8,128)S(1)}) custom-call(f32[192,1024]{1,0:T(8,128)} %vort_down.1, f32[192,1024]{1,0:T(8,128)} %swirl_down.1, f32[192,1024]{1,0:T(8,128)} %back_down.1), custom_call_target="tpu_custom_call" | custom-call | tf_op jit(solution)/shard_map/down_own/pallas_call | solution.py:456
  6.6 0.0 copy-start.2
  6.6 1.5 %collective-permute-start = (f32[80,128]{1,0:T(8,128)S(1)}, f32[80,128]{1,0:T(8,128)S(1)}, u32[]{:S(2)}, u32[]{:S(2)}) collective-permute-start(f32[80,128]{1,0:T(8,128)S(1)} %get-tuple-element.22), channel_id=1, source_target_pairs={{0,1},{1,0},{2,3},{3,2},{4,5},{5,4},{6,7},{7,6},{8,9},{9,8},{10,11... | collective-permute-start | bytes 122888 | tf_op jit(solution)/shard_map/ppermute | solution.py:876
  8.1 1.3 %collective-permute-start.1 = (f32[80,128]{1,0:T(8,128)S(1)}, f32[80,128]{1,0:T(8,128)S(1)}, u32[]{:S(2)}, u32[]{:S(2)}) collective-permute-start(f32[80,128]{1,0:T(8,128)S(1)} %get-tuple-element.23), channel_id=1, source_target_pairs={{0,15},{1,2},{2,1},{3,4},{4,3},{5,6},{6,5},{7,8},{8,7},{9,10},{10,... | collective-permute-start | bytes 122888 | tf_op jit(solution)/shard_map/ppermute | solution.py:876
  9.4 0.0 collective-permute-done.swap_a.row_a.row_a_hbm
  9.4 0.0 copy-start.3
  9.4 2.1 %collective-permute-done.1.swap_b.row_b.row_b_hbm = f32[80,128]{1,0:T(8,128)S(1)} collective-permute-done((f32[80,128]{1,0:T(8,128)S(1)}, f32[80,128]{1,0:T(8,128)S(1)}, u32[]{:S(2)}, u32[]{:S(2)}) %collective-permute-start.1) | collective-permute-done | bytes 40992 | tf_op jit(solution)/shard_map/ppermute | solution.py:876
  11.5 0.0 copy-start.4
  11.5 0.2 pack_gz.1
  11.7 1.5 %collective-permute-start.2 = (f32[344,128]{1,0:T(8,128)S(1)}, f32[344,128]{1,0:T(8,128)S(1)}, u32[]{:S(2)}, u32[]{:S(2)}) collective-permute-start(f32[344,128]{1,0:T(8,128)S(1)} %get-tuple-element.28), channel_id=1, source_target_pairs={{0,16},{16,0},{32,48},{48,32},{64,80},{80,64},{96,112},{112,96},{1... | collective-permute-start | bytes 528392 | tf_op jit(solution)/shard_map/ppermute | solution.py:876
  13.2 5.2 %collective-permute-start.3 = (f32[344,128]{1,0:T(8,128)S(1)}, f32[344,128]{1,0:T(8,128)S(1)}, u32[]{:S(2)}, u32[]{:S(2)}) collective-permute-start(f32[344,128]{1,0:T(8,128)S(1)} %get-tuple-element.29), channel_id=1, source_target_pairs={{0,112},{16,32},{32,16},{48,64},{64,48},{80,96},{96,80},{112,0},{1... | collective-permute-start | bytes 528392 | tf_op jit(solution)/shard_map/ppermute | solution.py:876
  18.4 0.0 collective-permute-done.2.u_a.p_a.w_a.swap_a.a_hbm
  18.4 2.8 %collective-permute-done.3.u_b.p_b.w_b.swap_b.b_hbm = f32[344,128]{1,0:T(8,128)S(1)} collective-permute-done((f32[344,128]{1,0:T(8,128)S(1)}, f32[344,128]{1,0:T(8,128)S(1)}, u32[]{:S(2)}, u32[]{:S(2)}) %collective-permute-start.3) | collective-permute-done | bytes 176160 | tf_op jit(solution)/shard_map/ppermute | solution.py:876
  21.2 2.4 %basis_gram.1 = (f32[320,256]{1,0:T(8,128)}, f32[256,128]{1,0:T(8,128)}) custom-call(f32[32,256]{1,0:T(8,128)S(1)} %get-tuple-element.32.whole, f32[344,128]{1,0:T(8,128)S(1)} %collective-permute-done.2.u_a.p_a.w_a.swap_a.a_hbm, f32[344,128]{1,0:T(8,128)S(1)} %collective-permute-done.3.u_b.p_b.w_b.swap_b.b_hbm), custom_call_target="tpu_custom_call" | custom-call | tf_op jit(solution)/shard_map/basis_gram/pallas_call | solution.py:591
  23.6 11.4 %all-to-all-start = ((f32[128,2,128]{2,1,0:T(2,128)}), f32[128,2,128]{2,1,0:T(2,128)S(1)}, u32[]{:S(2)}, u32[]{:S(2)}) async-start(f32[128,2,128]{2,1,0:T(2,128)} %bitcast), calls=%async_computation | async-start | bytes 262144 | tf_op jit(solution)/shard_map/all_to_all | solution.py:886
  35.1 0.0 copy-done.3
  35.1 0.0 copy-done.4
  35.1 0.0 copy-done
  35.1 0.0 copy-done.1
  35.1 5.7 %rates.1 = (f32[192,1024]{1,0:T(8,128)}, f32[192,1024]{1,0:T(8,128)}) custom-call(f32[192,1024]{1,0:T(8,128)} %swirl_down.1, f32[192,1024]{1,0:T(8,128)} %swirl_down.1, f32[192,1024]{1,0:T(8,128)} %swirl_down.1, f32[192,1024]{1,0:T(8,128)} %vort_down.1, f32[192,1024]{1,0:T(8,128)} %vort_down.1, f32[192,1024]{1,0:T(8,128)} %vort_down.1, ...), custom_call_target="tpu_custom_call" | custom-call | flops 5898240 | bytes 7077888 | tf_op jit(solution)/shard_map/rates/pallas_call | solution.py:860
  40.8 0.0 copy-done.2
  40.8 4.5 %down_all.1 = (f32[2304,128]{1,0:T(8,128)}, f32[1280,128]{1,0:T(8,128)}, f32[960,128]{1,0:T(8,128)}, f32[960,128]{1,0:T(8,128)}, f32[288,128]{1,0:T(8,128)}, /*index=5*/f32[288,128]{1,0:T(8,128)}) custom-call(f32[1536,128]{1,0:T(8,128)} %copy-done.2, f32[80,128]{1,0:T(8,128)} %copy-done.3, f32[80,128]{1,0:T(8,128)} %copy-done.4, f32[344,128]{1,0:T(8,128)} %copy-done, ...), custom_call_target="tpu_custom_call" | custom-call | flops 7864320 | bytes 5898240 | tf_op jit(solution)/shard_map/down_all/pallas_call | solution.py:730
  45.3 0.0 all-to-all-done
  45.3 6.1 %v_cycle.1 = f32[192,1024]{1,0:T(8,128)} custom-call(f32[256,128]{1,0:T(8,128)S(1)} %bitcast.2, f32[320,256]{1,0:T(8,128)} %get-tuple-element.34.basis_hbm, f32[2304,128]{1,0:T(8,128)} %get-tuple-element.35.s0_hbm, f32[1280,128]{1,0:T(8,128)} %get-tuple-element.36.b0_hbm, f32[960,128]{1,0:T(8,128)} %get-tuple-element.37.s1_hbm, ...), custom_call_target="tpu_custom_call" | custom-call | tf_op jit(solution)/shard_map/v_cycle/pallas_call | solution.py:794
  (2 shorter events, 0.0 us)
Async XLA Ops:
  6.6 34.2 %copy-start.2 = (f32[1536,128]{1,0:T(8,128)}, f32[1536,128]{1,0:T(8,128)S(1)}, u32[]{:S(2)}) copy-start(f32[1536,128]{1,0:T(8,128)S(1)} %get-tuple-element.25.planes.planes_hbm) | copy-start | bytes 2359300
  6.6 2.8 %collective-permute-start = (f32[80,128]{1,0:T(8,128)S(1)}, f32[80,128]{1,0:T(8,128)S(1)}, u32[]{:S(2)}, u32[]{:S(2)}) collective-permute-start(f32[80,128]{1,0:T(8,128)S(1)} %get-tuple-element.22), channel_id=1, source_target_pairs={{0,1},{1,0},{2,3},{3,2},{4,5},{5,4},{6,7},{7,6},{8,9},{9,8},{10,11... | collective-permute-start | bytes 122888 | tf_op jit(solution)/shard_map/ppermute | solution.py:876
  8.1 3.4 %collective-permute-start.1 = (f32[80,128]{1,0:T(8,128)S(1)}, f32[80,128]{1,0:T(8,128)S(1)}, u32[]{:S(2)}, u32[]{:S(2)}) collective-permute-start(f32[80,128]{1,0:T(8,128)S(1)} %get-tuple-element.23), channel_id=1, source_target_pairs={{0,15},{1,2},{2,1},{3,4},{4,3},{5,6},{6,5},{7,8},{8,7},{9,10},{10,... | collective-permute-start | bytes 122888 | tf_op jit(solution)/shard_map/ppermute | solution.py:876
  9.4 25.7 %copy-start.3 = (f32[80,128]{1,0:T(8,128)}, f32[80,128]{1,0:T(8,128)S(1)}, u32[]{:S(2)}) copy-start(f32[80,128]{1,0:T(8,128)S(1)} %collective-permute-done.swap_a.row_a.row_a_hbm) | copy-start | bytes 122884
  11.5 23.6 %copy-start.4 = (f32[80,128]{1,0:T(8,128)}, f32[80,128]{1,0:T(8,128)S(1)}, u32[]{:S(2)}) copy-start(f32[80,128]{1,0:T(8,128)S(1)} %collective-permute-done.1.swap_b.row_b.row_b_hbm) | copy-start | bytes 122884
  11.7 6.7 %collective-permute-start.2 = (f32[344,128]{1,0:T(8,128)S(1)}, f32[344,128]{1,0:T(8,128)S(1)}, u32[]{:S(2)}, u32[]{:S(2)}) collective-permute-start(f32[344,128]{1,0:T(8,128)S(1)} %get-tuple-element.28), channel_id=1, source_target_pairs={{0,16},{16,0},{32,48},{48,32},{64,80},{80,64},{96,112},{112,96},{1... | collective-permute-start | bytes 528392 | tf_op jit(solution)/shard_map/ppermute | solution.py:876
  13.2 8.1 %collective-permute-start.3 = (f32[344,128]{1,0:T(8,128)S(1)}, f32[344,128]{1,0:T(8,128)S(1)}, u32[]{:S(2)}, u32[]{:S(2)}) collective-permute-start(f32[344,128]{1,0:T(8,128)S(1)} %get-tuple-element.29), channel_id=1, source_target_pairs={{0,112},{16,32},{32,16},{48,64},{64,48},{80,96},{96,80},{112,0},{1... | collective-permute-start | bytes 528392 | tf_op jit(solution)/shard_map/ppermute | solution.py:876
  18.4 16.7 %copy-start = (f32[344,128]{1,0:T(8,128)}, f32[344,128]{1,0:T(8,128)S(1)}, u32[]{:S(2)}) copy-start(f32[344,128]{1,0:T(8,128)S(1)} %collective-permute-done.2.u_a.p_a.w_a.swap_a.a_hbm) | copy-start | bytes 528388
  21.2 13.9 %copy-start.1 = (f32[344,128]{1,0:T(8,128)}, f32[344,128]{1,0:T(8,128)S(1)}, u32[]{:S(2)}) copy-start(f32[344,128]{1,0:T(8,128)S(1)} %collective-permute-done.3.u_b.p_b.w_b.swap_b.b_hbm) | copy-start | bytes 528388
  23.6 21.7 %all-to-all-start = ((f32[128,2,128]{2,1,0:T(2,128)}), f32[128,2,128]{2,1,0:T(2,128)S(1)}, u32[]{:S(2)}, u32[]{:S(2)}) async-start(f32[128,2,128]{2,1,0:T(2,128)} %bitcast), calls=%async_computation | async-start | bytes 262144 | tf_op jit(solution)/shard_map/all_to_all | solution.py:886
